TPU v7x, 128 devices: a whole 4x4x4 slice. The times are simulated.
128 devices in a mesh: row: 16 (over y, x), col: 8 (over z, core).
Axes of the slice: x: 4, y: 4, z: 4, core: 2. Of those that a mesh axis runs over, the one named last changes fastest.
Arguments:
- out_grad: bfloat16 [131072, 256], P(('row', 'col')), may hold values from -6 to 6
- features: bfloat16 [131072, 256], P(('col', 'row')), may hold values from -6 to 6
- weight: bfloat16 [256, 256], replicated, may hold values from -0.375 to 0.375
- tiles: bfloat16 [16, 8, 384, 128, 128], P('row', 'col'), may hold values from -0.07470703 to 0.07470703
- row_block: int32 [16, 8, 384], P('row', 'col'), may hold values from 0 to 63
- col_block: int32 [16, 8, 384], P('row', 'col'), may hold values from 0 to 127
- live: int32 [16, 8, 384], P('row', 'col'), may hold values from 0 to 1, as said below
Outputs:
- input_grad: bfloat16 [131072, 256], P(('col', 'row'))
- weight_grad: float32 [256, 256], replicated
Inputs may be any that keep to these rules, and one draw needn't show every extreme that they name: Each cell's slots of live hold between 48 and 384 ones, and in some cell all 384 slots are live.
All inputs are finite; a program needn't handle non-finite values.
Results may differ from a plain program's by a relative error of at most 0.0049.
Values may be sent and summed in bfloat16 or wider, within the bound.
No kernel may reach another device: no remote copies, remote signals or barrier semaphores. Data moves between devices by JAX's collectives and lax.ppermute only.
A program may use at most 256 MiB of HBM per device.

v0:
```python
import jax
import jax.numpy as jnp
from jax import lax
from jax.sharding import PartitionSpec as P


def local(out_grad, features, weight, tiles, row_block, col_block, live):
    tile_set = tiles[0, 0]
    row_ids = row_block[0, 0]
    col_ids = col_block[0, 0]
    live_weights = live[0, 0].astype(jnp.float32)
    tile_size = tile_set.shape[-1]
    feature_width = out_grad.shape[1]
    own_rows = features.shape[0]
    group_rows = lax.all_gather(out_grad, "col", axis=0, tiled=True)
    grad_blocks = group_rows.reshape(-1, tile_size, feature_width)
    column_count = lax.axis_size("row") * own_rows // tile_size
    panels = grad_blocks[row_ids]
    contrib = jnp.einsum("kij,kif->kjf", tile_set, panels, preferred_element_type=jnp.float32)
    contrib = contrib * live_weights[:, None, None]
    partial_value = jax.ops.segment_sum(contrib, col_ids, num_segments=column_count)
    partial_value = partial_value.reshape(column_count * tile_size, feature_width)
    summed = lax.psum_scatter(partial_value, "row", scatter_dimension=0, tiled=True)
    column_grad = summed.astype(jnp.bfloat16)
    input_grad = jnp.einsum(
        "nf,gf->ng", column_grad, weight, preferred_element_type=jnp.float32
    ).astype(jnp.bfloat16)
    local_weight = jnp.einsum(
        "nf,ng->fg", features, column_grad, preferred_element_type=jnp.float32
    )
    summed_weight = lax.psum(local_weight, ("row", "col"))
    node_count = own_rows * lax.axis_size("row") * lax.axis_size("col")
    weight_grad = summed_weight * node_count ** (-0.5)
    return (input_grad, weight_grad)


def solution(mesh):
    return jax.shard_map(
        local,
        mesh=mesh,
        in_specs=(
            P(("row", "col"), None),
            P(("col", "row"), None),
            P(),
            P("row", "col", None, None, None),
            P("row", "col", None),
            P("row", "col", None),
            P("row", "col", None),
        ),
        out_specs=(P(("col", "row"), None), P()),
        check_vma=False,
    )
```

profile of v0, /device:TPU:1, one launch (start us, length us, event | category | flops | bytes accessed | tf_op | source)
XLA Modules:
  0.0 528.9 jit_solution(17368533770410654152)
XLA Ops:
  7.2 0.0 copy-start
  7.2 0.0 all-gather.2.cloned.1.call-start
  7.2 0.7 all-gather.2.cloned.1.call-update
  7.9 0.0 reduce-scatter.2.cloned.1.call-start
  8.0 0.7 reduce
  8.7 0.7 fusion.3
  9.4 0.7 convert_reduce_fusion
  10.1 35.7 %all-gather.2.cloned.1.call-done = bf16[8192,256]{1,0:T(8,128)(2,1)} async-done(((bf16[1024,256]{1,0:T(8,128)(2,1)}), bf16[8192,256]{1,0:T(8,128)(2,1)}) %all-gather.2.cloned.1.call-update) | async-done | bytes 4194320 | tf_op jit(solution)/shard_map/all_gather | solution.py:15
  45.7 15.1 %gather_fusion = bf16[384,128,256]{2,1,0:T(8,128)(2,1)} fusion(bf16[64,128,256]{2,1,0:T(8,128)(2,1)} %bitcast.15, s32[1024]{0:T(1024)S(1)} %pad_clamp_fusion), kind=kCustom, calls=%fused_computation | custom fusion | bytes 50333184 | tf_op jit(solution)/shard_map/gather | solution.py:18
  60.8 31.7 %multiply_bitcast_fusion = f32[384,128,256]{1,2,0:T(8,128)} fusion(f32[384]{0:T(512)S(1)} %convert_reduce_fusion, bf16[384,128,256]{2,1,0:T(8,128)(2,1)} %gather_fusion, bf16[1,1,384,128,128]{4,3,2,1,0:T(8,128)(2,1)} %param.10), kind=kOutput, calls=%fused_computation.2 | convolution fusion | flops 3233808384 | bytes 88081920 | tf_op jit(solution)/shard_map/kij,kif->kjf/dot_general | solution.py:19
  92.5 48.8 %copy.12 = f32[384,128,256]{2,1,0:T(8,128)} copy(f32[384,128,256]{1,2,0:T(8,128)} %multiply_bitcast_fusion) | data formatting | bytes 100663296 | tf_op jit(solution)/shard_map/mul | solution.py:20
  141.3 7.8 %broadcast_in_dim.2 = f32[128,128,256]{2,1,0:T(8,128)} broadcast(f32[]{:T(128)} %constant.0.clone.1), dimensions={} | broadcast | bytes 16777220 | tf_op jit(solution)/shard_map/broadcast_in_dim | solution.py:21
  149.2 114.5 %scatter_fusion = f32[128,128,256]{2,1,0:T(8,128)} fusion(f32[128,128,256]{2,1,0:T(8,128)} %broadcast_in_dim.2, s32[384]{0:T(512)S(1)} %reduce, f32[384,128,256]{2,1,0:T(8,128)} %copy.12), kind=kCustom, calls=%fused_computation.1 | custom fusion | flops 12582912 | bytes 150996480 | tf_op jit(solution)/shard_map/scatter-add | solution.py:21
  263.7 0.0 reduce-scatter.2.cloned.1.call-update
  263.7 0.0 all-reduce.2.cloned.1.call-start
  263.8 110.0 %reduce-scatter.2.cloned.1.call-done = f32[1024,256]{1,0:T(8,128)} async-done(((f32[16384,256]{1,0:T(8,128)}), f32[1024,256]{1,0:T(8,128)}) %reduce-scatter.2.cloned.1.call-update) | async-done | bytes 1048592 | tf_op jit(solution)/shard_map/reduce_scatter | solution.py:23
  373.8 0.0 copy-done
  373.8 2.3 convolution_bitcast_fusion
  376.1 0.0 all-reduce.2.cloned.1.call-update
  376.1 0.0 copy-done.1
  376.1 2.4 convolution_convert_fusion
  378.5 142.1 %all-reduce.2.cloned.1.call-done = f32[256,256]{0,1:T(8,128)} async-done(((f32[256,256]{0,1:T(8,128)}), f32[256,256]{0,1:T(8,128)}) %all-reduce.2.cloned.1.call-update) | async-done | bytes 262160 | tf_op jit(solution)/shard_map/psum | solution.py:31
  520.6 1.0 broadcast_multiply_fusion
  521.6 0.8 copy.13
  (2 shorter events, 0.0 us)
Async XLA Ops:
  7.2 366.7 %copy-start = (bf16[1024,256]{1,0:T(8,128)(2,1)S(1)}, bf16[1024,256]{1,0:T(8,128)(2,1)}, u32[]{:S(2)}) copy-start(bf16[1024,256]{1,0:T(8,128)(2,1)} %param.8) | copy-start | bytes 1572868
  7.2 38.5 %all-gather.2.cloned.1.call-start = ((), (), s32[]{:S(2)}) async-start(), calls=%async_computation.1 | async-start | bytes 4718592 | tf_op jit(solution)/shard_map/all_gather | solution.py:15
  7.9 365.9 %reduce-scatter.2.cloned.1.call-start = ((), (), s32[]{:S(2)}) async-start(), calls=%async_computation.2 | async-start | bytes 17825792 | tf_op jit(solution)/shard_map/reduce_scatter | solution.py:23
  149.2 227.0 %copy-start.1 = (bf16[256,256]{1,0:T(8,128)(2,1)S(1)}, bf16[256,256]{1,0:T(8,128)(2,1)}, u32[]{:S(2)}) copy-start(bf16[256,256]{1,0:T(8,128)(2,1)} %param.9) | copy-start | bytes 393220
  263.7 256.9 %all-reduce.2.cloned.1.call-start = ((), (), s32[]{:S(2)}) async-start(), calls=%async_computation.3 | async-start | bytes 524288 | tf_op jit(solution)/shard_map/psum | solution.py:31
Sparse Core Ops, SparseCore 0:
  9.7 35.9 all-gather.1
  263.8 109.9 reduce-scatter.1
  379.1 141.4 all-reduce.1
where the time goes:
time: 530 us; the launch traced here: 529 us
  waiting for transfers between devices  289 us (55%)
  other arithmetic  118 us (22%)
  local copies, waits for them, and re-layouts  72.6 us (14%)
  matrix products  36.3 us (7%)
  between operations  13.8 us (3%)
    psum x1, waiting for transfers between devices, local(): summed_weight = lax.psum(local_weight, ('row', 'col'))  142 us
    scatter-add x1, other arithmetic, local(): jax.ops.segment_sum(contrib, col_ids, num_segments=column_count)  115 us
    reduce_scatter x1, waiting for transfers between devices, local(): lax.psum_scatter(partial_value, 'row', scatter_dimension=0, tiled=True)  110 us
    mul x1, local copies, waits for them, and re-layouts, local(): contrib = contrib * live_weights[:, None, None]  48.8 us
    all_gather x1, waiting for transfers between devices, local(): group_rows = lax.all_gather(out_grad, 'col', axis=0, tiled=True)  35.7 us
    dot_general x1, matrix products, local(): jnp.einsum('kij,kif->kjf', tile_set, panels, preferred_element_type=jnp.f...  31.7 us
    gather x1, local copies, waits for them, and re-layouts, local(): panels = grad_blocks[row_ids]  15.1 us
  transfers between devices with their start and end apart: 3, of which 3 were waited for; matrix products, arithmetic and copies ran while one was open for 1% of the time, Pallas kernels for 0%

commit v1 on v0

v1 whole, which is shorter than its diff:
```python
import functools

import jax
import jax.numpy as jnp
from jax import lax
from jax.experimental import pallas as pl
from jax.experimental.pallas import tpu as pltpu
from jax.sharding import PartitionSpec as P

F32, BF16 = jnp.float32, jnp.bfloat16
B = 128
NY = NX = NZ = 4
DUMMY = 128
CHUNK = 32
SLOTS = 4

XP = [[(y * NX + x, y * NX + (x + s) % NX) for y in range(NY) for x in range(NX)] for s in range(4)]
YP = [[(y * NX + x, (y + s) % NY * NX + x) for y in range(NY) for x in range(NX)] for s in range(4)]
ZP = [[(z * 2 + c, (z + s) % NZ * 2 + c) for z in range(NZ) for c in range(2)] for s in range(4)]
CP = [(z * 2 + c, z * 2 + 1 - c) for z in range(NZ) for c in range(2)]


def xperm(v, s):
    return lax.ppermute(v, "row", XP[s])


def yperm(v, s):
    return lax.ppermute(v, "row", YP[s])


def zperm(v, s):
    return lax.ppermute(v, "col", ZP[s])


def cperm(v):
    return lax.ppermute(v, "col", CP)


def panels_kernel(x_ref, lo_ref, hi_ref):
    for b in range(8):
        block = x_ref[b * B : (b + 1) * B, :].astype(F32)
        lo_ref[b] = block[:, :B].T.astype(BF16)
        hi_ref[b] = block[:, B:].T.astype(BF16)


def panels(out_grad):
    shape = jax.ShapeDtypeStruct((8, B, B), BF16)
    return pl.pallas_call(panels_kernel, out_shape=(shape, shape), name="panels")(out_grad)


OUT_BLOCKS = (16, 16, 16, 8, 8) * 2


def tile_kernel(rmap, cmap, tiles, *refs):
    xs = refs[:8]
    outs = refs[8:18]
    xbuf, tbuf, acc, stage, tsem, xsem, osem = refs[18:]
    slots = tiles.shape[0] // CHUNK

    def tile_copy(c, slot):
        return pltpu.make_async_copy(tiles.at[pl.ds(c * CHUNK, CHUNK)], tbuf.at[slot], tsem.at[slot])

    x_copies = [pltpu.make_async_copy(xs[i], xbuf.at[pl.ds(i * 8, 8)], xsem.at[i]) for i in range(8)]
    for copy in x_copies:
        copy.start()
    for c in range(SLOTS - 1):
        tile_copy(c, c).start()
    acc[...] = jnp.zeros_like(acc)
    for copy in x_copies:
        copy.wait()

    def chunk(c, carry):
        slot = lax.rem(c, SLOTS)
        tile_copy(c, slot).wait()

        @pl.when(c + SLOTS - 1 < slots)
        def _():
            tile_copy(c + SLOTS - 1, lax.rem(c + SLOTS - 1, SLOTS)).start()

        products = [
            jnp.dot(xbuf[rmap[c * CHUNK + u]], tbuf[slot, u], preferred_element_type=F32) for u in range(CHUNK)
        ]
        for u in range(CHUNK):
            acc[cmap[c * CHUNK + u]] += products[u]
        return carry

    lax.fori_loop(0, slots, chunk, 0)
    at = 0
    copies = []
    for i, n in enumerate(OUT_BLOCKS):
        stage[pl.ds(at, n)] = acc[pl.ds(at, n)].astype(BF16)
        copy = pltpu.make_async_copy(stage.at[pl.ds(at, n)], outs[i], osem.at[i])
        copy.start()
        copies.append(copy)
        at += n
    for copy in copies:
        copy.wait()


def tile_products(rmap, cmap, tiles, xs):
    hbm = pl.BlockSpec(memory_space=pl.ANY)
    return pl.pallas_call(
        tile_kernel,
        grid_spec=pltpu.PrefetchScalarGridSpec(
            num_scalar_prefetch=2,
            grid=(1,),
            in_specs=[hbm] * 9,
            out_specs=[hbm] * 10,
            scratch_shapes=[
                pltpu.VMEM((64, B, B), BF16),
                pltpu.VMEM((SLOTS, CHUNK, B, B), BF16),
                pltpu.VMEM((DUMMY + 1, B, B), F32),
                pltpu.VMEM((128, B, B), BF16),
                pltpu.SemaphoreType.DMA((SLOTS,)),
                pltpu.SemaphoreType.DMA((8,)),
                pltpu.SemaphoreType.DMA((10,)),
            ],
        ),
        out_shape=[jax.ShapeDtypeStruct((n, B, B), BF16) for n in OUT_BLOCKS],
        compiler_params=pltpu.CompilerParams(vmem_limit_bytes=24 * 2**20),
        name="tile_products",
    )(rmap, cmap, tiles, *xs)


def finish_kernel(*refs):
    parts, (feat, weight, ig, wg) = refs[:16], refs[16:]
    total = jnp.zeros((256, 256), F32)
    for b in range(8):
        half, i = b // 4, b % 4
        cols = []
        for h in range(2):
            four = parts[(h * 2 + half) * 4 : (h * 2 + half) * 4 + 4]
            s = four[0][i] + four[1][i].astype(F32)
            s = s + four[2][i].astype(F32) + four[3][i].astype(F32)
            cols.append(s)
        cg = jnp.concatenate(cols, axis=0).astype(BF16)
        rows = slice(b * B, (b + 1) * B)
        ig[rows, :] = lax.dot_general(
            cg, weight[...], (((0,), (1,)), ((), ())), preferred_element_type=F32
        ).astype(BF16)
        total = total + jnp.dot(cg, feat[rows, :], preferred_element_type=F32)
    wg[...] = total


def finish(parts, features, weight):
    return pl.pallas_call(
        finish_kernel,
        out_shape=(
            jax.ShapeDtypeStruct((1024, 256), BF16),
            jax.ShapeDtypeStruct((256, 256), F32),
        ),
        compiler_params=pltpu.CompilerParams(vmem_limit_bytes=16 * 2**20),
        name="finish",
    )(*parts, features, weight)


def gather(own):
    one, three, two = zperm(own, 1), zperm(own, 3), zperm(own, 2)
    return [own, cperm(own), three, cperm(three), two, cperm(two), one, cperm(one)]


def f32(v):
    return v.astype(F32)


def reduce_part(part, first, second):
    own, up, um, vp, vm = part
    rp, rm = first(up, 1), first(um, 3)
    sp = first((f32(vp) + f32(rp[:8])).astype(BF16), 1)
    sm = first((f32(vm) + f32(rm[:8])).astype(BF16), 3)
    low = f32(own[:8]) + f32(rm[8:]) + f32(sp)
    high = f32(own[8:]) + f32(rp[8:]) + f32(sm)
    t1, t2, t3 = low[4:].astype(BF16), high[:4].astype(BF16), high[4:].astype(BF16)
    return [low[:4], second(t1, 1), second(t2, 2), second(t3, 3)]


def rel(stack, at):
    n = stack.shape[0] // 4
    return lax.dynamic_slice_in_dim(stack, (at % 4) * n, n, 0)


def all_sum(v, z, core):
    half = v.shape[0] // 2
    mine = lax.dynamic_slice_in_dim(v, core * half, half, 0)
    other = lax.dynamic_slice_in_dim(v, (1 - core) * half, half, 0)
    v = mine + cperm(other)
    v = (rel(v, z) + zperm(rel(v, z + 2), 2)) + (zperm(rel(v, z + 1), 1) + zperm(rel(v, z + 3), 3))
    v = (v + xperm(v, 2)) + (xperm(v, 1) + xperm(v, 3))
    v = (v + yperm(v, 2)) + (yperm(v, 1) + yperm(v, 3))
    four = jnp.concatenate([v, zperm(v, 3), zperm(v, 2), zperm(v, 1)] * 2, axis=0)
    n = v.shape[0]
    v = lax.dynamic_slice_in_dim(four, ((4 - z) % 4) * n, 4 * n, 0)
    two = jnp.concatenate([v, cperm(v)] * 2, axis=0)
    return lax.dynamic_slice_in_dim(two, core * half, 2 * half, 0)


def local(out_grad, features, weight, tiles, row_block, col_block, live):
    row, col = lax.axis_index("row"), lax.axis_index("col")
    y, x, z, core = row // NX, row % NX, col // 2, col % 2
    rb, cb, on = row_block[0, 0], col_block[0, 0], live[0, 0]
    src = rb // 8
    rmap = (((src // 2 - z) % NZ) * 2 + (src % 2 + core) % 2) * 8 + rb % 8
    dest, b = cb // 8, cb % 8
    rx, ry = (dest % NX - x) % NX, (dest // NX - y) % NY
    in_first = b < 4
    major, minor = jnp.where(in_first, rx, ry), jnp.where(in_first, ry, rx)
    low = minor < 2
    start = jnp.where(
        major == 0,
        minor * 4,
        jnp.where(
            major == 1,
            jnp.where(low, 48 + minor * 4, 24 + (minor - 2) * 4),
            jnp.where(
                major == 2,
                jnp.where(low, 16 + minor * 4, 32 + (minor - 2) * 4),
                jnp.where(low, 40 + minor * 4, 56 + (minor - 2) * 4),
            ),
        ),
    )
    cmap = jnp.where(on > 0, start + b % 4 + jnp.where(in_first, 0, 64), DUMMY)

    halves = panels(out_grad)
    parts = []
    for own in halves:
        outs = tile_products(rmap, cmap, tiles[0, 0], gather(own))
        parts += reduce_part(outs[:5], xperm, yperm)
        parts += reduce_part(outs[5:], yperm, xperm)
    input_grad, wg = finish(parts, features, weight)
    wg = all_sum(wg, z, core)
    nodes = 1024 * 128
    return input_grad, wg.T * nodes ** (-0.5)


def solution(mesh):
    return jax.shard_map(
        local,
        mesh=mesh,
        in_specs=(
            P(("row", "col"), None),
            P(("col", "row"), None),
            P(),
            P("row", "col", None, None, None),
            P("row", "col", None),
            P("row", "col", None),
            P("row", "col", None),
        ),
        out_specs=(P(("col", "row"), None), P()),
        check_vma=False,
    )
```

time: 530 us -> 148 us (0.28)
  waiting for transfers between devices: 289 us -> 35.4 us
  other arithmetic: 118 us -> 3.75 us
  starting transfers between devices: 0.12 us -> 76.1 us
  local copies, waits for them, and re-layouts: 72.6 us -> 10 us
  matrix products: 36.3 us -> 0 us
  Pallas kernels: 0 us -> 21.4 us
  between operations: 13.8 us -> 1.14 us
    psum x1 -> x0, waiting for transfers between devices: 142 us -> none  [local(): summed_weight = lax.psum(local_weight, ('row', 'col'))]
    scatter-add x1 -> x0, other arithmetic: 115 us -> none  [local(): jax.ops.segment_sum(contrib, col_ids, num_segments=column_count)]
    reduce_scatter x1 -> x0, waiting for transfers between devices: 110 us -> none  [local(): lax.psum_scatter(partial_value, 'row', scatter_dimension=0, tiled=True)]
    ppermute x0 -> x56, starting transfers between devices: none -> 76.1 us  [the longest x17 21.1 us: xperm(): return lax.ppermute(v, 'row', XP[s])]
    mul x1 -> x0, local copies, waits for them, and re-layouts: 48.8 us -> none  [local(): contrib = contrib * live_weights[:, None, None]]
    dot_general x3 -> x0, matrix products: 36.3 us -> none  [the longest x1 31.7 us: local(): jnp.einsum('kij,kif->kjf', tile_set, panels, preferred_element_type=jnp.f...]
    all_gather x1 -> x0, waiting for transfers between devices: 35.7 us -> none  [local(): group_rows = lax.all_gather(out_grad, 'col', axis=0, tiled=True)]
    ppermute x0 -> x56, waiting for transfers between devices: none -> 35.4 us  [the longest x17 13.8 us: yperm(): return lax.ppermute(v, 'row', YP[s])]
  transfers between devices with their start and end apart: 3 -> 56, of which waited for: 3 -> 20; matrix products, arithmetic and copies ran while one was open for 1% -> 5% of each run, Pallas kernels for 0% -> 12%
where the time goes in v1:
time: 148 us
  starting transfers between devices  76.1 us (51%)
  waiting for transfers between devices  35.4 us (24%)
  Pallas kernels  21.4 us (14%)
  local copies, waits for them, and re-layouts  10 us (7%)
  other arithmetic  3.75 us (3%)
    ppermute x17, starting transfers between devices, xperm(): return lax.ppermute(v, 'row', XP[s])  21.1 us
    ppermute x17, starting transfers between devices, yperm(): return lax.ppermute(v, 'row', YP[s])  19.9 us
    ppermute x10, starting transfers between devices, cperm(): return lax.ppermute(v, 'col', CP)  18.7 us
    pallas_call x2, Pallas kernels, tile_products(): pl.pallas_call(tile_kernel, grid_spec=pltpu.PrefetchScalarGridSpec(num_sc...  17.8 us
    ppermute x12, starting transfers between devices, zperm(): return lax.ppermute(v, 'col', ZP[s])  16.4 us
    ppermute x17, waiting for transfers between devices, yperm(): return lax.ppermute(v, 'row', YP[s])  13.8 us
    ppermute x12, waiting for transfers between devices, zperm(): return lax.ppermute(v, 'col', ZP[s])  13.7 us
    unnamed x21, local copies, waits for them, and re-layouts  6.42 us
  transfers between devices with their start and end apart: 56, of which 20 were waited for; matrix products, arithmetic and copies ran while one was open for 5% of the time, Pallas kernels for 12%

profile of v1, /device:TPU:1, one launch (start us, length us, event | category | flops | bytes accessed | tf_op | source)
XLA Modules:
  0.0 147.7 jit_solution(12615629434967933560)
XLA Ops:
  0.6 2.0 %panels.1 = (bf16[8,128,128]{2,1,0:T(8,128)(2,1)}, bf16[8,128,128]{2,1,0:T(8,128)(2,1)}) custom-call(bf16[1024,256]{1,0:T(8,128)(2,1)} %x_ref.1), custom_call_target="tpu_custom_call" | custom-call | tf_op jit(solution)/shard_map/panels/pallas_call | solution.py:48
  2.7 4.6 %collective-permute-start.22 = (bf16[8,128,128]{2,1,0:T(8,128)(2,1)}, bf16[8,128,128]{2,1,0:T(8,128)(2,1)S(1)}, u32[]{:S(2)}, u32[]{:S(2)}) collective-permute-start(bf16[8,128,128]{2,1,0:T(8,128)(2,1)} %get-tuple-element.37.refs_0_), channel_id=1, source_target_pairs={{0,6},{1,7},{2,0},{3,1},{4,2},{5,3},{6,4},{7,5},{8,14},{9,15},{10,... | collective-permute-start | bytes 786440 | tf_op jit(solution)/shard_map/ppermute | solution.py:32
  11.2 6.8 %collective-permute-done.22.refs_2_ = bf16[8,128,128]{2,1,0:T(8,128)(2,1)S(1)} collective-permute-done((bf16[8,128,128]{2,1,0:T(8,128)(2,1)}, bf16[8,128,128]{2,1,0:T(8,128)(2,1)S(1)}, u32[]{:S(2)}, u32[]{:S(2)}) %collective-permute-start.22) | collective-permute-done | bytes 262176 | tf_op jit(solution)/shard_map/ppermute | solution.py:32
  18.0 2.8 %collective-permute-start.23 = (bf16[8,128,128]{2,1,0:T(8,128)(2,1)S(1)}, bf16[8,128,128]{2,1,0:T(8,128)(2,1)S(1)}, u32[]{:S(2)}, u32[]{:S(2)}) collective-permute-start(bf16[8,128,128]{2,1,0:T(8,128)(2,1)S(1)} %collective-permute-done.22.refs_2_), channel_id=1, source_target_pairs={{0,1},{1,0},{2,3},{3,2},{4,5},{5,4},{6,7},{7,6},{8,9},{9,8},{10,11... | collective-permute-start | bytes 786440 | tf_op jit(solution)/shard_map/ppermute | solution.py:36
  25.6 2.0 %collective-permute-start.5 = (bf16[8,128,128]{2,1,0:T(8,128)(2,1)}, bf16[8,128,128]{2,1,0:T(8,128)(2,1)S(1)}, u32[]{:S(2)}, u32[]{:S(2)}) collective-permute-start(bf16[8,128,128]{2,1,0:T(8,128)(2,1)} %get-tuple-element.26.refs_0_), channel_id=1, source_target_pairs={{0,2},{1,3},{2,4},{3,5},{4,6},{5,7},{6,0},{7,1},{8,10},{9,11},{10,... | collective-permute-start | bytes 786440 | tf_op jit(solution)/shard_map/ppermute | solution.py:32
  28.3 4.6 %copy-done = bf16[1,1,384,128,128]{4,3,2,1,0:T(8,128)(2,1)S(1)} copy-done((bf16[1,1,384,128,128]{4,3,2,1,0:T(8,128)(2,1)S(1)}, bf16[1,1,384,128,128]{4,3,2,1,0:T(8,128)(2,1)}, u32[]{:S(2)}) %copy-start) | copy-done | bytes 12582936
  33.8 8.9 %tile_products.3 = (bf16[16,128,128]{2,1,0:T(8,128)(2,1)S(1)}, bf16[16,128,128]{2,1,0:T(8,128)(2,1)S(1)}, bf16[16,128,128]{2,1,0:T(8,128)(2,1)S(1)}, bf16[8,128,...) custom-call(s32[384]{0:T(512)S(1)} %get-tuple-element.73.rmap, ...), custom_call_target="tpu_custom_call" | custom-call | tf_op jit(solution)/shard_map/tile_products/pallas_call | solution.py:102
  47.7 2.3 %collective-permute-start.28 = (bf16[16,128,128]{2,1,0:T(8,128)(2,1)S(1)}, bf16[16,128,128]{2,1,0:T(8,128)(2,1)S(1)}, u32[]{:S(2)}, u32[]{:S(2)}) collective-permute-start(bf16[16,128,128]{2,1,0:T(8,128)(2,1)S(1)} %get-tuple-element.39), channel_id=1, source_target_pairs={{0,24},{8,0},{16,8},{24,16},{32,56},{40,32},{48,40},{56,48},{64,88... | collective-permute-start | bytes 1572872 | tf_op jit(solution)/shard_map/ppermute | solution.py:24
  50.1 8.9 %tile_products.2 = (bf16[16,128,128]{2,1,0:T(8,128)(2,1)S(1)}, bf16[16,128,128]{2,1,0:T(8,128)(2,1)S(1)}, bf16[16,128,128]{2,1,0:T(8,128)(2,1)S(1)}, bf16[8,128,...) custom-call(s32[384]{0:T(512)S(1)} %get-tuple-element.73.rmap, ...), custom_call_target="tpu_custom_call" | custom-call | tf_op jit(solution)/shard_map/tile_products/pallas_call | solution.py:102
  59.1 2.7 %collective-permute-start.14 = (bf16[16,128,128]{2,1,0:T(8,128)(2,1)S(1)}, bf16[16,128,128]{2,1,0:T(8,128)(2,1)S(1)}, u32[]{:S(2)}, u32[]{:S(2)}) collective-permute-start(bf16[16,128,128]{2,1,0:T(8,128)(2,1)S(1)} %get-tuple-element.33), channel_id=1, source_target_pairs={{0,96},{8,104},{16,112},{24,120},{32,0},{40,8},{48,16},{56,24},{64... | collective-permute-start | bytes 1572872 | tf_op jit(solution)/shard_map/ppermute | solution.py:28
  62.0 2.9 %collective-permute-start.7 = (bf16[16,128,128]{2,1,0:T(8,128)(2,1)S(1)}, bf16[16,128,128]{2,1,0:T(8,128)(2,1)S(1)}, u32[]{:S(2)}, u32[]{:S(2)}) collective-permute-start(bf16[16,128,128]{2,1,0:T(8,128)(2,1)S(1)} %get-tuple-element.28), channel_id=1, source_target_pairs={{0,24},{8,0},{16,8},{24,16},{32,56},{40,32},{48,40},{56,48},{64,88... | collective-permute-start | bytes 1572872 | tf_op jit(solution)/shard_map/ppermute | solution.py:24
  65.2 7.9 %collective-permute-done.15 = bf16[16,128,128]{2,1,0:T(8,128)(2,1)S(1)} collective-permute-done((bf16[16,128,128]{2,1,0:T(8,128)(2,1)S(1)}, bf16[16,128,128]{2,1,0:T(8,128)(2,1)S(1)}, u32[]{:S(2)}, u32[]{:S(2)}) %collective-permute-start.15) | collective-permute-done | bytes 524320 | tf_op jit(solution)/shard_map/ppermute | solution.py:28
  80.0 2.2 %collective-permute-start.11 = (bf16[8,128,128]{2,1,0:T(8,128)(2,1)S(1)}, bf16[8,128,128]{2,1,0:T(8,128)(2,1)S(1)}, u32[]{:S(2)}, u32[]{:S(2)}) collective-permute-start(bf16[8,128,128]{2,1,0:T(8,128)(2,1)S(1)} %add_convert_fusion.10), channel_id=1, source_target_pairs={{0,24},{8,0},{16,8},{24,16},{32,56},{40,32},{48,40},{56,48},{64,88... | collective-permute-start | bytes 786440 | tf_op jit(solution)/shard_map/ppermute | solution.py:24
  87.5 2.3 %collective-permute-start.34 = (bf16[4,128,128]{2,1,0:T(8,128)(2,1)S(1)}, bf16[4,128,128]{2,1,0:T(8,128)(2,1)S(1)}, u32[]{:S(2)}, u32[]{:S(2)}) collective-permute-start(bf16[4,128,128]{2,1,0:T(8,128)(2,1)S(1)} %get-tuple-element.64), channel_id=1, source_target_pairs={{0,96},{8,104},{16,112},{24,120},{32,0},{40,8},{48,16},{56,24},{64... | collective-permute-start | bytes 393224 | tf_op jit(solution)/shard_map/ppermute | solution.py:28
  97.4 3.7 %collective-permute-start.13 = (bf16[4,128,128]{2,1,0:T(8,128)(2,1)}, bf16[4,128,128]{2,1,0:T(8,128)(2,1)S(1)}, u32[]{:S(2)}, u32[]{:S(2)}) collective-permute-start(bf16[4,128,128]{2,1,0:T(8,128)(2,1)} %get-tuple-element.68), channel_id=1, source_target_pairs={{0,96},{8,104},{16,112},{24,120},{32,0},{40,8},{48,16},{56,24},{64... | collective-permute-start | bytes 393224 | tf_op jit(solution)/shard_map/ppermute | solution.py:28
  103.4 3.1 %collective-permute-done.10.refs_1_ = bf16[4,128,128]{2,1,0:T(8,128)(2,1)S(1)} collective-permute-done((bf16[4,128,128]{2,1,0:T(8,128)(2,1)S(1)}, bf16[4,128,128]{2,1,0:T(8,128)(2,1)S(1)}, u32[]{:S(2)}, u32[]{:S(2)}) %collective-permute-start.10) | collective-permute-done | bytes 131104 | tf_op jit(solution)/shard_map/ppermute | solution.py:28
  108.1 5.8 %collective-permute-start.42 = (f32[128,256]{1,0:T(8,128)S(1)}, f32[128,256]{1,0:T(8,128)S(1)}, u32[]{:S(2)}, u32[]{:S(2)}) collective-permute-start(f32[128,256]{1,0:T(8,128)S(1)} %constant_dynamic-slice_fusion.4), channel_id=1, source_target_pairs={{0,1},{1,0},{2,3},{3,2},{4,5},{5,4},{6,7},{7,6},{8,9},{9,8},{10,11... | collective-permute-start | bytes 393224 | tf_op jit(solution)/shard_map/ppermute | solution.py:36
  116.3 2.4 %collective-permute-start.45 = (f32[32,256]{1,0:T(8,128)S(1)}, f32[32,256]{1,0:T(8,128)S(1)}, u32[]{:S(2)}, u32[]{:S(2)}) collective-permute-start(f32[32,256]{1,0:T(8,128)S(1)} %get-tuple-element.71), channel_id=1, source_target_pairs={{0,6},{1,7},{2,0},{3,1},{4,2},{5,3},{6,4},{7,5},{8,14},{9,15},{10,... | collective-permute-start | bytes 98312 | tf_op jit(solution)/shard_map/ppermute | solution.py:32
  120.6 2.4 %collective-permute-start.46 = (f32[32,256]{1,0:T(8,128)S(1)}, f32[32,256]{1,0:T(8,128)S(1)}, u32[]{:S(2)}, u32[]{:S(2)}) collective-permute-start(f32[32,256]{1,0:T(8,128)S(1)} %add_add_fusion.2), channel_id=1, source_target_pairs={{0,16},{8,24},{16,0},{24,8},{32,48},{40,56},{48,32},{56,40},{64,80... | collective-permute-start | bytes 98312 | tf_op jit(solution)/shard_map/ppermute | solution.py:24
  123.3 2.4 %collective-permute-start.48 = (f32[32,256]{1,0:T(8,128)S(1)}, f32[32,256]{1,0:T(8,128)S(1)}, u32[]{:S(2)}, u32[]{:S(2)}) collective-permute-start(f32[32,256]{1,0:T(8,128)S(1)} %add_add_fusion.2), channel_id=1, source_target_pairs={{0,24},{8,0},{16,8},{24,16},{32,56},{40,32},{48,40},{56,48},{64,88... | collective-permute-start | bytes 98312 | tf_op jit(solution)/shard_map/ppermute | solution.py:24
  129.2 2.2 %collective-permute-start.51 = (f32[32,256]{1,0:T(8,128)S(1)}, f32[32,256]{1,0:T(8,128)S(1)}, u32[]{:S(2)}, u32[]{:S(2)}) collective-permute-start(f32[32,256]{1,0:T(8,128)S(1)} %add_add_fusion.1), channel_id=1, source_target_pairs={{0,96},{8,104},{16,112},{24,120},{32,0},{40,8},{48,16},{56,24},{64... | collective-permute-start | bytes 98312 | tf_op jit(solution)/shard_map/ppermute | solution.py:28
  132.7 2.6 %collective-permute-start.52 = (f32[32,256]{1,0:T(8,128)S(1)}, f32[32,256]{1,0:T(8,128)S(1)}, u32[]{:S(2)}, u32[]{:S(2)}) collective-permute-start(f32[32,256]{1,0:T(8,128)S(1)} %get-tuple-element.53), channel_id=1, source_target_pairs={{0,6},{1,7},{2,0},{3,1},{4,2},{5,3},{6,4},{7,5},{8,14},{9,15},{10,... | collective-permute-start | bytes 98312 | tf_op jit(solution)/shard_map/ppermute | solution.py:32
  136.3 3.3 %collective-permute-done.53 = f32[32,256]{1,0:T(8,128)S(1)} collective-permute-done((f32[32,256]{1,0:T(8,128)S(1)}, f32[32,256]{1,0:T(8,128)S(1)}, u32[]{:S(2)}, u32[]{:S(2)}) %collective-permute-start.53) | collective-permute-done | bytes 32800 | tf_op jit(solution)/shard_map/ppermute | solution.py:32
  139.7 6.0 %collective-permute-start.55 = (f32[128,256]{1,0:T(8,128)S(1)}, f32[128,256]{1,0:T(8,128)S(1)}, u32[]{:S(2)}, u32[]{:S(2)}) collective-permute-start(f32[128,256]{1,0:T(8,128)S(1)} %constant_dynamic-slice_fusion), channel_id=1, source_target_pairs={{0,1},{1,0},{2,3},{3,2},{4,5},{5,4},{6,7},{7,6},{8,9},{9,8},{10,11... | collective-permute-start | bytes 393224 | tf_op jit(solution)/shard_map/ppermute | solution.py:36
  (150 shorter events, 51.6 us)
Async XLA Ops:
  2.7 15.3 %collective-permute-start.22 = (bf16[8,128,128]{2,1,0:T(8,128)(2,1)}, bf16[8,128,128]{2,1,0:T(8,128)(2,1)S(1)}, u32[]{:S(2)}, u32[]{:S(2)}) collective-permute-start(bf16[8,128,128]{2,1,0:T(8,128)(2,1)} %get-tuple-element.37.refs_0_), channel_id=1, source_target_pairs={{0,6},{1,7},{2,0},{3,1},{4,2},{5,3},{6,4},{7,5},{8,14},{9,15},{10,... | collective-permute-start | bytes 786440 | tf_op jit(solution)/shard_map/ppermute | solution.py:32
  7.3 13.6 %collective-permute-start.24 = (bf16[8,128,128]{2,1,0:T(8,128)(2,1)}, bf16[8,128,128]{2,1,0:T(8,128)(2,1)S(1)}, u32[]{:S(2)}, u32[]{:S(2)}) collective-permute-start(bf16[8,128,128]{2,1,0:T(8,128)(2,1)} %get-tuple-element.37.refs_0_), channel_id=1, source_target_pairs={{0,4},{1,5},{2,6},{3,7},{4,0},{5,1},{6,2},{7,3},{8,12},{9,13},{10,... | collective-permute-start | bytes 786440 | tf_op jit(solution)/shard_map/ppermute | solution.py:32
  7.3 14.9 %collective-permute-start.26 = (bf16[8,128,128]{2,1,0:T(8,128)(2,1)}, bf16[8,128,128]{2,1,0:T(8,128)(2,1)S(1)}, u32[]{:S(2)}, u32[]{:S(2)}) collective-permute-start(bf16[8,128,128]{2,1,0:T(8,128)(2,1)} %get-tuple-element.37.refs_0_), channel_id=1, source_target_pairs={{0,2},{1,3},{2,4},{3,5},{4,6},{5,7},{6,0},{7,1},{8,10},{9,11},{10,... | collective-permute-start | bytes 786440 | tf_op jit(solution)/shard_map/ppermute | solution.py:32
  8.0 17.2 %collective-permute-start.21 = (bf16[8,128,128]{2,1,0:T(8,128)(2,1)}, bf16[8,128,128]{2,1,0:T(8,128)(2,1)S(1)}, u32[]{:S(2)}, u32[]{:S(2)}) collective-permute-start(bf16[8,128,128]{2,1,0:T(8,128)(2,1)} %get-tuple-element.37.refs_0_), channel_id=1, source_target_pairs={{0,1},{1,0},{2,3},{3,2},{4,5},{5,4},{6,7},{7,6},{8,9},{9,8},{10,11... | collective-permute-start | bytes 786440 | tf_op jit(solution)/shard_map/ppermute | solution.py:36
  9.5 34.6 %collective-permute-start.1 = (bf16[8,128,128]{2,1,0:T(8,128)(2,1)}, bf16[8,128,128]{2,1,0:T(8,128)(2,1)S(1)}, u32[]{:S(2)}, u32[]{:S(2)}) collective-permute-start(bf16[8,128,128]{2,1,0:T(8,128)(2,1)} %get-tuple-element.26.refs_0_), channel_id=1, source_target_pairs={{0,6},{1,7},{2,0},{3,1},{4,2},{5,3},{6,4},{7,5},{8,14},{9,15},{10,... | collective-permute-start | bytes 786440 | tf_op jit(solution)/shard_map/ppermute | solution.py:32
  25.2 19.2 %collective-permute-start.3 = (bf16[8,128,128]{2,1,0:T(8,128)(2,1)}, bf16[8,128,128]{2,1,0:T(8,128)(2,1)S(1)}, u32[]{:S(2)}, u32[]{:S(2)}) collective-permute-start(bf16[8,128,128]{2,1,0:T(8,128)(2,1)} %get-tuple-element.26.refs_0_), channel_id=1, source_target_pairs={{0,4},{1,5},{2,6},{3,7},{4,0},{5,1},{6,2},{7,3},{8,12},{9,13},{10,... | collective-permute-start | bytes 786440 | tf_op jit(solution)/shard_map/ppermute | solution.py:32
  25.6 20.1 %collective-permute-start.5 = (bf16[8,128,128]{2,1,0:T(8,128)(2,1)}, bf16[8,128,128]{2,1,0:T(8,128)(2,1)S(1)}, u32[]{:S(2)}, u32[]{:S(2)}) collective-permute-start(bf16[8,128,128]{2,1,0:T(8,128)(2,1)} %get-tuple-element.26.refs_0_), channel_id=1, source_target_pairs={{0,2},{1,3},{2,4},{3,5},{4,6},{5,7},{6,0},{7,1},{8,10},{9,11},{10,... | collective-permute-start | bytes 786440 | tf_op jit(solution)/shard_map/ppermute | solution.py:32
  27.6 18.8 %collective-permute-start = (bf16[8,128,128]{2,1,0:T(8,128)(2,1)}, bf16[8,128,128]{2,1,0:T(8,128)(2,1)S(1)}, u32[]{:S(2)}, u32[]{:S(2)}) collective-permute-start(bf16[8,128,128]{2,1,0:T(8,128)(2,1)} %get-tuple-element.26.refs_0_), channel_id=1, source_target_pairs={{0,1},{1,0},{2,3},{3,2},{4,5},{5,4},{6,7},{7,6},{8,9},{9,8},{10,11... | collective-permute-start | bytes 786440 | tf_op jit(solution)/shard_map/ppermute | solution.py:36
  42.7 16.4 %collective-permute-start.36 = (bf16[16,128,128]{2,1,0:T(8,128)(2,1)S(1)}, bf16[16,128,128]{2,1,0:T(8,128)(2,1)S(1)}, u32[]{:S(2)}, u32[]{:S(2)}) collective-permute-start(bf16[16,128,128]{2,1,0:T(8,128)(2,1)S(1)} %get-tuple-element.46), channel_id=1, source_target_pairs={{0,32},{8,40},{16,48},{24,56},{32,64},{40,72},{48,80},{56,88},{64,... | collective-permute-start | bytes 1572872 | tf_op jit(solution)/shard_map/ppermute | solution.py:28
  44.4 17.5 %collective-permute-start.35 = (bf16[16,128,128]{2,1,0:T(8,128)(2,1)S(1)}, bf16[16,128,128]{2,1,0:T(8,128)(2,1)S(1)}, u32[]{:S(2)}, u32[]{:S(2)}) collective-permute-start(bf16[16,128,128]{2,1,0:T(8,128)(2,1)S(1)} %get-tuple-element.44), channel_id=1, source_target_pairs={{0,96},{8,104},{16,112},{24,120},{32,0},{40,8},{48,16},{56,24},{64... | collective-permute-start | bytes 1572872 | tf_op jit(solution)/shard_map/ppermute | solution.py:28
  46.5 15.5 %collective-permute-start.29 = (bf16[16,128,128]{2,1,0:T(8,128)(2,1)S(1)}, bf16[16,128,128]{2,1,0:T(8,128)(2,1)S(1)}, u32[]{:S(2)}, u32[]{:S(2)}) collective-permute-start(bf16[16,128,128]{2,1,0:T(8,128)(2,1)S(1)} %get-tuple-element.41), channel_id=1, source_target_pairs={{0,8},{8,16},{16,24},{24,0},{32,40},{40,48},{48,56},{56,32},{64,72... | collective-permute-start | bytes 1572872 | tf_op jit(solution)/shard_map/ppermute | solution.py:24
  47.7 17.3 %collective-permute-start.28 = (bf16[16,128,128]{2,1,0:T(8,128)(2,1)S(1)}, bf16[16,128,128]{2,1,0:T(8,128)(2,1)S(1)}, u32[]{:S(2)}, u32[]{:S(2)}) collective-permute-start(bf16[16,128,128]{2,1,0:T(8,128)(2,1)S(1)} %get-tuple-element.39), channel_id=1, source_target_pairs={{0,24},{8,0},{16,8},{24,16},{32,56},{40,32},{48,40},{56,48},{64,88... | collective-permute-start | bytes 1572872 | tf_op jit(solution)/shard_map/ppermute | solution.py:24
  59.0 14.1 %collective-permute-start.15 = (bf16[16,128,128]{2,1,0:T(8,128)(2,1)S(1)}, bf16[16,128,128]{2,1,0:T(8,128)(2,1)S(1)}, u32[]{:S(2)}, u32[]{:S(2)}) collective-permute-start(bf16[16,128,128]{2,1,0:T(8,128)(2,1)S(1)} %get-tuple-element.35), channel_id=1, source_target_pairs={{0,32},{8,40},{16,48},{24,56},{32,64},{40,72},{48,80},{56,88},{64,... | collective-permute-start | bytes 1572872 | tf_op jit(solution)/shard_map/ppermute | solution.py:28
  59.1 14.2 %collective-permute-start.14 = (bf16[16,128,128]{2,1,0:T(8,128)(2,1)S(1)}, bf16[16,128,128]{2,1,0:T(8,128)(2,1)S(1)}, u32[]{:S(2)}, u32[]{:S(2)}) collective-permute-start(bf16[16,128,128]{2,1,0:T(8,128)(2,1)S(1)} %get-tuple-element.33), channel_id=1, source_target_pairs={{0,96},{8,104},{16,112},{24,120},{32,0},{40,8},{48,16},{56,24},{64... | collective-permute-start | bytes 1572872 | tf_op jit(solution)/shard_map/ppermute | solution.py:28
  61.8 13.5 %collective-permute-start.8 = (bf16[16,128,128]{2,1,0:T(8,128)(2,1)S(1)}, bf16[16,128,128]{2,1,0:T(8,128)(2,1)S(1)}, u32[]{:S(2)}, u32[]{:S(2)}) collective-permute-start(bf16[16,128,128]{2,1,0:T(8,128)(2,1)S(1)} %get-tuple-element.30), channel_id=1, source_target_pairs={{0,8},{8,16},{16,24},{24,0},{32,40},{40,48},{48,56},{56,32},{64,72... | collective-permute-start | bytes 1572872 | tf_op jit(solution)/shard_map/ppermute | solution.py:24
  62.0 14.3 %collective-permute-start.7 = (bf16[16,128,128]{2,1,0:T(8,128)(2,1)S(1)}, bf16[16,128,128]{2,1,0:T(8,128)(2,1)S(1)}, u32[]{:S(2)}, u32[]{:S(2)}) collective-permute-start(bf16[16,128,128]{2,1,0:T(8,128)(2,1)S(1)} %get-tuple-element.28), channel_id=1, source_target_pairs={{0,24},{8,0},{16,8},{24,16},{32,56},{40,32},{48,40},{56,48},{64,88... | collective-permute-start | bytes 1572872 | tf_op jit(solution)/shard_map/ppermute | solution.py:24
  65.0 13.7 %collective-permute-start.37 = (bf16[8,128,128]{2,1,0:T(8,128)(2,1)S(1)}, bf16[8,128,128]{2,1,0:T(8,128)(2,1)S(1)}, u32[]{:S(2)}, u32[]{:S(2)}) collective-permute-start(bf16[8,128,128]{2,1,0:T(8,128)(2,1)S(1)} %add_convert_fusion.2), channel_id=1, source_target_pairs={{0,32},{8,40},{16,48},{24,56},{32,64},{40,72},{48,80},{56,88},{64,... | collective-permute-start | bytes 786440 | tf_op jit(solution)/shard_map/ppermute | solution.py:28
  82.2 8.5 %collective-permute-start.40 = (bf16[4,128,128]{2,1,0:T(8,128)(2,1)S(1)}, bf16[4,128,128]{2,1,0:T(8,128)(2,1)S(1)}, u32[]{:S(2)}, u32[]{:S(2)}) collective-permute-start(bf16[4,128,128]{2,1,0:T(8,128)(2,1)S(1)} %get-tuple-element.63), channel_id=1, source_target_pairs={{0,16},{8,24},{16,0},{24,8},{32,48},{40,56},{48,32},{56,40},{64,80... | collective-permute-start | bytes 393224 | tf_op jit(solution)/shard_map/ppermute | solution.py:24
  84.8 8.4 %collective-permute-start.38 = (bf16[4,128,128]{2,1,0:T(8,128)(2,1)S(1)}, bf16[4,128,128]{2,1,0:T(8,128)(2,1)S(1)}, u32[]{:S(2)}, u32[]{:S(2)}) collective-permute-start(bf16[4,128,128]{2,1,0:T(8,128)(2,1)S(1)} %slice.232), channel_id=1, source_target_pairs={{0,8},{8,16},{16,24},{24,0},{32,40},{40,48},{48,56},{56,32},{64,72... | collective-permute-start | bytes 393224 | tf_op jit(solution)/shard_map/ppermute | solution.py:24
  86.3 8.6 %collective-permute-start.33 = (bf16[4,128,128]{2,1,0:T(8,128)(2,1)S(1)}, bf16[4,128,128]{2,1,0:T(8,128)(2,1)S(1)}, u32[]{:S(2)}, u32[]{:S(2)}) collective-permute-start(bf16[4,128,128]{2,1,0:T(8,128)(2,1)S(1)} %get-tuple-element.65), channel_id=1, source_target_pairs={{0,64},{8,72},{16,80},{24,88},{32,96},{40,104},{48,112},{56,120},{... | collective-permute-start | bytes 393224 | tf_op jit(solution)/shard_map/ppermute | solution.py:28
  87.5 8.1 %collective-permute-start.34 = (bf16[4,128,128]{2,1,0:T(8,128)(2,1)S(1)}, bf16[4,128,128]{2,1,0:T(8,128)(2,1)S(1)}, u32[]{:S(2)}, u32[]{:S(2)}) collective-permute-start(bf16[4,128,128]{2,1,0:T(8,128)(2,1)S(1)} %get-tuple-element.64), channel_id=1, source_target_pairs={{0,96},{8,104},{16,112},{24,120},{32,0},{40,8},{48,16},{56,24},{64... | collective-permute-start | bytes 393224 | tf_op jit(solution)/shard_map/ppermute | solution.py:28
  91.1 10.1 %collective-permute-start.19 = (bf16[4,128,128]{2,1,0:T(8,128)(2,1)S(1)}, bf16[4,128,128]{2,1,0:T(8,128)(2,1)S(1)}, u32[]{:S(2)}, u32[]{:S(2)}) collective-permute-start(bf16[4,128,128]{2,1,0:T(8,128)(2,1)S(1)} %get-tuple-element.67), channel_id=1, source_target_pairs={{0,16},{8,24},{16,0},{24,8},{32,48},{40,56},{48,32},{56,40},{64,80... | collective-permute-start | bytes 393224 | tf_op jit(solution)/shard_map/ppermute | solution.py:24
  93.2 10.0 %collective-permute-start.20 = (bf16[4,128,128]{2,1,0:T(8,128)(2,1)}, bf16[4,128,128]{2,1,0:T(8,128)(2,1)S(1)}, u32[]{:S(2)}, u32[]{:S(2)}) collective-permute-start(bf16[4,128,128]{2,1,0:T(8,128)(2,1)} %get-tuple-element.66), channel_id=1, source_target_pairs={{0,24},{8,0},{16,8},{24,16},{32,56},{40,32},{48,40},{56,48},{64,88... | collective-permute-start | bytes 393224 | tf_op jit(solution)/shard_map/ppermute | solution.py:24
  94.9 8.4 %collective-permute-start.17 = (bf16[4,128,128]{2,1,0:T(8,128)(2,1)S(1)}, bf16[4,128,128]{2,1,0:T(8,128)(2,1)S(1)}, u32[]{:S(2)}, u32[]{:S(2)}) collective-permute-start(bf16[4,128,128]{2,1,0:T(8,128)(2,1)S(1)} %slice.234), channel_id=1, source_target_pairs={{0,8},{8,16},{16,24},{24,0},{32,40},{40,48},{48,56},{56,32},{64,72... | collective-permute-start | bytes 393224 | tf_op jit(solution)/shard_map/ppermute | solution.py:24
  (39 other events, 318.1 us)

commit v2 on v0

v2 whole, which is shorter than its diff:
```python
import functools

import jax
import jax.numpy as jnp
from jax import lax
from jax.experimental import pallas as pl
from jax.experimental.pallas import tpu as pltpu
from jax.sharding import PartitionSpec as P

F32, BF16 = jnp.float32, jnp.bfloat16
B = 128
NY = NX = NZ = 4
HALF = 64
UNROLL = 16
FW = 256
KT = 384
VMEM = pl.BlockSpec(memory_space=pltpu.VMEM)
SMEM = pl.BlockSpec(memory_space=pltpu.SMEM)
ANY = pl.BlockSpec(memory_space=pl.ANY)


def params(mib):
    return pltpu.CompilerParams(vmem_limit_bytes=mib * 2**20)


def shaped(shape, dtype=BF16):
    return jax.ShapeDtypeStruct(shape, dtype)


XP = [[(y * NX + x, y * NX + (x + s) % NX) for y in range(NY) for x in range(NX)] for s in range(4)]
YP = [[(y * NX + x, (y + s) % NY * NX + x) for y in range(NY) for x in range(NX)] for s in range(4)]
ZP = [[(z * 2 + c, (z + s) % NZ * 2 + c) for z in range(NZ) for c in range(2)] for s in range(4)]
CP = [(z * 2 + c, z * 2 + 1 - c) for z in range(NZ) for c in range(2)]


def xperm(v, s):
    return lax.ppermute(v, "row", XP[s])


def yperm(v, s):
    return lax.ppermute(v, "row", YP[s])


def zperm(v, s):
    return lax.ppermute(v, "col", ZP[s])


def cperm(v):
    return lax.ppermute(v, "col", CP)


def panels_kernel(x_ref, out_ref):
    for b in range(8):
        out_ref[b] = x_ref[b * B : (b + 1) * B, :].astype(F32).T.astype(BF16)


def panels(out_grad):
    return pl.pallas_call(
        panels_kernel,
        out_shape=shaped((8, FW, B)),
        compiler_params=params(6),
        name="panels",
    )(out_grad)


def codes_kernel(at, row_block, col_block, live, after, code):
    y, x, z, core = (at[i] for i in range(4))
    rb, cb = row_block[...], col_block[...]
    src = rb >> 3
    panel = (((src + core) & 1) << 5) + ((((src >> 1) - z) & 3) << 3) + (rb & 7)
    dest, b = cb >> 3, cb & 7
    rx, ry = (dest - x) & 3, ((dest >> 2) - y) & 3
    in_first = b < 4
    major, minor = jnp.where(in_first, rx, ry), jnp.where(in_first, ry, rx)
    low = minor < 2
    kept = (major == 0) | (low & (major == 1)) | ((minor >= 2) & (major == 3))
    kept_at = minor * 4 + jnp.where(major == 0, 0, 16)
    far = minor * 4 + jnp.where(low, 0, 8)
    near = minor * 4 + jnp.where(major == 1, 0, 24)
    sent_at = jnp.where(major == 2, far, near)
    target = jnp.where(kept, kept_at, sent_at) + (b & 3) + jnp.where(in_first, 0, 32)
    group = jnp.where(live[...] > 0, jnp.where(kept, 1, 0), 2)
    tile = lax.broadcasted_iota(jnp.int32, rb.shape, 2)
    code[...] = (group << 23) + (target << 15) + (panel << 9) + tile


def codes(at, row_block, col_block, live, after):
    return pl.pallas_call(
        codes_kernel,
        in_specs=[SMEM] + [VMEM] * 3 + [ANY],
        out_shape=shaped((1, 1, KT), jnp.int32),
        compiler_params=params(4),
        name="codes",
    )(at, row_block, col_block, live, after)


def again_kernel(a, b, c, *refs):
    for source, target in zip((a, b, c), refs[-3:]):
        target[...] = source[...]


def again(arrays, after):
    return pl.pallas_call(
        again_kernel,
        in_specs=[VMEM] * 3 + [ANY] * len(after),
        out_shape=[shaped(a.shape) for a in arrays],
        compiler_params=params(6),
        name="again",
    )(*arrays, *after)


def stage_kernel(tiles, code, place, after, held, first, second, count, masks, sem):
    copy = pltpu.make_async_copy(tiles, held, sem)
    copy.start()
    for i in range(2):
        masks[i] = jnp.full((8, 256), place[i], jnp.int32)

    def step(g, counts):
        a, b = counts
        for u in range(8):
            v = code[0, 0, g * 8 + u]
            group = v >> 23
            entry = v & (2**23 - 1)
            first[a] = entry
            second[b] = entry
            a = a + (group == 0).astype(jnp.int32)
            b = b + (group & 1)
        return a, b

    a, b = lax.fori_loop(0, KT // 8, step, (jnp.int32(0), jnp.int32(0)))
    for u in range(UNROLL):
        first[a + u] = HALF * 2**15
        second[b + u] = HALF * 2**15
    count[0] = (a + UNROLL - 1) // UNROLL
    count[1] = (b + UNROLL - 1) // UNROLL
    copy.wait()


def stage(tiles, code, place, after):
    return pl.pallas_call(
        stage_kernel,
        in_specs=[ANY, SMEM, SMEM, ANY],
        out_specs=[VMEM, SMEM, SMEM, SMEM, VMEM],
        out_shape=[
            shaped((KT, B, B)),
            shaped((KT + UNROLL,), jnp.int32),
            shaped((KT + UNROLL,), jnp.int32),
            shaped((2,), jnp.int32),
            shaped((2, 8, 256), jnp.int32),
        ],
        scratch_shapes=[pltpu.SemaphoreType.DMA(())],
        compiler_params=params(16),
        name="stage",
    )(tiles, code, place, after)


def products(which, entries, count, tiles, x, acc):
    acc[...] = jnp.zeros_like(acc)

    def step(g, carry):
        targets, values = [], []
        for u in range(UNROLL):
            v = entries[g * UNROLL + u]
            c = v >> 15
            r = (v >> 9) & 63
            k = v & 511
            targets.append(c)
            values.append(jnp.dot(x[r], tiles[k], preferred_element_type=F32))
        for c, value in zip(targets, values):
            acc[c] += value
        return carry

    lax.fori_loop(0, count[which], step, 0)


def write_out(acc, outs):
    at = 0
    for out in outs:
        n = out.shape[0]
        out[...] = acc[pl.ds(at, n)].astype(BF16)
        at += n


SEND = (16, 16) * 2
KEEP = (16, 8, 8) * 2


def send_kernel(entries, count, tiles, *refs):
    xs, x, outs, acc = refs[:8], refs[8], refs[9:13], refs[13]
    for i in range(8):
        x[i * 8 : (i + 1) * 8] = xs[i][...]
    products(0, entries, count, tiles, x, acc)
    write_out(acc, outs)


def keep_kernel(entries, count, tiles, x, *refs):
    outs, acc = refs[:6], refs[6]
    products(1, entries, count, tiles, x, acc)
    write_out(acc, outs)


ACC = pltpu.VMEM((HALF + 1, FW, B), F32)


def send_products(entries, count, tiles, xs):
    out = pl.pallas_call(
        send_kernel,
        in_specs=[SMEM, SMEM, VMEM] + [VMEM] * 8,
        out_specs=[VMEM] * 5,
        out_shape=[shaped((n, FW, B)) for n in (64,) + SEND],
        scratch_shapes=[ACC],
        compiler_params=params(12),
        name="send_products",
    )(entries, count, tiles, *xs)
    return out[0], out[1:]


def keep_products(entries, count, tiles, x):
    return pl.pallas_call(
        keep_kernel,
        in_specs=[SMEM, SMEM, VMEM, VMEM],
        out_specs=[VMEM] * 6,
        out_shape=[shaped((n, FW, B)) for n in KEEP],
        scratch_shapes=[ACC],
        compiler_params=params(12),
        name="keep_products",
    )(entries, count, tiles, x)


def middle_kernel(*refs):
    received, outs = refs[:10], refs[10:]
    for half in range(2):
        own, rp, rm, sp, sm = received[half * 5 : half * 5 + 5]
        for place in range(4):
            out = outs[half * 4 + place]
            for i in range(4):
                n = place * 4 + i
                if place < 2:
                    s = own[n].astype(F32) + rm[8 + n].astype(F32) + sp[n].astype(F32)
                else:
                    s = own[n].astype(F32) + rp[n].astype(F32) + sm[n - 8].astype(F32)
                out[i] = s.astype(out.dtype)


def middle(received):
    dtypes = (F32, BF16, BF16, BF16) * 2
    return pl.pallas_call(
        middle_kernel,
        out_shape=[shaped((4, FW, B), t) for t in dtypes],
        compiler_params=params(14),
        name="middle",
    )(*received)


def finish_kernel(*refs):
    parts, (feat, weight, ig, wg) = refs[:8], refs[8:]
    total = jnp.zeros((FW, 256), F32)
    for b in range(8):
        four = parts[b // 4 * 4 : b // 4 * 4 + 4]
        i = b % 4
        rows = slice(b * B, (b + 1) * B)
        s = four[0][i] + four[1][i].astype(F32)
        cg = (s + four[2][i].astype(F32) + four[3][i].astype(F32)).astype(BF16)
        total = total + jnp.dot(cg, feat[rows, :], preferred_element_type=F32)
        ig[rows, :] = lax.dot_general(
            cg, weight[...], (((0,), (1,)), ((), ())), preferred_element_type=F32
        ).astype(BF16)
    wg[...] = total


def finish(parts, features, weight):
    return pl.pallas_call(
        finish_kernel,
        out_shape=[shaped((8 * B, 256)), shaped((FW, 256), F32)],
        compiler_params=params(10),
        name="finish",
    )(*parts, features, weight)


def f32(v):
    return v.astype(F32)


def split(v, at):
    n = v.shape[0] // 2
    low, high = v[:n], v[n:]
    return jnp.where(at == 0, low, high), jnp.where(at == 0, high, low)


def unite(mine, other, at):
    return jnp.concatenate([jnp.where(at == 0, mine, other), jnp.where(at == 0, other, mine)], axis=0)


def all_sum(v, masks):
    core, z = masks[0, :1], masks[1, :1]
    mine, other = split(v, core)
    v = mine + lax.ppermute(other, "col", CP)
    n = v.shape[0] // 4
    pieces = [v[i * n : (i + 1) * n] for i in range(4)]

    def piece(k):
        at = (z + k) & 3
        return jnp.where(at < 2, jnp.where(at == 0, pieces[0], pieces[1]), jnp.where(at == 2, pieces[2], pieces[3]))

    v = (piece(0) + zperm(piece(2), 2)) + (zperm(piece(1), 1) + zperm(piece(3), 3))
    v = (v + xperm(v, 2)) + (xperm(v, 1) + xperm(v, 3))
    v = (v + yperm(v, 2)) + (yperm(v, 1) + yperm(v, 3))
    four = [v, zperm(v, 3), zperm(v, 2), zperm(v, 1)]

    def placed(i):
        at = (i - z) & 3
        return jnp.where(at < 2, jnp.where(at == 0, four[0], four[1]), jnp.where(at == 2, four[2], four[3]))

    v = jnp.concatenate([placed(i) for i in range(4)], axis=0)
    return unite(v, cperm(v), core)


def local(out_grad, features, weight, tiles, row_block, col_block, live):
    row, col = lax.axis_index("row"), lax.axis_index("col")
    y, x, z, core = row // NX, row % NX, col // 2, col % 2
    own = panels(out_grad)
    own_turned = cperm(own)
    one, three, two = zperm(own, 1), zperm(own, 3), zperm(own, 2)
    at = jnp.stack([y, x, z, core]).astype(jnp.int32)
    place = jnp.stack([core, z]).astype(jnp.int32)
    code = codes(at, row_block, col_block, live, own)
    held, first, second, count, masks = stage(tiles[0, 0], code, place, own)
    one, three, two = again((one, three, two), [held])
    xs = [own, three, two, one, own_turned, cperm(three), cperm(two), cperm(one)]

    ways = ((xperm, 1), (xperm, 3), (yperm, 1), (yperm, 3))

    def swap(buffers):
        return [perm(v, s) for v, (perm, s) in zip(buffers, ways)]

    stacked, send = send_products(first, count, held, xs)
    got = swap(send)
    keep = keep_products(second, count, held, stacked)
    turned = [keep[1], keep[2], keep[4], keep[5]]
    more = swap([(f32(v) + f32(g[:8])).astype(BF16) for v, g in zip(turned, got)])
    received = [keep[0], *got[:2], *more[:2], keep[3], *got[2:], *more[2:]]
    sums = middle(received)
    parts = [sums[0]] + [yperm(sums[k], k) for k in (1, 2, 3)]
    parts += [sums[4]] + [xperm(sums[4 + k], k) for k in (1, 2, 3)]
    input_grad, wg = finish(parts, features, weight)
    nodes = 1024 * 128
    return input_grad, all_sum(wg, masks).T * nodes ** (-0.5)


def solution(mesh):
    return jax.shard_map(
        local,
        mesh=mesh,
        in_specs=(
            P(("row", "col"), None),
            P(("col", "row"), None),
            P(),
            P("row", "col", None, None, None),
            P("row", "col", None),
            P("row", "col", None),
            P("row", "col", None),
        ),
        out_specs=(P(("col", "row"), None), P()),
        check_vma=False,
    )
```

time: 530 us -> 142 us (0.27)
  waiting for transfers between devices: 289 us -> 64 us
  other arithmetic: 118 us -> 1 us
  local copies, waits for them, and re-layouts: 72.6 us -> 8.5 us
  starting transfers between devices: 0.12 us -> 53.5 us
  matrix products: 36.3 us -> 0 us
  Pallas kernels: 0 us -> 13.9 us
  between operations: 13.8 us -> 0.85 us
    psum x1 -> x0, waiting for transfers between devices: 142 us -> none  [local(): summed_weight = lax.psum(local_weight, ('row', 'col'))]
    scatter-add x1 -> x0, other arithmetic: 115 us -> none  [local(): jax.ops.segment_sum(contrib, col_ids, num_segments=column_count)]
    reduce_scatter x1 -> x0, waiting for transfers between devices: 110 us -> none  [local(): lax.psum_scatter(partial_value, 'row', scatter_dimension=0, tiled=True)]
    ppermute x0 -> x35, waiting for transfers between devices: none -> 64 us  [the longest x10 28.2 us: xperm(): return lax.ppermute(v, 'row', XP[s])]
    ppermute x0 -> x35, starting transfers between devices: none -> 53.5 us  [the longest x10 14.1 us: yperm(): return lax.ppermute(v, 'row', YP[s])]
    mul x1 -> x0, local copies, waits for them, and re-layouts: 48.8 us -> none  [local(): contrib = contrib * live_weights[:, None, None]]
    dot_general x3 -> x0, matrix products: 36.3 us -> none  [the longest x1 31.7 us: local(): jnp.einsum('kij,kif->kjf', tile_set, panels, preferred_element_type=jnp.f...]
    all_gather x1 -> x0, waiting for transfers between devices: 35.7 us -> none  [local(): group_rows = lax.all_gather(out_grad, 'col', axis=0, tiled=True)]
  transfers between devices with their start and end apart: 3 -> 35, of which waited for: 3 -> 26; matrix products, arithmetic and copies ran while one was open for 1% -> 1% of each run, Pallas kernels for 0% -> 5%
where the time goes in v2:
time: 142 us
  waiting for transfers between devices  64 us (45%)
  starting transfers between devices  53.5 us (38%)
  Pallas kernels  13.9 us (10%)
  local copies, waits for them, and re-layouts  8.5 us (6%)
    ppermute x10, waiting for transfers between devices, xperm(): return lax.ppermute(v, 'row', XP[s])  28.2 us
    ppermute x10, waiting for transfers between devices, yperm(): return lax.ppermute(v, 'row', YP[s])  16.4 us
    ppermute x9, waiting for transfers between devices, zperm(): return lax.ppermute(v, 'col', ZP[s])  14.9 us
    ppermute x10, starting transfers between devices, yperm(): return lax.ppermute(v, 'row', YP[s])  14.1 us
    ppermute x9, starting transfers between devices, zperm(): return lax.ppermute(v, 'col', ZP[s])  13.5 us
    ppermute x10, starting transfers between devices, xperm(): return lax.ppermute(v, 'row', XP[s])  13.5 us
    ppermute x5, starting transfers between devices, cperm(): return lax.ppermute(v, 'col', CP)  10.1 us
    unnamed x15, local copies, waits for them, and re-layouts  8.5 us
  transfers between devices with their start and end apart: 35, of which 26 were waited for; matrix products, arithmetic and copies ran while one was open for 1% of the time, Pallas kernels for 5%

profile of v2, /device:TPU:1, one launch (start us, length us, event | category | flops | bytes accessed | tf_op | source)
XLA Modules:
  0.0 141.7 jit_solution(15982843066941173984)
XLA Ops:
  1.9 4.5 %collective-permute-start.2 = (bf16[8,256,128]{2,1,0:T(8,128)(2,1)S(1)}, bf16[8,256,128]{2,1,0:T(8,128)(2,1)S(1)}, u32[]{:S(2)}, u32[]{:S(2)}) collective-permute-start(bf16[8,256,128]{2,1,0:T(8,128)(2,1)S(1)} %panels.1.after.refs_0_), channel_id=1, source_target_pairs={{0,4},{1,5},{2,6},{3,7},{4,0},{5,1},{6,2},{7,3},{8,12},{9,13},{10,... | collective-permute-start | bytes 1572872 | tf_op jit(solution)/shard_map/ppermute | solution.py:45
  12.1 4.6 %copy-done = bf16[1,1,384,128,128]{4,3,2,1,0:T(8,128)(2,1)S(1)} copy-done((bf16[1,1,384,128,128]{4,3,2,1,0:T(8,128)(2,1)S(1)}, bf16[1,1,384,128,128]{4,3,2,1,0:T(8,128)(2,1)}, u32[]{:S(2)}) %copy-start) | copy-done | bytes 12582936
  16.7 3.7 %stage.1 = (bf16[384,128,128]{2,1,0:T(8,128)(2,1)S(1)}, s32[400]{0:T(512)S(1)}, s32[400]{0:T(512)S(1)}, s32[2]{0:T(128)S(1)}, s32[2,8,256]{2,1,0:T(8,128)S(1)}) custom-call(bf16[384,128,128]{2,1,0:T(8,128)(2,1)S(1)} %bitcast.7, s32[1,1,384]{2,1,0:T(1,128)S(1)} %codes.1.code, s32[2]{0:T(128)S(1)} %pad_add_fusion.1.place, ...), custom_call_target="tpu_custom_call" | custom-call | tf_op jit(solution)/shard_map/stage/pallas_call | solution.py:140
  20.4 9.3 %collective-permute-done.1.b = bf16[8,256,128]{2,1,0:T(8,128)(2,1)S(1)} collective-permute-done((bf16[8,256,128]{2,1,0:T(8,128)(2,1)S(1)}, bf16[8,256,128]{2,1,0:T(8,128)(2,1)S(1)}, u32[]{:S(2)}, u32[]{:S(2)}) %collective-permute-start.1) | collective-permute-done | bytes 524320 | tf_op jit(solution)/shard_map/ppermute | solution.py:45
  34.5 3.6 %send_products.1 = (bf16[64,256,128]{2,1,0:T(8,128)(2,1)S(1)}, bf16[16,256,128]{2,1,0:T(8,128)(2,1)S(1)}, bf16[16,256,128]{2,1,0:T(8,128)(2,1)S(1)}, bf16[16,256...) custom-call(s32[400]{0:T(512)S(1)} %get-tuple-element.34.entries, s32[2]{0:T(128)S(1)} %get-tuple-element.32.count, ...), custom_call_target="tpu_custom_call" | custom-call | tf_op jit(solution)/shard_map/send_products/pallas_call | solution.py:206
  38.1 3.1 %collective-permute-start.7 = (bf16[16,256,128]{2,1,0:T(8,128)(2,1)S(1)}, bf16[16,256,128]{2,1,0:T(8,128)(2,1)S(1)}, u32[]{:S(2)}, u32[]{:S(2)}) collective-permute-start(bf16[16,256,128]{2,1,0:T(8,128)(2,1)S(1)} %get-tuple-element.40), channel_id=1, source_target_pairs={{0,8},{8,16},{16,24},{24,0},{32,40},{40,48},{48,56},{56,32},{64,72... | collective-permute-start | bytes 3145736 | tf_op jit(solution)/shard_map/ppermute | solution.py:37
  41.3 2.7 %collective-permute-start.8 = (bf16[16,256,128]{2,1,0:T(8,128)(2,1)S(1)}, bf16[16,256,128]{2,1,0:T(8,128)(2,1)S(1)}, u32[]{:S(2)}, u32[]{:S(2)}) collective-permute-start(bf16[16,256,128]{2,1,0:T(8,128)(2,1)S(1)} %get-tuple-element.41), channel_id=1, source_target_pairs={{0,24},{8,0},{16,8},{24,16},{32,56},{40,32},{48,40},{56,48},{64,88... | collective-permute-start | bytes 3145736 | tf_op jit(solution)/shard_map/ppermute | solution.py:37
  44.0 2.7 %collective-permute-start.12 = (bf16[16,256,128]{2,1,0:T(8,128)(2,1)S(1)}, bf16[16,256,128]{2,1,0:T(8,128)(2,1)S(1)}, u32[]{:S(2)}, u32[]{:S(2)}) collective-permute-start(bf16[16,256,128]{2,1,0:T(8,128)(2,1)S(1)} %get-tuple-element.46), channel_id=1, source_target_pairs={{0,96},{8,104},{16,112},{24,120},{32,0},{40,8},{48,16},{56,24},{64... | collective-permute-start | bytes 3145736 | tf_op jit(solution)/shard_map/ppermute | solution.py:41
  46.7 3.4 %keep_products.1 = (bf16[16,256,128]{2,1,0:T(8,128)(2,1)S(1)}, bf16[8,256,128]{2,1,0:T(8,128)(2,1)S(1)}, bf16[8,256,128]{2,1,0:T(8,128)(2,1)S(1)}, bf16[16,256,1...) custom-call(s32[400]{0:T(512)S(1)} %get-tuple-element.31.entries, ...), custom_call_target="tpu_custom_call" | custom-call | tf_op jit(solution)/shard_map/keep_products/pallas_call | solution.py:219
  50.0 14.9 %collective-permute-done.7.refs_1_ = bf16[16,256,128]{2,1,0:T(8,128)(2,1)S(1)} collective-permute-done((bf16[16,256,128]{2,1,0:T(8,128)(2,1)S(1)}, bf16[16,256,128]{2,1,0:T(8,128)(2,1)S(1)}, u32[]{:S(2)}, u32[]{:S(2)}) %collective-permute-start.7) | collective-permute-done | bytes 1048608 | tf_op jit(solution)/shard_map/ppermute | solution.py:37
  69.8 3.2 %collective-permute-start.14 = (bf16[8,256,128]{2,1,0:T(8,128)(2,1)S(1)}, bf16[8,256,128]{2,1,0:T(8,128)(2,1)S(1)}, u32[]{:S(2)}, u32[]{:S(2)}) collective-permute-start(bf16[8,256,128]{2,1,0:T(8,128)(2,1)S(1)} %add_convert_fusion), channel_id=1, source_target_pairs={{0,96},{8,104},{16,112},{24,120},{32,0},{40,8},{48,16},{56,24},{64... | collective-permute-start | bytes 1572872 | tf_op jit(solution)/shard_map/ppermute | solution.py:41
  72.9 6.8 %collective-permute-done.9.refs_3_ = bf16[8,256,128]{2,1,0:T(8,128)(2,1)S(1)} collective-permute-done((bf16[8,256,128]{2,1,0:T(8,128)(2,1)S(1)}, bf16[8,256,128]{2,1,0:T(8,128)(2,1)S(1)}, u32[]{:S(2)}, u32[]{:S(2)}) %collective-permute-start.9) | collective-permute-done | bytes 524320 | tf_op jit(solution)/shard_map/ppermute | solution.py:37
  80.0 4.4 %collective-permute-done.13.refs_8_ = bf16[8,256,128]{2,1,0:T(8,128)(2,1)S(1)} collective-permute-done((bf16[8,256,128]{2,1,0:T(8,128)(2,1)S(1)}, bf16[8,256,128]{2,1,0:T(8,128)(2,1)S(1)}, u32[]{:S(2)}, u32[]{:S(2)}) %collective-permute-start.13) | collective-permute-done | bytes 524320 | tf_op jit(solution)/shard_map/ppermute | solution.py:41
  85.2 4.4 %collective-permute-start.16 = (bf16[4,256,128]{2,1,0:T(8,128)(2,1)S(1)}, bf16[4,256,128]{2,1,0:T(8,128)(2,1)S(1)}, u32[]{:S(2)}, u32[]{:S(2)}) collective-permute-start(bf16[4,256,128]{2,1,0:T(8,128)(2,1)S(1)} %get-tuple-element.51), channel_id=1, source_target_pairs={{0,64},{8,72},{16,80},{24,88},{32,96},{40,104},{48,112},{56,120},{... | collective-permute-start | bytes 786440 | tf_op jit(solution)/shard_map/ppermute | solution.py:41
  89.6 1.9 %collective-permute-start.19 = (bf16[4,256,128]{2,1,0:T(8,128)(2,1)S(1)}, bf16[4,256,128]{2,1,0:T(8,128)(2,1)S(1)}, u32[]{:S(2)}, u32[]{:S(2)}) collective-permute-start(bf16[4,256,128]{2,1,0:T(8,128)(2,1)S(1)} %get-tuple-element.55), channel_id=1, source_target_pairs={{0,16},{8,24},{16,0},{24,8},{32,48},{40,56},{48,32},{56,40},{64,80... | collective-permute-start | bytes 786440 | tf_op jit(solution)/shard_map/ppermute | solution.py:37
  91.5 2.8 %collective-permute-done.15.refs_1_ = bf16[4,256,128]{2,1,0:T(8,128)(2,1)S(1)} collective-permute-done((bf16[4,256,128]{2,1,0:T(8,128)(2,1)S(1)}, bf16[4,256,128]{2,1,0:T(8,128)(2,1)S(1)}, u32[]{:S(2)}, u32[]{:S(2)}) %collective-permute-start.15) | collective-permute-done | bytes 262176 | tf_op jit(solution)/shard_map/ppermute | solution.py:41
  94.8 6.0 %collective-permute-done.16.refs_2_ = bf16[4,256,128]{2,1,0:T(8,128)(2,1)S(1)} collective-permute-done((bf16[4,256,128]{2,1,0:T(8,128)(2,1)S(1)}, bf16[4,256,128]{2,1,0:T(8,128)(2,1)S(1)}, u32[]{:S(2)}, u32[]{:S(2)}) %collective-permute-start.16) | collective-permute-done | bytes 262176 | tf_op jit(solution)/shard_map/ppermute | solution.py:41
  105.1 2.3 %collective-permute-start.21 = (f32[128,256]{1,0:T(8,128)S(1)}, f32[128,256]{1,0:T(8,128)S(1)}, u32[]{:S(2)}, u32[]{:S(2)}) collective-permute-start(f32[128,256]{1,0:T(8,128)S(1)} %slice_select_fusion), channel_id=1, source_target_pairs={{0,1},{1,0},{2,3},{3,2},{4,5},{5,4},{6,7},{7,6},{8,9},{9,8},{10,11... | collective-permute-start | bytes 393224 | tf_op jit(solution)/shard_map/ppermute | solution.py:297
  108.5 3.4 %collective-permute-start.24 = (f32[32,256]{1,0:T(8,128)S(1)}, f32[32,256]{1,0:T(8,128)S(1)}, u32[]{:S(2)}, u32[]{:S(2)}) collective-permute-start(f32[32,256]{1,0:T(8,128)S(1)} %select_select_fusion.4), channel_id=1, source_target_pairs={{0,6},{1,7},{2,0},{3,1},{4,2},{5,3},{6,4},{7,5},{8,14},{9,15},{10,... | collective-permute-start | bytes 98312 | tf_op jit(solution)/shard_map/ppermute | solution.py:45
  112.9 3.5 %collective-permute-done.22 = f32[32,256]{1,0:T(8,128)S(1)} collective-permute-done((f32[32,256]{1,0:T(8,128)S(1)}, f32[32,256]{1,0:T(8,128)S(1)}, u32[]{:S(2)}, u32[]{:S(2)}) %collective-permute-start.22) | collective-permute-done | bytes 32800 | tf_op jit(solution)/shard_map/ppermute | solution.py:45
  119.3 2.3 %collective-permute-done.26 = f32[32,256]{1,0:T(8,128)S(1)} collective-permute-done((f32[32,256]{1,0:T(8,128)S(1)}, f32[32,256]{1,0:T(8,128)S(1)}, u32[]{:S(2)}, u32[]{:S(2)}) %collective-permute-start.26) | collective-permute-done | bytes 32800 | tf_op jit(solution)/shard_map/ppermute | solution.py:37
  123.8 2.1 %collective-permute-start.28 = (f32[32,256]{1,0:T(8,128)S(1)}, f32[32,256]{1,0:T(8,128)S(1)}, u32[]{:S(2)}, u32[]{:S(2)}) collective-permute-start(f32[32,256]{1,0:T(8,128)S(1)} %add_add_fusion.1), channel_id=1, source_target_pairs={{0,64},{8,72},{16,80},{24,88},{32,96},{40,104},{48,112},{56,120},{... | collective-permute-start | bytes 98312 | tf_op jit(solution)/shard_map/ppermute | solution.py:41
  128.1 2.0 %collective-permute-start.32 = (f32[32,256]{1,0:T(8,128)S(1)}, f32[32,256]{1,0:T(8,128)S(1)}, u32[]{:S(2)}, u32[]{:S(2)}) collective-permute-start(f32[32,256]{1,0:T(8,128)S(1)} %add_add_fusion), channel_id=1, source_target_pairs={{0,4},{1,5},{2,6},{3,7},{4,0},{5,1},{6,2},{7,3},{8,12},{9,13},{10,... | collective-permute-start | bytes 98312 | tf_op jit(solution)/shard_map/ppermute | solution.py:45
  133.1 6.7 %collective-permute-start.34 = (f32[128,256]{1,0:T(8,128)S(1)}, f32[128,256]{1,0:T(8,128)S(1)}, u32[]{:S(2)}, u32[]{:S(2)}) collective-permute-start(f32[128,256]{1,0:T(8,128)S(1)} %pad_maximum_fusion), channel_id=1, source_target_pairs={{0,1},{1,0},{2,3},{3,2},{4,5},{5,4},{6,7},{7,6},{8,9},{9,8},{10,11... | collective-permute-start | bytes 393224 | tf_op jit(solution)/shard_map/ppermute | solution.py:49
  (87 shorter events, 36.6 us)
Async XLA Ops:
  1.9 18.5 %collective-permute-start.2 = (bf16[8,256,128]{2,1,0:T(8,128)(2,1)S(1)}, bf16[8,256,128]{2,1,0:T(8,128)(2,1)S(1)}, u32[]{:S(2)}, u32[]{:S(2)}) collective-permute-start(bf16[8,256,128]{2,1,0:T(8,128)(2,1)S(1)} %panels.1.after.refs_0_), channel_id=1, source_target_pairs={{0,4},{1,5},{2,6},{3,7},{4,0},{5,1},{6,2},{7,3},{8,12},{9,13},{10,... | collective-permute-start | bytes 1572872 | tf_op jit(solution)/shard_map/ppermute | solution.py:45
  6.4 23.4 %collective-permute-start.1 = (bf16[8,256,128]{2,1,0:T(8,128)(2,1)S(1)}, bf16[8,256,128]{2,1,0:T(8,128)(2,1)S(1)}, u32[]{:S(2)}, u32[]{:S(2)}) collective-permute-start(bf16[8,256,128]{2,1,0:T(8,128)(2,1)S(1)} %panels.1.after.refs_0_), channel_id=1, source_target_pairs={{0,6},{1,7},{2,0},{3,1},{4,2},{5,3},{6,4},{7,5},{8,14},{9,15},{10,... | collective-permute-start | bytes 1572872 | tf_op jit(solution)/shard_map/ppermute | solution.py:45
  6.8 23.2 %collective-permute-start = (bf16[8,256,128]{2,1,0:T(8,128)(2,1)S(1)}, bf16[8,256,128]{2,1,0:T(8,128)(2,1)S(1)}, u32[]{:S(2)}, u32[]{:S(2)}) collective-permute-start(bf16[8,256,128]{2,1,0:T(8,128)(2,1)S(1)} %panels.1.after.refs_0_), channel_id=1, source_target_pairs={{0,2},{1,3},{2,4},{3,5},{4,6},{5,7},{6,0},{7,1},{8,10},{9,11},{10,... | collective-permute-start | bytes 1572872 | tf_op jit(solution)/shard_map/ppermute | solution.py:45
  7.9 24.1 %collective-permute-start.3 = (bf16[8,256,128]{2,1,0:T(8,128)(2,1)S(1)}, bf16[8,256,128]{2,1,0:T(8,128)(2,1)S(1)}, u32[]{:S(2)}, u32[]{:S(2)}) collective-permute-start(bf16[8,256,128]{2,1,0:T(8,128)(2,1)S(1)} %panels.1.after.refs_0_), channel_id=1, source_target_pairs={{0,1},{1,0},{2,3},{3,2},{4,5},{5,4},{6,7},{7,6},{8,9},{9,8},{10,11... | collective-permute-start | bytes 1572872 | tf_op jit(solution)/shard_map/ppermute | solution.py:49
  38.1 26.8 %collective-permute-start.7 = (bf16[16,256,128]{2,1,0:T(8,128)(2,1)S(1)}, bf16[16,256,128]{2,1,0:T(8,128)(2,1)S(1)}, u32[]{:S(2)}, u32[]{:S(2)}) collective-permute-start(bf16[16,256,128]{2,1,0:T(8,128)(2,1)S(1)} %get-tuple-element.40), channel_id=1, source_target_pairs={{0,8},{8,16},{16,24},{24,0},{32,40},{40,48},{48,56},{56,32},{64,72... | collective-permute-start | bytes 3145736 | tf_op jit(solution)/shard_map/ppermute | solution.py:37
  41.3 25.6 %collective-permute-start.8 = (bf16[16,256,128]{2,1,0:T(8,128)(2,1)S(1)}, bf16[16,256,128]{2,1,0:T(8,128)(2,1)S(1)}, u32[]{:S(2)}, u32[]{:S(2)}) collective-permute-start(bf16[16,256,128]{2,1,0:T(8,128)(2,1)S(1)} %get-tuple-element.41), channel_id=1, source_target_pairs={{0,24},{8,0},{16,8},{24,16},{32,56},{40,32},{48,40},{56,48},{64,88... | collective-permute-start | bytes 3145736 | tf_op jit(solution)/shard_map/ppermute | solution.py:37
  44.0 25.4 %collective-permute-start.11 = (bf16[16,256,128]{2,1,0:T(8,128)(2,1)S(1)}, bf16[16,256,128]{2,1,0:T(8,128)(2,1)S(1)}, u32[]{:S(2)}, u32[]{:S(2)}) collective-permute-start(bf16[16,256,128]{2,1,0:T(8,128)(2,1)S(1)} %get-tuple-element.45), channel_id=1, source_target_pairs={{0,32},{8,40},{16,48},{24,56},{32,64},{40,72},{48,80},{56,88},{64,... | collective-permute-start | bytes 3145736 | tf_op jit(solution)/shard_map/ppermute | solution.py:41
  44.0 25.6 %collective-permute-start.12 = (bf16[16,256,128]{2,1,0:T(8,128)(2,1)S(1)}, bf16[16,256,128]{2,1,0:T(8,128)(2,1)S(1)}, u32[]{:S(2)}, u32[]{:S(2)}) collective-permute-start(bf16[16,256,128]{2,1,0:T(8,128)(2,1)S(1)} %get-tuple-element.46), channel_id=1, source_target_pairs={{0,96},{8,104},{16,112},{24,120},{32,0},{40,8},{48,16},{56,24},{64... | collective-permute-start | bytes 3145736 | tf_op jit(solution)/shard_map/ppermute | solution.py:41
  65.1 14.7 %collective-permute-start.9 = (bf16[8,256,128]{2,1,0:T(8,128)(2,1)S(1)}, bf16[8,256,128]{2,1,0:T(8,128)(2,1)S(1)}, u32[]{:S(2)}, u32[]{:S(2)}) collective-permute-start(bf16[8,256,128]{2,1,0:T(8,128)(2,1)S(1)} %add_convert_fusion.3), channel_id=1, source_target_pairs={{0,8},{8,16},{16,24},{24,0},{32,40},{40,48},{48,56},{56,32},{64,72... | collective-permute-start | bytes 1572872 | tf_op jit(solution)/shard_map/ppermute | solution.py:37
  67.0 13.1 %collective-permute-start.10 = (bf16[8,256,128]{2,1,0:T(8,128)(2,1)S(1)}, bf16[8,256,128]{2,1,0:T(8,128)(2,1)S(1)}, u32[]{:S(2)}, u32[]{:S(2)}) collective-permute-start(bf16[8,256,128]{2,1,0:T(8,128)(2,1)S(1)} %add_convert_fusion.2), channel_id=1, source_target_pairs={{0,24},{8,0},{16,8},{24,16},{32,56},{40,32},{48,40},{56,48},{64,88... | collective-permute-start | bytes 1572872 | tf_op jit(solution)/shard_map/ppermute | solution.py:37
  69.5 14.9 %collective-permute-start.13 = (bf16[8,256,128]{2,1,0:T(8,128)(2,1)S(1)}, bf16[8,256,128]{2,1,0:T(8,128)(2,1)S(1)}, u32[]{:S(2)}, u32[]{:S(2)}) collective-permute-start(bf16[8,256,128]{2,1,0:T(8,128)(2,1)S(1)} %add_convert_fusion.1), channel_id=1, source_target_pairs={{0,32},{8,40},{16,48},{24,56},{32,64},{40,72},{48,80},{56,88},{64,... | collective-permute-start | bytes 1572872 | tf_op jit(solution)/shard_map/ppermute | solution.py:41
  69.8 14.6 %collective-permute-start.14 = (bf16[8,256,128]{2,1,0:T(8,128)(2,1)S(1)}, bf16[8,256,128]{2,1,0:T(8,128)(2,1)S(1)}, u32[]{:S(2)}, u32[]{:S(2)}) collective-permute-start(bf16[8,256,128]{2,1,0:T(8,128)(2,1)S(1)} %add_convert_fusion), channel_id=1, source_target_pairs={{0,96},{8,104},{16,112},{24,120},{32,0},{40,8},{48,16},{56,24},{64... | collective-permute-start | bytes 1572872 | tf_op jit(solution)/shard_map/ppermute | solution.py:41
  85.1 9.2 %collective-permute-start.15 = (bf16[4,256,128]{2,1,0:T(8,128)(2,1)S(1)}, bf16[4,256,128]{2,1,0:T(8,128)(2,1)S(1)}, u32[]{:S(2)}, u32[]{:S(2)}) collective-permute-start(bf16[4,256,128]{2,1,0:T(8,128)(2,1)S(1)} %get-tuple-element.50), channel_id=1, source_target_pairs={{0,32},{8,40},{16,48},{24,56},{32,64},{40,72},{48,80},{56,88},{64,... | collective-permute-start | bytes 786440 | tf_op jit(solution)/shard_map/ppermute | solution.py:41
  85.2 15.6 %collective-permute-start.16 = (bf16[4,256,128]{2,1,0:T(8,128)(2,1)S(1)}, bf16[4,256,128]{2,1,0:T(8,128)(2,1)S(1)}, u32[]{:S(2)}, u32[]{:S(2)}) collective-permute-start(bf16[4,256,128]{2,1,0:T(8,128)(2,1)S(1)} %get-tuple-element.51), channel_id=1, source_target_pairs={{0,64},{8,72},{16,80},{24,88},{32,96},{40,104},{48,112},{56,120},{... | collective-permute-start | bytes 786440 | tf_op jit(solution)/shard_map/ppermute | solution.py:41
  89.6 11.1 %collective-permute-start.17 = (bf16[4,256,128]{2,1,0:T(8,128)(2,1)S(1)}, bf16[4,256,128]{2,1,0:T(8,128)(2,1)S(1)}, u32[]{:S(2)}, u32[]{:S(2)}) collective-permute-start(bf16[4,256,128]{2,1,0:T(8,128)(2,1)S(1)} %get-tuple-element.52), channel_id=1, source_target_pairs={{0,96},{8,104},{16,112},{24,120},{32,0},{40,8},{48,16},{56,24},{64... | collective-permute-start | bytes 786440 | tf_op jit(solution)/shard_map/ppermute | solution.py:41
  89.6 11.1 %collective-permute-start.18 = (bf16[4,256,128]{2,1,0:T(8,128)(2,1)S(1)}, bf16[4,256,128]{2,1,0:T(8,128)(2,1)S(1)}, u32[]{:S(2)}, u32[]{:S(2)}) collective-permute-start(bf16[4,256,128]{2,1,0:T(8,128)(2,1)S(1)} %get-tuple-element.54), channel_id=1, source_target_pairs={{0,8},{8,16},{16,24},{24,0},{32,40},{40,48},{48,56},{56,32},{64,72... | collective-permute-start | bytes 786440 | tf_op jit(solution)/shard_map/ppermute | solution.py:37
  89.6 12.1 %collective-permute-start.19 = (bf16[4,256,128]{2,1,0:T(8,128)(2,1)S(1)}, bf16[4,256,128]{2,1,0:T(8,128)(2,1)S(1)}, u32[]{:S(2)}, u32[]{:S(2)}) collective-permute-start(bf16[4,256,128]{2,1,0:T(8,128)(2,1)S(1)} %get-tuple-element.55), channel_id=1, source_target_pairs={{0,16},{8,24},{16,0},{24,8},{32,48},{40,56},{48,32},{56,40},{64,80... | collective-permute-start | bytes 786440 | tf_op jit(solution)/shard_map/ppermute | solution.py:37
  94.3 9.2 %collective-permute-start.20 = (bf16[4,256,128]{2,1,0:T(8,128)(2,1)S(1)}, bf16[4,256,128]{2,1,0:T(8,128)(2,1)S(1)}, u32[]{:S(2)}, u32[]{:S(2)}) collective-permute-start(bf16[4,256,128]{2,1,0:T(8,128)(2,1)S(1)} %get-tuple-element.56), channel_id=1, source_target_pairs={{0,24},{8,0},{16,8},{24,16},{32,56},{40,32},{48,40},{56,48},{64,88... | collective-permute-start | bytes 786440 | tf_op jit(solution)/shard_map/ppermute | solution.py:37
  108.5 4.4 %collective-permute-start.24 = (f32[32,256]{1,0:T(8,128)S(1)}, f32[32,256]{1,0:T(8,128)S(1)}, u32[]{:S(2)}, u32[]{:S(2)}) collective-permute-start(f32[32,256]{1,0:T(8,128)S(1)} %select_select_fusion.4), channel_id=1, source_target_pairs={{0,6},{1,7},{2,0},{3,1},{4,2},{5,3},{6,4},{7,5},{8,14},{9,15},{10,... | collective-permute-start | bytes 98312 | tf_op jit(solution)/shard_map/ppermute | solution.py:45
  111.9 4.5 %collective-permute-start.22 = (f32[32,256]{1,0:T(8,128)S(1)}, f32[32,256]{1,0:T(8,128)S(1)}, u32[]{:S(2)}, u32[]{:S(2)}) collective-permute-start(f32[32,256]{1,0:T(8,128)S(1)} %get-tuple-element.93), channel_id=1, source_target_pairs={{0,4},{1,5},{2,6},{3,7},{4,0},{5,1},{6,2},{7,3},{8,12},{9,13},{10,... | collective-permute-start | bytes 98312 | tf_op jit(solution)/shard_map/ppermute | solution.py:45
  112.0 4.4 %collective-permute-start.23 = (f32[32,256]{1,0:T(8,128)S(1)}, f32[32,256]{1,0:T(8,128)S(1)}, u32[]{:S(2)}, u32[]{:S(2)}) collective-permute-start(f32[32,256]{1,0:T(8,128)S(1)} %get-tuple-element.94), channel_id=1, source_target_pairs={{0,2},{1,3},{2,4},{3,5},{4,6},{5,7},{6,0},{7,1},{8,10},{9,11},{10,... | collective-permute-start | bytes 98312 | tf_op jit(solution)/shard_map/ppermute | solution.py:45
  118.0 4.3 %collective-permute-start.25 = (f32[32,256]{1,0:T(8,128)S(1)}, f32[32,256]{1,0:T(8,128)S(1)}, u32[]{:S(2)}, u32[]{:S(2)}) collective-permute-start(f32[32,256]{1,0:T(8,128)S(1)} %add_add_fusion.2), channel_id=1, source_target_pairs={{0,16},{8,24},{16,0},{24,8},{32,48},{40,56},{48,32},{56,40},{64,80... | collective-permute-start | bytes 98312 | tf_op jit(solution)/shard_map/ppermute | solution.py:37
  128.1 4.6 %collective-permute-start.32 = (f32[32,256]{1,0:T(8,128)S(1)}, f32[32,256]{1,0:T(8,128)S(1)}, u32[]{:S(2)}, u32[]{:S(2)}) collective-permute-start(f32[32,256]{1,0:T(8,128)S(1)} %add_add_fusion), channel_id=1, source_target_pairs={{0,4},{1,5},{2,6},{3,7},{4,0},{5,1},{6,2},{7,3},{8,12},{9,13},{10,... | collective-permute-start | bytes 98312 | tf_op jit(solution)/shard_map/ppermute | solution.py:45
  133.1 7.7 %collective-permute-start.34 = (f32[128,256]{1,0:T(8,128)S(1)}, f32[128,256]{1,0:T(8,128)S(1)}, u32[]{:S(2)}, u32[]{:S(2)}) collective-permute-start(f32[128,256]{1,0:T(8,128)S(1)} %pad_maximum_fusion), channel_id=1, source_target_pairs={{0,1},{1,0},{2,3},{3,2},{4,5},{5,4},{6,7},{7,6},{8,9},{9,8},{10,11... | collective-permute-start | bytes 393224 | tf_op jit(solution)/shard_map/ppermute | solution.py:49
  (18 other events, 158.6 us)

commit v3 on v2

--- a/solution.py
+++ b/solution.py
@@ -11,8 +11,7 @@
 B = 128
 NY = NX = NZ = 4
 HALF = 64
-UNROLL = 16
-FW = 256
+UNROLL = 32
 KT = 384
 VMEM = pl.BlockSpec(memory_space=pltpu.VMEM)
 SMEM = pl.BlockSpec(memory_space=pltpu.SMEM)
@@ -49,17 +48,24 @@
     return lax.ppermute(v, "col", CP)
 
 
-def panels_kernel(x_ref, out_ref):
+def transposed(x_ref, out_ref):
     for b in range(8):
         out_ref[b] = x_ref[b * B : (b + 1) * B, :].astype(F32).T.astype(BF16)
 
 
-def panels(out_grad):
-    return pl.pallas_call(
-        panels_kernel,
-        out_shape=shaped((8, FW, B)),
-        compiler_params=params(6),
-        name="panels",
+def low_kernel(x_ref, out_ref):
+    transposed(x_ref, out_ref)
+
+
+def low_panels(out_grad):
+    return pl.pallas_call(
+        low_kernel,
+        grid=(1,),
+        in_specs=[pl.BlockSpec((8 * B, B), lambda i: (0, 0))],
+        out_specs=pl.BlockSpec((8, B, B), lambda i: (0, 0, 0)),
+        out_shape=shaped((8, B, B)),
+        compiler_params=params(4),
+        name="low_panels",
     )(out_grad)
 
 
@@ -94,6 +100,22 @@
     )(at, row_block, col_block, live, after)
 
 
+def high_kernel(x_ref, *refs):
+    transposed(x_ref, refs[-1])
+
+
+def high_panels(out_grad, after):
+    return pl.pallas_call(
+        high_kernel,
+        grid=(1,),
+        in_specs=[pl.BlockSpec((8 * B, B), lambda i: (0, 1))] + [ANY] * len(after),
+        out_specs=pl.BlockSpec((8, B, B), lambda i: (0, 0, 0)),
+        out_shape=shaped((8, B, B)),
+        compiler_params=params(4),
+        name="high_panels",
+    )(out_grad, *after)
+
+
 def again_kernel(a, b, c, *refs):
     for source, target in zip((a, b, c), refs[-3:]):
         target[...] = source[...]
@@ -102,18 +124,18 @@
 def again(arrays, after):
     return pl.pallas_call(
         again_kernel,
-        in_specs=[VMEM] * 3 + [ANY] * len(after),
+        in_specs=[VMEM] * 3 + [ANY],
         out_shape=[shaped(a.shape) for a in arrays],
         compiler_params=params(6),
         name="again",
-    )(*arrays, *after)
+    )(*arrays, after)
 
 
 def stage_kernel(tiles, code, place, after, held, first, second, count, masks, sem):
     copy = pltpu.make_async_copy(tiles, held, sem)
     copy.start()
     for i in range(2):
-        masks[i] = jnp.full((8, 256), place[i], jnp.int32)
+        masks[i] = jnp.full((8, 256), place[2 + i], jnp.int32)
 
     def step(g, counts):
         a, b = counts
@@ -199,7 +221,7 @@
     write_out(acc, outs)
 
 
-ACC = pltpu.VMEM((HALF + 1, FW, B), F32)
+ACC = pltpu.VMEM((HALF + 1, B, B), F32)
 
 
 def send_products(entries, count, tiles, xs):
@@ -207,7 +229,7 @@
         send_kernel,
         in_specs=[SMEM, SMEM, VMEM] + [VMEM] * 8,
         out_specs=[VMEM] * 5,
-        out_shape=[shaped((n, FW, B)) for n in (64,) + SEND],
+        out_shape=[shaped((n, B, B)) for n in (64,) + SEND],
         scratch_shapes=[ACC],
         compiler_params=params(12),
         name="send_products",
@@ -220,15 +242,41 @@
         keep_kernel,
         in_specs=[SMEM, SMEM, VMEM, VMEM],
         out_specs=[VMEM] * 6,
-        out_shape=[shaped((n, FW, B)) for n in KEEP],
+        out_shape=[shaped((n, B, B)) for n in KEEP],
         scratch_shapes=[ACC],
         compiler_params=params(12),
         name="keep_products",
     )(entries, count, tiles, x)
 
 
+def join_kernel(*refs):
+    ins, outs = refs[:12], refs[12:]
+    for i in range(4):
+        kept, got, sent = ins[i * 3 : i * 3 + 3]
+        outs[i][:8] = (kept[...].astype(F32) + got[:8].astype(F32)).astype(BF16)
+        outs[i][8:] = sent[...]
+
+
+def join(keep, received, send):
+    ins = []
+    for kept, got, sent in zip(keep, received, send):
+        ins += [kept, got, sent]
+    return pl.pallas_call(
+        join_kernel,
+        out_shape=[shaped((24, B, B))] * 4,
+        compiler_params=params(12),
+        name="join",
+    )(*ins)
+
+
 def middle_kernel(*refs):
-    received, outs = refs[:10], refs[10:]
+    received = refs[:10]
+    last = len(refs) > 18
+    before, outs = (refs[10:18], refs[18:]) if last else ((), refs[10:])
+    at, skip = (4, 8) if last else (0, 0)
+    if last:
+        for i in range(8):
+            outs[i][:4] = before[i][...]
     for half in range(2):
         own, rp, rm, sp, sm = received[half * 5 : half * 5 + 5]
         for place in range(4):
@@ -236,45 +284,67 @@
             for i in range(4):
                 n = place * 4 + i
                 if place < 2:
-                    s = own[n].astype(F32) + rm[8 + n].astype(F32) + sp[n].astype(F32)
+                    s = own[n].astype(F32) + rm[skip + 8 + n].astype(F32) + sp[n].astype(F32)
                 else:
-                    s = own[n].astype(F32) + rp[n].astype(F32) + sm[n - 8].astype(F32)
-                out[i] = s.astype(out.dtype)
-
-
-def middle(received):
+                    s = own[n].astype(F32) + rp[skip + n].astype(F32) + sm[n - 8].astype(F32)
+                out[at + i] = s.astype(out.dtype)
+
+
+def middle(received, before):
+    n = 8 if before else 4
     dtypes = (F32, BF16, BF16, BF16) * 2
     return pl.pallas_call(
         middle_kernel,
-        out_shape=[shaped((4, FW, B), t) for t in dtypes],
+        out_shape=[shaped((n, B, B), t) for t in dtypes],
         compiler_params=params(14),
         name="middle",
-    )(*received)
-
-
-def finish_kernel(*refs):
-    parts, (feat, weight, ig, wg) = refs[:8], refs[8:]
-    total = jnp.zeros((FW, 256), F32)
+    )(*received, *before)
+
+
+def column_grad(parts, b):
+    four = parts[b // 4 * 4 : b // 4 * 4 + 4]
+    halves = []
+    for h in range(2):
+        i = h * 4 + b % 4
+        s = four[0][i] + four[1][i].astype(F32)
+        halves.append(s + four[2][i].astype(F32) + four[3][i].astype(F32))
+    return jnp.concatenate(halves, axis=0).astype(BF16)
+
+
+def weight_kernel(*refs):
+    parts, (feat, wg) = refs[:8], refs[8:]
+    total = jnp.zeros((256, 256), F32)
     for b in range(8):
-        four = parts[b // 4 * 4 : b // 4 * 4 + 4]
-        i = b % 4
-        rows = slice(b * B, (b + 1) * B)
-        s = four[0][i] + four[1][i].astype(F32)
-        cg = (s + four[2][i].astype(F32) + four[3][i].astype(F32)).astype(BF16)
-        total = total + jnp.dot(cg, feat[rows, :], preferred_element_type=F32)
-        ig[rows, :] = lax.dot_general(
-            cg, weight[...], (((0,), (1,)), ((), ())), preferred_element_type=F32
+        total = total + jnp.dot(
+            column_grad(parts, b), feat[b * B : (b + 1) * B, :], preferred_element_type=F32
+        )
+    wg[...] = total.T
+
+
+def input_kernel(*refs):
+    parts, (weight, ig) = refs[:8], refs[8:]
+    for b in range(8):
+        ig[b * B : (b + 1) * B, :] = lax.dot_general(
+            column_grad(parts, b), weight[...], (((0,), (1,)), ((), ())), preferred_element_type=F32
         ).astype(BF16)
-    wg[...] = total
-
-
-def finish(parts, features, weight):
-    return pl.pallas_call(
-        finish_kernel,
-        out_shape=[shaped((8 * B, 256)), shaped((FW, 256), F32)],
+
+
+def weight_share(parts, features):
+    return pl.pallas_call(
+        weight_kernel,
+        out_shape=shaped((256, 256), F32),
         compiler_params=params(10),
-        name="finish",
-    )(*parts, features, weight)
+        name="weight_share",
+    )(*parts, features)
+
+
+def input_share(parts, weight):
+    return pl.pallas_call(
+        input_kernel,
+        out_shape=shaped((8 * B, 256)),
+        compiler_params=params(10),
+        name="input_share",
+    )(*parts, weight)
 
 
 def f32(v):
@@ -318,33 +388,45 @@
 def local(out_grad, features, weight, tiles, row_block, col_block, live):
     row, col = lax.axis_index("row"), lax.axis_index("col")
     y, x, z, core = row // NX, row % NX, col // 2, col % 2
-    own = panels(out_grad)
-    own_turned = cperm(own)
-    one, three, two = zperm(own, 1), zperm(own, 3), zperm(own, 2)
+    low = low_panels(out_grad)
+    one, three, two = zperm(low, 1), zperm(low, 3), zperm(low, 2)
     at = jnp.stack([y, x, z, core]).astype(jnp.int32)
-    place = jnp.stack([core, z]).astype(jnp.int32)
-    code = codes(at, row_block, col_block, live, own)
-    held, first, second, count, masks = stage(tiles[0, 0], code, place, own)
-    one, three, two = again((one, three, two), [held])
-    xs = [own, three, two, one, own_turned, cperm(three), cperm(two), cperm(one)]
+    place = jnp.stack([y, x, core, z]).astype(jnp.int32)
+    code = codes(at, row_block, col_block, live, low)
+    held, first, second, count, masks = stage(tiles[0, 0], code, place, low)
+    low_turned = cperm(low)
+    three, two, one = again((three, two, one), held)
+    low_all = [low, three, two, one, low_turned, cperm(three), cperm(two), cperm(one)]
+    high = high_panels(out_grad, [three])
+    one, three = zperm(high, 1), zperm(high, 3)
 
     ways = ((xperm, 1), (xperm, 3), (yperm, 1), (yperm, 3))
 
     def swap(buffers):
         return [perm(v, s) for v, (perm, s) in zip(buffers, ways)]
 
-    stacked, send = send_products(first, count, held, xs)
+    x_low, send = send_products(first, count, held, low_all)
+    high, three, one = again((high, three, one), x_low)
+    two = zperm(high, 2)
     got = swap(send)
-    keep = keep_products(second, count, held, stacked)
-    turned = [keep[1], keep[2], keep[4], keep[5]]
-    more = swap([(f32(v) + f32(g[:8])).astype(BF16) for v, g in zip(turned, got)])
-    received = [keep[0], *got[:2], *more[:2], keep[3], *got[2:], *more[2:]]
-    sums = middle(received)
+    keep = keep_products(second, count, held, x_low)
+    high_all = [high, three, two, one, cperm(high), cperm(three), cperm(two), cperm(one)]
+    x_high, send_high = send_products(first, count, held, high_all)
+    got_both = swap(join([keep[1], keep[2], keep[4], keep[5]], got, send_high))
+    keep_high = keep_products(second, count, held, x_high)
+    turned = [keep_high[1], keep_high[2], keep_high[4], keep_high[5]]
+    got_high = swap([(f32(v) + f32(g[8:16])).astype(BF16) for v, g in zip(turned, got_both)])
+
+    def ordered(keep, ones, twos):
+        return [keep[0], *ones[:2], *twos[:2], keep[3], *ones[2:], *twos[2:]]
+
+    before = middle(ordered(keep, got, got_both), [])
+    sums = middle(ordered(keep_high, got_both, got_high), before)
     parts = [sums[0]] + [yperm(sums[k], k) for k in (1, 2, 3)]
     parts += [sums[4]] + [xperm(sums[4 + k], k) for k in (1, 2, 3)]
-    input_grad, wg = finish(parts, features, weight)
+    input_grad, wg = input_share(parts, weight), weight_share(parts, features)
     nodes = 1024 * 128
-    return input_grad, all_sum(wg, masks).T * nodes ** (-0.5)
+    return input_grad, all_sum(wg, masks) * nodes ** (-0.5)
 
 
 def solution(mesh):

time: 142 us -> 140 us (0.986)
  waiting for transfers between devices: 64 us -> 46.4 us
  starting transfers between devices: 53.5 us -> 69.4 us
    ppermute x10 -> x12, waiting for transfers between devices: 28.2 us -> 20.1 us  [xperm(): return lax.ppermute(v, 'row', XP[s])]
    ppermute x10 -> x12, starting transfers between devices: 13.5 us -> 19.1 us  [xperm(): return lax.ppermute(v, 'row', XP[s])]
    ppermute x9 -> x12, starting transfers between devices: 13.5 us -> 18.3 us  [zperm(): return lax.ppermute(v, 'col', ZP[s])]
    ppermute x5 -> x9, waiting for transfers between devices: 3.51 us -> 0.02 us  [cperm(): return lax.ppermute(v, 'col', CP)]
    ppermute x10 -> x12, waiting for transfers between devices: 16.4 us -> 13.2 us  [yperm(): return lax.ppermute(v, 'row', YP[s])]
    ppermute x9 -> x12, waiting for transfers between devices: 14.9 us -> 12.1 us  [zperm(): return lax.ppermute(v, 'col', ZP[s])]
    ppermute x10 -> x12, starting transfers between devices: 14.1 us -> 16.4 us  [yperm(): return lax.ppermute(v, 'row', YP[s])]
    ppermute x1, starting transfers between devices: 2.34 us -> 4.29 us  [all_sum(): v = mine + lax.ppermute(other, 'col', CP)]
  transfers between devices with their start and end apart: 35 -> 46, of which waited for: 26 -> 21; matrix products, arithmetic and copies ran while one was open for 1% -> 0% of each run, Pallas kernels for 5% -> 9%
where the time goes in v3:
time: 140 us
  starting transfers between devices  69.4 us (50%)
  waiting for transfers between devices  46.4 us (33%)
  Pallas kernels  14.3 us (10%)
  local copies, waits for them, and re-layouts  7.66 us (5%)
    ppermute x12, waiting for transfers between devices, xperm(): return lax.ppermute(v, 'row', XP[s])  20.1 us
    ppermute x12, starting transfers between devices, xperm(): return lax.ppermute(v, 'row', XP[s])  19.1 us
    ppermute x12, starting transfers between devices, zperm(): return lax.ppermute(v, 'col', ZP[s])  18.3 us
    ppermute x12, starting transfers between devices, yperm(): return lax.ppermute(v, 'row', YP[s])  16.4 us
    ppermute x12, waiting for transfers between devices, yperm(): return lax.ppermute(v, 'row', YP[s])  13.2 us
    ppermute x12, waiting for transfers between devices, zperm(): return lax.ppermute(v, 'col', ZP[s])  12.1 us
    ppermute x9, starting transfers between devices, cperm(): return lax.ppermute(v, 'col', CP)  11.3 us
    unnamed x16, local copies, waits for them, and re-layouts  7.66 us
  transfers between devices with their start and end apart: 46, of which 21 were waited for; matrix products, arithmetic and copies ran while one was open for 0% of the time, Pallas kernels for 9%

profile of v3, /device:TPU:1, one launch (start us, length us, event | category | flops | bytes accessed | tf_op | source)
XLA Modules:
  0.0 140.1 jit_solution(17463548730480159027)
XLA Ops:
  1.8 2.5 %collective-permute-start.2 = (bf16[8,128,128]{2,1,0:T(8,128)(2,1)S(1)}, bf16[8,128,128]{2,1,0:T(8,128)(2,1)S(1)}, u32[]{:S(2)}, u32[]{:S(2)}) collective-permute-start(bf16[8,128,128]{2,1,0:T(8,128)(2,1)S(1)} %low_panels.1.after.refs_0_), channel_id=1, source_target_pairs={{0,2},{1,3},{2,4},{3,5},{4,6},{5,7},{6,0},{7,1},{8,10},{9,11},{10,... | collective-permute-start | bytes 786440 | tf_op jit(solution)/shard_map/ppermute | solution.py:44
  4.4 3.3 %collective-permute-start.1 = (bf16[8,128,128]{2,1,0:T(8,128)(2,1)S(1)}, bf16[8,128,128]{2,1,0:T(8,128)(2,1)S(1)}, u32[]{:S(2)}, u32[]{:S(2)}) collective-permute-start(bf16[8,128,128]{2,1,0:T(8,128)(2,1)S(1)} %low_panels.1.after.refs_0_), channel_id=1, source_target_pairs={{0,4},{1,5},{2,6},{3,7},{4,0},{5,1},{6,2},{7,3},{8,12},{9,13},{10,... | collective-permute-start | bytes 786440 | tf_op jit(solution)/shard_map/ppermute | solution.py:44
  12.6 4.6 %copy-done = bf16[1,1,384,128,128]{4,3,2,1,0:T(8,128)(2,1)S(1)} copy-done((bf16[1,1,384,128,128]{4,3,2,1,0:T(8,128)(2,1)S(1)}, bf16[1,1,384,128,128]{4,3,2,1,0:T(8,128)(2,1)}, u32[]{:S(2)}) %copy-start) | copy-done | bytes 12582936
  17.2 3.7 %stage.1 = (bf16[384,128,128]{2,1,0:T(8,128)(2,1)S(1)}, s32[416]{0:T(512)S(1)}, s32[416]{0:T(512)S(1)}, s32[2]{0:T(128)S(1)}, s32[2,8,256]{2,1,0:T(8,128)S(1)}) custom-call(bf16[384,128,128]{2,1,0:T(8,128)(2,1)S(1)} %bitcast.5, s32[1,1,384]{2,1,0:T(1,128)S(1)} %codes.1.code, s32[4]{0:T(128)S(1)} %get-tuple-element.148.place, ...), custom_call_target="tpu_custom_call" | custom-call | tf_op jit(solution)/shard_map/stage/pallas_call | solution.py:162
  26.3 4.3 %collective-permute-done.4.c = bf16[8,128,128]{2,1,0:T(8,128)(2,1)S(1)} collective-permute-done((bf16[8,128,128]{2,1,0:T(8,128)(2,1)S(1)}, bf16[8,128,128]{2,1,0:T(8,128)(2,1)S(1)}, u32[]{:S(2)}, u32[]{:S(2)}) %collective-permute-start.4) | collective-permute-done | bytes 262176 | tf_op jit(solution)/shard_map/ppermute | solution.py:44
  39.4 2.5 %collective-permute-done.9.refs_2_ = bf16[8,128,128]{2,1,0:T(8,128)(2,1)S(1)} collective-permute-done((bf16[8,128,128]{2,1,0:T(8,128)(2,1)S(1)}, bf16[8,128,128]{2,1,0:T(8,128)(2,1)S(1)}, u32[]{:S(2)}, u32[]{:S(2)}) %collective-permute-start.9) | collective-permute-done | bytes 262176 | tf_op jit(solution)/shard_map/ppermute | solution.py:44
  46.0 2.2 %collective-permute-done.14.refs_1_ = bf16[16,128,128]{2,1,0:T(8,128)(2,1)S(1)} collective-permute-done((bf16[16,128,128]{2,1,0:T(8,128)(2,1)S(1)}, bf16[16,128,128]{2,1,0:T(8,128)(2,1)S(1)}, u32[]{:S(2)}, u32[]{:S(2)}) %collective-permute-start.14) | collective-permute-done | bytes 524320 | tf_op jit(solution)/shard_map/ppermute | solution.py:36
  48.2 2.2 %collective-permute-done.16.refs_7_.refs_6_ = bf16[16,128,128]{2,1,0:T(8,128)(2,1)S(1)} collective-permute-done((bf16[16,128,128]{2,1,0:T(8,128)(2,1)S(1)}, bf16[16,128,128]{2,1,0:T(8,128)(2,1)S(1)}, u32[]{:S(2)}, u32[]{:S(2)}) %collective-permute-start.16) | collective-permute-done | bytes 524320 | tf_op jit(solution)/shard_map/ppermute | solution.py:40
  50.8 2.7 %collective-permute-start.19 = (bf16[24,128,128]{2,1,0:T(8,128)(2,1)S(1)}, bf16[24,128,128]{2,1,0:T(8,128)(2,1)S(1)}, u32[]{:S(2)}, u32[]{:S(2)}) collective-permute-start(bf16[24,128,128]{2,1,0:T(8,128)(2,1)S(1)} %get-tuple-element.81), channel_id=1, source_target_pairs={{0,24},{8,0},{16,8},{24,16},{32,56},{40,32},{48,40},{56,48},{64,88... | collective-permute-start | bytes 2359304 | tf_op jit(solution)/shard_map/ppermute | solution.py:36
  58.9 10.3 %collective-permute-done.18.refs_3_.refs_1_ = bf16[24,128,128]{2,1,0:T(8,128)(2,1)S(1)} collective-permute-done((bf16[24,128,128]{2,1,0:T(8,128)(2,1)S(1)}, bf16[24,128,128]{2,1,0:T(8,128)(2,1)S(1)}, u32[]{:S(2)}, u32[]{:S(2)}) %collective-permute-start.18) | collective-permute-done | bytes 786464 | tf_op jit(solution)/shard_map/ppermute | solution.py:36
  69.5 2.7 %collective-permute-start.21 = (bf16[8,128,128]{2,1,0:T(8,128)(2,1)S(1)}, bf16[8,128,128]{2,1,0:T(8,128)(2,1)S(1)}, u32[]{:S(2)}, u32[]{:S(2)}) collective-permute-start(bf16[8,128,128]{2,1,0:T(8,128)(2,1)S(1)} %add_convert_fusion.2), channel_id=1, source_target_pairs={{0,24},{8,0},{16,8},{24,16},{32,56},{40,32},{48,40},{56,48},{64,88... | collective-permute-start | bytes 786440 | tf_op jit(solution)/shard_map/ppermute | solution.py:36
  74.9 2.3 %collective-permute-start.25 = (bf16[8,128,128]{2,1,0:T(8,128)(2,1)S(1)}, bf16[8,128,128]{2,1,0:T(8,128)(2,1)S(1)}, u32[]{:S(2)}, u32[]{:S(2)}) collective-permute-start(bf16[8,128,128]{2,1,0:T(8,128)(2,1)S(1)} %add_convert_fusion), channel_id=1, source_target_pairs={{0,96},{8,104},{16,112},{24,120},{32,0},{40,8},{48,16},{56,24},{64... | collective-permute-start | bytes 786440 | tf_op jit(solution)/shard_map/ppermute | solution.py:40
  77.6 3.8 %collective-permute-done.24.refs_8_ = bf16[8,128,128]{2,1,0:T(8,128)(2,1)S(1)} collective-permute-done((bf16[8,128,128]{2,1,0:T(8,128)(2,1)S(1)}, bf16[8,128,128]{2,1,0:T(8,128)(2,1)S(1)}, u32[]{:S(2)}, u32[]{:S(2)}) %collective-permute-start.24) | collective-permute-done | bytes 262176 | tf_op jit(solution)/shard_map/ppermute | solution.py:40
  82.7 3.1 %collective-permute-start.27 = (bf16[8,128,128]{2,1,0:T(8,128)(2,1)S(1)}, bf16[8,128,128]{2,1,0:T(8,128)(2,1)S(1)}, u32[]{:S(2)}, u32[]{:S(2)}) collective-permute-start(bf16[8,128,128]{2,1,0:T(8,128)(2,1)S(1)} %get-tuple-element.101), channel_id=1, source_target_pairs={{0,64},{8,72},{16,80},{24,88},{32,96},{40,104},{48,112},{56,120},{... | collective-permute-start | bytes 786440 | tf_op jit(solution)/shard_map/ppermute | solution.py:40
  86.5 3.7 %collective-permute-start.30 = (bf16[8,128,128]{2,1,0:T(8,128)(2,1)S(1)}, bf16[8,128,128]{2,1,0:T(8,128)(2,1)S(1)}, u32[]{:S(2)}, u32[]{:S(2)}) collective-permute-start(bf16[8,128,128]{2,1,0:T(8,128)(2,1)S(1)} %get-tuple-element.105), channel_id=1, source_target_pairs={{0,16},{8,24},{16,0},{24,8},{32,48},{40,56},{48,32},{56,40},{64,80... | collective-permute-start | bytes 786440 | tf_op jit(solution)/shard_map/ppermute | solution.py:36
  90.3 2.4 %collective-permute-start.31 = (bf16[8,128,128]{2,1,0:T(8,128)(2,1)S(1)}, bf16[8,128,128]{2,1,0:T(8,128)(2,1)S(1)}, u32[]{:S(2)}, u32[]{:S(2)}) collective-permute-start(bf16[8,128,128]{2,1,0:T(8,128)(2,1)S(1)} %get-tuple-element.106), channel_id=1, source_target_pairs={{0,24},{8,0},{16,8},{24,16},{32,56},{40,32},{48,40},{56,48},{64,88... | collective-permute-start | bytes 786440 | tf_op jit(solution)/shard_map/ppermute | solution.py:36
  94.5 4.5 %collective-permute-done.30.refs_6_ = bf16[8,128,128]{2,1,0:T(8,128)(2,1)S(1)} collective-permute-done((bf16[8,128,128]{2,1,0:T(8,128)(2,1)S(1)}, bf16[8,128,128]{2,1,0:T(8,128)(2,1)S(1)}, u32[]{:S(2)}, u32[]{:S(2)}) %collective-permute-start.30) | collective-permute-done | bytes 262176 | tf_op jit(solution)/shard_map/ppermute | solution.py:36
  99.5 4.3 %collective-permute-start.32 = (f32[128,256]{1,0:T(8,128)S(1)}, f32[128,256]{1,0:T(8,128)S(1)}, u32[]{:S(2)}, u32[]{:S(2)}) collective-permute-start(f32[128,256]{1,0:T(8,128)S(1)} %slice_select_fusion), channel_id=1, source_target_pairs={{0,1},{1,0},{2,3},{3,2},{4,5},{5,4},{6,7},{7,6},{8,9},{9,8},{10,11... | collective-permute-start | bytes 393224 | tf_op jit(solution)/shard_map/ppermute | solution.py:367
  104.9 3.5 %collective-permute-start.35 = (f32[32,256]{1,0:T(8,128)S(1)}, f32[32,256]{1,0:T(8,128)S(1)}, u32[]{:S(2)}, u32[]{:S(2)}) collective-permute-start(f32[32,256]{1,0:T(8,128)S(1)} %select_select_fusion.4), channel_id=1, source_target_pairs={{0,6},{1,7},{2,0},{3,1},{4,2},{5,3},{6,4},{7,5},{8,14},{9,15},{10,... | collective-permute-start | bytes 98312 | tf_op jit(solution)/shard_map/ppermute | solution.py:44
  109.4 3.5 %collective-permute-done.33 = f32[32,256]{1,0:T(8,128)S(1)} collective-permute-done((f32[32,256]{1,0:T(8,128)S(1)}, f32[32,256]{1,0:T(8,128)S(1)}, u32[]{:S(2)}, u32[]{:S(2)}) %collective-permute-start.33) | collective-permute-done | bytes 32800 | tf_op jit(solution)/shard_map/ppermute | solution.py:44
  112.9 3.5 %collective-permute-start.38 = (f32[32,256]{1,0:T(8,128)S(1)}, f32[32,256]{1,0:T(8,128)S(1)}, u32[]{:S(2)}, u32[]{:S(2)}) collective-permute-start(f32[32,256]{1,0:T(8,128)S(1)} %add_add_fusion.2), channel_id=1, source_target_pairs={{0,24},{8,0},{16,8},{24,16},{32,56},{40,32},{48,40},{56,48},{64,88... | collective-permute-start | bytes 98312 | tf_op jit(solution)/shard_map/ppermute | solution.py:36
  117.6 2.7 %collective-permute-done.37 = f32[32,256]{1,0:T(8,128)S(1)} collective-permute-done((f32[32,256]{1,0:T(8,128)S(1)}, f32[32,256]{1,0:T(8,128)S(1)}, u32[]{:S(2)}, u32[]{:S(2)}) %collective-permute-start.37) | collective-permute-done | bytes 32800 | tf_op jit(solution)/shard_map/ppermute | solution.py:36
  126.6 2.0 %collective-permute-start.43 = (f32[32,256]{1,0:T(8,128)S(1)}, f32[32,256]{1,0:T(8,128)S(1)}, u32[]{:S(2)}, u32[]{:S(2)}) collective-permute-start(f32[32,256]{1,0:T(8,128)S(1)} %add_add_fusion), channel_id=1, source_target_pairs={{0,4},{1,5},{2,6},{3,7},{4,0},{5,1},{6,2},{7,3},{8,12},{9,13},{10,... | collective-permute-start | bytes 98312 | tf_op jit(solution)/shard_map/ppermute | solution.py:44
  131.5 6.4 %collective-permute-start.45 = (f32[128,256]{1,0:T(8,128)S(1)}, f32[128,256]{1,0:T(8,128)S(1)}, u32[]{:S(2)}, u32[]{:S(2)}) collective-permute-start(f32[128,256]{1,0:T(8,128)S(1)} %pad_maximum_fusion), channel_id=1, source_target_pairs={{0,1},{1,0},{2,3},{3,2},{4,5},{5,4},{6,7},{7,6},{8,9},{9,8},{10,11... | collective-permute-start | bytes 393224 | tf_op jit(solution)/shard_map/ppermute | solution.py:48
  (116 shorter events, 52.5 us)
Async XLA Ops:
  1.8 19.1 %collective-permute-start.2 = (bf16[8,128,128]{2,1,0:T(8,128)(2,1)S(1)}, bf16[8,128,128]{2,1,0:T(8,128)(2,1)S(1)}, u32[]{:S(2)}, u32[]{:S(2)}) collective-permute-start(bf16[8,128,128]{2,1,0:T(8,128)(2,1)S(1)} %low_panels.1.after.refs_0_), channel_id=1, source_target_pairs={{0,2},{1,3},{2,4},{3,5},{4,6},{5,7},{6,0},{7,1},{8,10},{9,11},{10,... | collective-permute-start | bytes 786440 | tf_op jit(solution)/shard_map/ppermute | solution.py:44
  4.4 16.6 %collective-permute-start.1 = (bf16[8,128,128]{2,1,0:T(8,128)(2,1)S(1)}, bf16[8,128,128]{2,1,0:T(8,128)(2,1)S(1)}, u32[]{:S(2)}, u32[]{:S(2)}) collective-permute-start(bf16[8,128,128]{2,1,0:T(8,128)(2,1)S(1)} %low_panels.1.after.refs_0_), channel_id=1, source_target_pairs={{0,4},{1,5},{2,6},{3,7},{4,0},{5,1},{6,2},{7,3},{8,12},{9,13},{10,... | collective-permute-start | bytes 786440 | tf_op jit(solution)/shard_map/ppermute | solution.py:44
  7.7 13.3 %collective-permute-start = (bf16[8,128,128]{2,1,0:T(8,128)(2,1)S(1)}, bf16[8,128,128]{2,1,0:T(8,128)(2,1)S(1)}, u32[]{:S(2)}, u32[]{:S(2)}) collective-permute-start(bf16[8,128,128]{2,1,0:T(8,128)(2,1)S(1)} %low_panels.1.after.refs_0_), channel_id=1, source_target_pairs={{0,6},{1,7},{2,0},{3,1},{4,2},{5,3},{6,4},{7,5},{8,14},{9,15},{10,... | collective-permute-start | bytes 786440 | tf_op jit(solution)/shard_map/ppermute | solution.py:44
  8.4 14.3 %collective-permute-start.5 = (bf16[8,128,128]{2,1,0:T(8,128)(2,1)S(1)}, bf16[8,128,128]{2,1,0:T(8,128)(2,1)S(1)}, u32[]{:S(2)}, u32[]{:S(2)}) collective-permute-start(bf16[8,128,128]{2,1,0:T(8,128)(2,1)S(1)} %low_panels.1.after.refs_0_), channel_id=1, source_target_pairs={{0,1},{1,0},{2,3},{3,2},{4,5},{5,4},{6,7},{7,6},{8,9},{9,8},{10,11... | collective-permute-start | bytes 786440 | tf_op jit(solution)/shard_map/ppermute | solution.py:48
  21.9 8.8 %collective-permute-start.4 = (bf16[8,128,128]{2,1,0:T(8,128)(2,1)S(1)}, bf16[8,128,128]{2,1,0:T(8,128)(2,1)S(1)}, u32[]{:S(2)}, u32[]{:S(2)}) collective-permute-start(bf16[8,128,128]{2,1,0:T(8,128)(2,1)S(1)} %high_panels.1.a), channel_id=1, source_target_pairs={{0,2},{1,3},{2,4},{3,5},{4,6},{5,7},{6,0},{7,1},{8,10},{9,11},{10,... | collective-permute-start | bytes 786440 | tf_op jit(solution)/shard_map/ppermute | solution.py:44
  22.7 7.9 %collective-permute-start.3 = (bf16[8,128,128]{2,1,0:T(8,128)(2,1)S(1)}, bf16[8,128,128]{2,1,0:T(8,128)(2,1)S(1)}, u32[]{:S(2)}, u32[]{:S(2)}) collective-permute-start(bf16[8,128,128]{2,1,0:T(8,128)(2,1)S(1)} %high_panels.1.a), channel_id=1, source_target_pairs={{0,6},{1,7},{2,0},{3,1},{4,2},{5,3},{6,4},{7,5},{8,14},{9,15},{10,... | collective-permute-start | bytes 786440 | tf_op jit(solution)/shard_map/ppermute | solution.py:44
  32.5 9.4 %collective-permute-start.9 = (bf16[8,128,128]{2,1,0:T(8,128)(2,1)S(1)}, bf16[8,128,128]{2,1,0:T(8,128)(2,1)S(1)}, u32[]{:S(2)}, u32[]{:S(2)}) collective-permute-start(bf16[8,128,128]{2,1,0:T(8,128)(2,1)S(1)} %get-tuple-element.63.refs_0_), channel_id=1, source_target_pairs={{0,4},{1,5},{2,6},{3,7},{4,0},{5,1},{6,2},{7,3},{8,12},{9,13},{10,... | collective-permute-start | bytes 786440 | tf_op jit(solution)/shard_map/ppermute | solution.py:44
  33.9 14.4 %collective-permute-start.14 = (bf16[16,128,128]{2,1,0:T(8,128)(2,1)S(1)}, bf16[16,128,128]{2,1,0:T(8,128)(2,1)S(1)}, u32[]{:S(2)}, u32[]{:S(2)}) collective-permute-start(bf16[16,128,128]{2,1,0:T(8,128)(2,1)S(1)} %get-tuple-element.69), channel_id=1, source_target_pairs={{0,8},{8,16},{16,24},{24,0},{32,40},{40,48},{48,56},{56,32},{64,72... | collective-permute-start | bytes 1572872 | tf_op jit(solution)/shard_map/ppermute | solution.py:36
  35.1 13.1 %collective-permute-start.15 = (bf16[16,128,128]{2,1,0:T(8,128)(2,1)S(1)}, bf16[16,128,128]{2,1,0:T(8,128)(2,1)S(1)}, u32[]{:S(2)}, u32[]{:S(2)}) collective-permute-start(bf16[16,128,128]{2,1,0:T(8,128)(2,1)S(1)} %get-tuple-element.72), channel_id=1, source_target_pairs={{0,24},{8,0},{16,8},{24,16},{32,56},{40,32},{48,40},{56,48},{64,88... | collective-permute-start | bytes 1572872 | tf_op jit(solution)/shard_map/ppermute | solution.py:36
  36.6 13.8 %collective-permute-start.16 = (bf16[16,128,128]{2,1,0:T(8,128)(2,1)S(1)}, bf16[16,128,128]{2,1,0:T(8,128)(2,1)S(1)}, u32[]{:S(2)}, u32[]{:S(2)}) collective-permute-start(bf16[16,128,128]{2,1,0:T(8,128)(2,1)S(1)} %get-tuple-element.75), channel_id=1, source_target_pairs={{0,32},{8,40},{16,48},{24,56},{32,64},{40,72},{48,80},{56,88},{64,... | collective-permute-start | bytes 1572872 | tf_op jit(solution)/shard_map/ppermute | solution.py:40
  37.9 12.6 %collective-permute-start.17 = (bf16[16,128,128]{2,1,0:T(8,128)(2,1)S(1)}, bf16[16,128,128]{2,1,0:T(8,128)(2,1)S(1)}, u32[]{:S(2)}, u32[]{:S(2)}) collective-permute-start(bf16[16,128,128]{2,1,0:T(8,128)(2,1)S(1)} %get-tuple-element.78), channel_id=1, source_target_pairs={{0,96},{8,104},{16,112},{24,120},{32,0},{40,8},{48,16},{56,24},{64... | collective-permute-start | bytes 1572872 | tf_op jit(solution)/shard_map/ppermute | solution.py:40
  50.7 18.5 %collective-permute-start.18 = (bf16[24,128,128]{2,1,0:T(8,128)(2,1)S(1)}, bf16[24,128,128]{2,1,0:T(8,128)(2,1)S(1)}, u32[]{:S(2)}, u32[]{:S(2)}) collective-permute-start(bf16[24,128,128]{2,1,0:T(8,128)(2,1)S(1)} %get-tuple-element.80), channel_id=1, source_target_pairs={{0,8},{8,16},{16,24},{24,0},{32,40},{40,48},{48,56},{56,32},{64,72... | collective-permute-start | bytes 2359304 | tf_op jit(solution)/shard_map/ppermute | solution.py:36
  50.8 18.6 %collective-permute-start.19 = (bf16[24,128,128]{2,1,0:T(8,128)(2,1)S(1)}, bf16[24,128,128]{2,1,0:T(8,128)(2,1)S(1)}, u32[]{:S(2)}, u32[]{:S(2)}) collective-permute-start(bf16[24,128,128]{2,1,0:T(8,128)(2,1)S(1)} %get-tuple-element.81), channel_id=1, source_target_pairs={{0,24},{8,0},{16,8},{24,16},{32,56},{40,32},{48,40},{56,48},{64,88... | collective-permute-start | bytes 2359304 | tf_op jit(solution)/shard_map/ppermute | solution.py:36
  53.5 20.0 %collective-permute-start.22 = (bf16[24,128,128]{2,1,0:T(8,128)(2,1)S(1)}, bf16[24,128,128]{2,1,0:T(8,128)(2,1)S(1)}, u32[]{:S(2)}, u32[]{:S(2)}) collective-permute-start(bf16[24,128,128]{2,1,0:T(8,128)(2,1)S(1)} %get-tuple-element.85), channel_id=1, source_target_pairs={{0,32},{8,40},{16,48},{24,56},{32,64},{40,72},{48,80},{56,88},{64,... | collective-permute-start | bytes 2359304 | tf_op jit(solution)/shard_map/ppermute | solution.py:40
  55.3 19.6 %collective-permute-start.23 = (bf16[24,128,128]{2,1,0:T(8,128)(2,1)S(1)}, bf16[24,128,128]{2,1,0:T(8,128)(2,1)S(1)}, u32[]{:S(2)}, u32[]{:S(2)}) collective-permute-start(bf16[24,128,128]{2,1,0:T(8,128)(2,1)S(1)} %get-tuple-element.86), channel_id=1, source_target_pairs={{0,96},{8,104},{16,112},{24,120},{32,0},{40,8},{48,16},{56,24},{64... | collective-permute-start | bytes 2359304 | tf_op jit(solution)/shard_map/ppermute | solution.py:40
  69.3 8.3 %collective-permute-start.20 = (bf16[8,128,128]{2,1,0:T(8,128)(2,1)S(1)}, bf16[8,128,128]{2,1,0:T(8,128)(2,1)S(1)}, u32[]{:S(2)}, u32[]{:S(2)}) collective-permute-start(bf16[8,128,128]{2,1,0:T(8,128)(2,1)S(1)} %add_convert_fusion.3), channel_id=1, source_target_pairs={{0,8},{8,16},{16,24},{24,0},{32,40},{40,48},{48,56},{56,32},{64,72... | collective-permute-start | bytes 786440 | tf_op jit(solution)/shard_map/ppermute | solution.py:36
  69.5 8.1 %collective-permute-start.21 = (bf16[8,128,128]{2,1,0:T(8,128)(2,1)S(1)}, bf16[8,128,128]{2,1,0:T(8,128)(2,1)S(1)}, u32[]{:S(2)}, u32[]{:S(2)}) collective-permute-start(bf16[8,128,128]{2,1,0:T(8,128)(2,1)S(1)} %add_convert_fusion.2), channel_id=1, source_target_pairs={{0,24},{8,0},{16,8},{24,16},{32,56},{40,32},{48,40},{56,48},{64,88... | collective-permute-start | bytes 786440 | tf_op jit(solution)/shard_map/ppermute | solution.py:36
  73.5 8.0 %collective-permute-start.24 = (bf16[8,128,128]{2,1,0:T(8,128)(2,1)S(1)}, bf16[8,128,128]{2,1,0:T(8,128)(2,1)S(1)}, u32[]{:S(2)}, u32[]{:S(2)}) collective-permute-start(bf16[8,128,128]{2,1,0:T(8,128)(2,1)S(1)} %add_convert_fusion.1), channel_id=1, source_target_pairs={{0,32},{8,40},{16,48},{24,56},{32,64},{40,72},{48,80},{56,88},{64,... | collective-permute-start | bytes 786440 | tf_op jit(solution)/shard_map/ppermute | solution.py:40
  81.9 8.3 %collective-permute-start.26 = (bf16[8,128,128]{2,1,0:T(8,128)(2,1)S(1)}, bf16[8,128,128]{2,1,0:T(8,128)(2,1)S(1)}, u32[]{:S(2)}, u32[]{:S(2)}) collective-permute-start(bf16[8,128,128]{2,1,0:T(8,128)(2,1)S(1)} %get-tuple-element.100), channel_id=1, source_target_pairs={{0,32},{8,40},{16,48},{24,56},{32,64},{40,72},{48,80},{56,88},{64,... | collective-permute-start | bytes 786440 | tf_op jit(solution)/shard_map/ppermute | solution.py:40
  82.7 11.6 %collective-permute-start.27 = (bf16[8,128,128]{2,1,0:T(8,128)(2,1)S(1)}, bf16[8,128,128]{2,1,0:T(8,128)(2,1)S(1)}, u32[]{:S(2)}, u32[]{:S(2)}) collective-permute-start(bf16[8,128,128]{2,1,0:T(8,128)(2,1)S(1)} %get-tuple-element.101), channel_id=1, source_target_pairs={{0,64},{8,72},{16,80},{24,88},{32,96},{40,104},{48,112},{56,120},{... | collective-permute-start | bytes 786440 | tf_op jit(solution)/shard_map/ppermute | solution.py:40
  85.7 8.8 %collective-permute-start.28 = (bf16[8,128,128]{2,1,0:T(8,128)(2,1)S(1)}, bf16[8,128,128]{2,1,0:T(8,128)(2,1)S(1)}, u32[]{:S(2)}, u32[]{:S(2)}) collective-permute-start(bf16[8,128,128]{2,1,0:T(8,128)(2,1)S(1)} %get-tuple-element.102), channel_id=1, source_target_pairs={{0,96},{8,104},{16,112},{24,120},{32,0},{40,8},{48,16},{56,24},{64... | collective-permute-start | bytes 786440 | tf_op jit(solution)/shard_map/ppermute | solution.py:40
  86.5 8.0 %collective-permute-start.29 = (bf16[8,128,128]{2,1,0:T(8,128)(2,1)S(1)}, bf16[8,128,128]{2,1,0:T(8,128)(2,1)S(1)}, u32[]{:S(2)}, u32[]{:S(2)}) collective-permute-start(bf16[8,128,128]{2,1,0:T(8,128)(2,1)S(1)} %get-tuple-element.104), channel_id=1, source_target_pairs={{0,8},{8,16},{16,24},{24,0},{32,40},{40,48},{48,56},{56,32},{64,72... | collective-permute-start | bytes 786440 | tf_op jit(solution)/shard_map/ppermute | solution.py:36
  86.5 12.5 %collective-permute-start.30 = (bf16[8,128,128]{2,1,0:T(8,128)(2,1)S(1)}, bf16[8,128,128]{2,1,0:T(8,128)(2,1)S(1)}, u32[]{:S(2)}, u32[]{:S(2)}) collective-permute-start(bf16[8,128,128]{2,1,0:T(8,128)(2,1)S(1)} %get-tuple-element.105), channel_id=1, source_target_pairs={{0,16},{8,24},{16,0},{24,8},{32,48},{40,56},{48,32},{56,40},{64,80... | collective-permute-start | bytes 786440 | tf_op jit(solution)/shard_map/ppermute | solution.py:36
  90.3 8.7 %collective-permute-start.31 = (bf16[8,128,128]{2,1,0:T(8,128)(2,1)S(1)}, bf16[8,128,128]{2,1,0:T(8,128)(2,1)S(1)}, u32[]{:S(2)}, u32[]{:S(2)}) collective-permute-start(bf16[8,128,128]{2,1,0:T(8,128)(2,1)S(1)} %get-tuple-element.106), channel_id=1, source_target_pairs={{0,24},{8,0},{16,8},{24,16},{32,56},{40,32},{48,40},{56,48},{64,88... | collective-permute-start | bytes 786440 | tf_op jit(solution)/shard_map/ppermute | solution.py:36
  (30 other events, 229.2 us)

commit v4 on v3

--- a/solution.py
+++ b/solution.py
@@ -302,7 +302,7 @@
 
 
 def column_grad(parts, b):
-    four = parts[b // 4 * 4 : b // 4 * 4 + 4]
+    four = parts[b // 4 :: 2]
     halves = []
     for h in range(2):
         i = h * 4 + b % 4
@@ -393,9 +393,9 @@
     at = jnp.stack([y, x, z, core]).astype(jnp.int32)
     place = jnp.stack([y, x, core, z]).astype(jnp.int32)
     code = codes(at, row_block, col_block, live, low)
-    held, first, second, count, masks = stage(tiles[0, 0], code, place, low)
+    held, first, second, count, masks = stage(pltpu.with_memory_space_constraint(tiles[0, 0], pltpu.HBM), code, place, low)
     low_turned = cperm(low)
-    three, two, one = again((three, two, one), held)
+    two, three, one = again((two, three, one), held)
     low_all = [low, three, two, one, low_turned, cperm(three), cperm(two), cperm(one)]
     high = high_panels(out_grad, [three])
     one, three = zperm(high, 1), zperm(high, 3)
@@ -422,8 +422,9 @@
 
     before = middle(ordered(keep, got, got_both), [])
     sums = middle(ordered(keep_high, got_both, got_high), before)
-    parts = [sums[0]] + [yperm(sums[k], k) for k in (1, 2, 3)]
-    parts += [sums[4]] + [xperm(sums[4 + k], k) for k in (1, 2, 3)]
+    parts = [sums[0], sums[4]]
+    for k in (1, 3, 2):
+        parts += [yperm(sums[k], k), xperm(sums[4 + k], k)]
     input_grad, wg = input_share(parts, weight), weight_share(parts, features)
     nodes = 1024 * 128
     return input_grad, all_sum(wg, masks) * nodes ** (-0.5)

time: 140 us -> 138 us (0.986)
  Pallas kernels: 14.3 us -> 22.4 us
  waiting for transfers between devices: 46.4 us -> 40 us
  local copies, waits for them, and re-layouts: 7.66 us -> 3.1 us
    ppermute x12, waiting for transfers between devices: 20.1 us -> 13.2 us  [xperm(): return lax.ppermute(v, 'row', XP[s])]
    unnamed x16 -> x14, local copies, waits for them, and re-layouts: 7.66 us -> 3.1 us
    ppermute x1, starting transfers between devices: 4.29 us -> 7.33 us  [all_sum(): v = mine + lax.ppermute(other, 'col', CP)]
    pallas_call x2, Pallas kernels: 3.38 us -> 6.35 us  [send_products(): pl.pallas_call(send_kernel, in_specs=[SMEM, SMEM, VMEM] + [VMEM] * 8, out...]
    pallas_call x2, Pallas kernels: 3.28 us -> 6.24 us  [keep_products(): pl.pallas_call(keep_kernel, in_specs=[SMEM, SMEM, VMEM, VMEM], out_specs=...]
    ppermute x12, starting transfers between devices: 16.4 us -> 14.2 us  [yperm(): return lax.ppermute(v, 'row', YP[s])]
    pallas_call x1, Pallas kernels: 3.73 us -> 5.81 us  [stage(): pl.pallas_call(stage_kernel, in_specs=[ANY, SMEM, SMEM, ANY], out_specs=[...]
  transfers between devices with their start and end apart: 46 -> 46, of which waited for: 21 -> 18; matrix products, arithmetic and copies ran while one was open for 0% -> 0% of each run, Pallas kernels for 9% -> 15%
where the time goes in v4:
time: 138 us; the launch traced here: 137 us
  starting transfers between devices  69.2 us (50%)
  waiting for transfers between devices  40 us (29%)
  Pallas kernels  22.4 us (16%)
  local copies, waits for them, and re-layouts  3.1 us (2%)
    ppermute x12, starting transfers between devices, xperm(): return lax.ppermute(v, 'row', XP[s])  18.1 us
    ppermute x12, starting transfers between devices, zperm(): return lax.ppermute(v, 'col', ZP[s])  17.4 us
    ppermute x12, starting transfers between devices, yperm(): return lax.ppermute(v, 'row', YP[s])  14.2 us
    ppermute x12, waiting for transfers between devices, xperm(): return lax.ppermute(v, 'row', XP[s])  13.2 us
    ppermute x12, waiting for transfers between devices, yperm(): return lax.ppermute(v, 'row', YP[s])  13.2 us
    ppermute x12, waiting for transfers between devices, zperm(): return lax.ppermute(v, 'col', ZP[s])  12.6 us
    ppermute x9, starting transfers between devices, cperm(): return lax.ppermute(v, 'col', CP)  12.2 us
    ppermute x1, starting transfers between devices, all_sum(): v = mine + lax.ppermute(other, 'col', CP)  7.33 us
  transfers between devices with their start and end apart: 46, of which 18 were waited for; matrix products, arithmetic and copies ran while one was open for 0% of the time, Pallas kernels for 15%

profile of v4, /device:TPU:1, one launch (start us, length us, event | category | flops | bytes accessed | tf_op | source)
XLA Modules:
  0.0 136.9 jit_solution(16698327402436834914)
XLA Ops:
  1.8 2.5 %collective-permute-start.2 = (bf16[8,128,128]{2,1,0:T(8,128)(2,1)S(1)}, bf16[8,128,128]{2,1,0:T(8,128)(2,1)S(1)}, u32[]{:S(2)}, u32[]{:S(2)}) collective-permute-start(bf16[8,128,128]{2,1,0:T(8,128)(2,1)S(1)} %low_panels.1.after.refs_0_), channel_id=1, source_target_pairs={{0,2},{1,3},{2,4},{3,5},{4,6},{5,7},{6,0},{7,1},{8,10},{9,11},{10,... | collective-permute-start | bytes 786440 | tf_op jit(solution)/shard_map/ppermute | solution.py:44
  4.4 2.2 %collective-permute-start.1 = (bf16[8,128,128]{2,1,0:T(8,128)(2,1)S(1)}, bf16[8,128,128]{2,1,0:T(8,128)(2,1)S(1)}, u32[]{:S(2)}, u32[]{:S(2)}) collective-permute-start(bf16[8,128,128]{2,1,0:T(8,128)(2,1)S(1)} %low_panels.1.after.refs_0_), channel_id=1, source_target_pairs={{0,6},{1,7},{2,0},{3,1},{4,2},{5,3},{6,4},{7,5},{8,14},{9,15},{10,... | collective-permute-start | bytes 786440 | tf_op jit(solution)/shard_map/ppermute | solution.py:44
  12.0 5.8 %stage.1 = (bf16[384,128,128]{2,1,0:T(8,128)(2,1)S(1)}, s32[416]{0:T(512)S(1)}, s32[416]{0:T(512)S(1)}, s32[2]{0:T(128)S(1)}, s32[2,8,256]{2,1,0:T(8,128)S(1)}) custom-call(bf16[384,128,128]{2,1,0:T(8,128)(2,1)} %bitcast.5, s32[1,1,384]{2,1,0:T(1,128)S(1)} %codes.1.code, s32[4]{0:T(128)S(1)} %get-tuple-element.148.place, ...), custom_call_target="tpu_custom_call" | custom-call | tf_op jit(solution)/shard_map/stage/pallas_call | solution.py:162
  24.1 3.2 %send_products.2 = (bf16[64,128,128]{2,1,0:T(8,128)(2,1)S(1)}, bf16[16,128,128]{2,1,0:T(8,128)(2,1)S(1)}, bf16[16,128,128]{2,1,0:T(8,128)(2,1)S(1)}, bf16[16,128...) custom-call(s32[416]{0:T(512)S(1)} %get-tuple-element.58.entries, s32[2]{0:T(128)S(1)} %get-tuple-element.56.count, ...), custom_call_target="tpu_custom_call" | custom-call | tf_op jit(solution)/shard_map/send_products/pallas_call | solution.py:228
  27.3 3.2 %collective-permute-done.4.c = bf16[8,128,128]{2,1,0:T(8,128)(2,1)S(1)} collective-permute-done((bf16[8,128,128]{2,1,0:T(8,128)(2,1)S(1)}, bf16[8,128,128]{2,1,0:T(8,128)(2,1)S(1)}, u32[]{:S(2)}, u32[]{:S(2)}) %collective-permute-start.4) | collective-permute-done | bytes 262176 | tf_op jit(solution)/shard_map/ppermute | solution.py:44
  39.1 2.3 %collective-permute-done.9.refs_2_ = bf16[8,128,128]{2,1,0:T(8,128)(2,1)S(1)} collective-permute-done((bf16[8,128,128]{2,1,0:T(8,128)(2,1)S(1)}, bf16[8,128,128]{2,1,0:T(8,128)(2,1)S(1)}, u32[]{:S(2)}, u32[]{:S(2)}) %collective-permute-start.9) | collective-permute-done | bytes 262176 | tf_op jit(solution)/shard_map/ppermute | solution.py:44
  42.3 3.0 %keep_products.3 = (bf16[16,128,128]{2,1,0:T(8,128)(2,1)S(1)}, bf16[8,128,128]{2,1,0:T(8,128)(2,1)S(1)}, bf16[8,128,128]{2,1,0:T(8,128)(2,1)S(1)}, bf16[16,128,1...) custom-call(s32[416]{0:T(512)S(1)} %get-tuple-element.55.entries, ...), custom_call_target="tpu_custom_call" | custom-call | tf_op jit(solution)/shard_map/keep_products/pallas_call | solution.py:241
  45.3 3.2 %send_products.3 = (bf16[64,128,128]{2,1,0:T(8,128)(2,1)S(1)}, bf16[16,128,128]{2,1,0:T(8,128)(2,1)S(1)}, bf16[16,128,128]{2,1,0:T(8,128)(2,1)S(1)}, bf16[16,128...) custom-call(s32[416]{0:T(512)S(1)} %get-tuple-element.58.entries, s32[2]{0:T(128)S(1)} %get-tuple-element.56.count, ...), custom_call_target="tpu_custom_call" | custom-call | tf_op jit(solution)/shard_map/send_products/pallas_call | solution.py:228
  50.6 2.6 %collective-permute-start.19 = (bf16[24,128,128]{2,1,0:T(8,128)(2,1)S(1)}, bf16[24,128,128]{2,1,0:T(8,128)(2,1)S(1)}, u32[]{:S(2)}, u32[]{:S(2)}) collective-permute-start(bf16[24,128,128]{2,1,0:T(8,128)(2,1)S(1)} %get-tuple-element.81), channel_id=1, source_target_pairs={{0,24},{8,0},{16,8},{24,16},{32,56},{40,32},{48,40},{56,48},{64,88... | collective-permute-start | bytes 2359304 | tf_op jit(solution)/shard_map/ppermute | solution.py:36
  55.9 3.2 %keep_products.2 = (bf16[16,128,128]{2,1,0:T(8,128)(2,1)S(1)}, bf16[8,128,128]{2,1,0:T(8,128)(2,1)S(1)}, bf16[8,128,128]{2,1,0:T(8,128)(2,1)S(1)}, bf16[16,128,1...) custom-call(s32[416]{0:T(512)S(1)} %get-tuple-element.55.entries, ...), custom_call_target="tpu_custom_call" | custom-call | tf_op jit(solution)/shard_map/keep_products/pallas_call | solution.py:241
  59.1 9.9 %collective-permute-done.18.refs_3_.refs_1_ = bf16[24,128,128]{2,1,0:T(8,128)(2,1)S(1)} collective-permute-done((bf16[24,128,128]{2,1,0:T(8,128)(2,1)S(1)}, bf16[24,128,128]{2,1,0:T(8,128)(2,1)S(1)}, u32[]{:S(2)}, u32[]{:S(2)}) %collective-permute-start.18) | collective-permute-done | bytes 786464 | tf_op jit(solution)/shard_map/ppermute | solution.py:36
  69.2 2.7 %collective-permute-start.21 = (bf16[8,128,128]{2,1,0:T(8,128)(2,1)S(1)}, bf16[8,128,128]{2,1,0:T(8,128)(2,1)S(1)}, u32[]{:S(2)}, u32[]{:S(2)}) collective-permute-start(bf16[8,128,128]{2,1,0:T(8,128)(2,1)S(1)} %add_convert_fusion.2), channel_id=1, source_target_pairs={{0,24},{8,0},{16,8},{24,16},{32,56},{40,32},{48,40},{56,48},{64,88... | collective-permute-start | bytes 786440 | tf_op jit(solution)/shard_map/ppermute | solution.py:36
  72.8 2.1 %collective-permute-start.25 = (bf16[8,128,128]{2,1,0:T(8,128)(2,1)S(1)}, bf16[8,128,128]{2,1,0:T(8,128)(2,1)S(1)}, u32[]{:S(2)}, u32[]{:S(2)}) collective-permute-start(bf16[8,128,128]{2,1,0:T(8,128)(2,1)S(1)} %add_convert_fusion), channel_id=1, source_target_pairs={{0,96},{8,104},{16,112},{24,120},{32,0},{40,8},{48,16},{56,24},{64... | collective-permute-start | bytes 786440 | tf_op jit(solution)/shard_map/ppermute | solution.py:40
  75.5 3.3 %collective-permute-done.24.refs_8_ = bf16[8,128,128]{2,1,0:T(8,128)(2,1)S(1)} collective-permute-done((bf16[8,128,128]{2,1,0:T(8,128)(2,1)S(1)}, bf16[8,128,128]{2,1,0:T(8,128)(2,1)S(1)}, u32[]{:S(2)}, u32[]{:S(2)}) %collective-permute-start.24) | collective-permute-done | bytes 262176 | tf_op jit(solution)/shard_map/ppermute | solution.py:40
  80.0 2.1 %collective-permute-start.27 = (bf16[8,128,128]{2,1,0:T(8,128)(2,1)S(1)}, bf16[8,128,128]{2,1,0:T(8,128)(2,1)S(1)}, u32[]{:S(2)}, u32[]{:S(2)}) collective-permute-start(bf16[8,128,128]{2,1,0:T(8,128)(2,1)S(1)} %get-tuple-element.102), channel_id=1, source_target_pairs={{0,8},{8,16},{16,24},{24,0},{32,40},{40,48},{48,56},{56,32},{64,72... | collective-permute-start | bytes 786440 | tf_op jit(solution)/shard_map/ppermute | solution.py:36
  85.9 2.7 %collective-permute-start.31 = (bf16[8,128,128]{2,1,0:T(8,128)(2,1)S(1)}, bf16[8,128,128]{2,1,0:T(8,128)(2,1)S(1)}, u32[]{:S(2)}, u32[]{:S(2)}) collective-permute-start(bf16[8,128,128]{2,1,0:T(8,128)(2,1)S(1)} %get-tuple-element.106), channel_id=1, source_target_pairs={{0,16},{8,24},{16,0},{24,8},{32,48},{40,56},{48,32},{56,40},{64,80... | collective-permute-start | bytes 786440 | tf_op jit(solution)/shard_map/ppermute | solution.py:36
  88.8 5.2 %collective-permute-done.30.refs_6_ = bf16[8,128,128]{2,1,0:T(8,128)(2,1)S(1)} collective-permute-done((bf16[8,128,128]{2,1,0:T(8,128)(2,1)S(1)}, bf16[8,128,128]{2,1,0:T(8,128)(2,1)S(1)}, u32[]{:S(2)}, u32[]{:S(2)}) %collective-permute-start.30) | collective-permute-done | bytes 262176 | tf_op jit(solution)/shard_map/ppermute | solution.py:40
  94.6 7.3 %collective-permute-start.32 = (f32[128,256]{1,0:T(8,128)S(1)}, f32[128,256]{1,0:T(8,128)S(1)}, u32[]{:S(2)}, u32[]{:S(2)}) collective-permute-start(f32[128,256]{1,0:T(8,128)S(1)} %slice_select_fusion), channel_id=1, source_target_pairs={{0,1},{1,0},{2,3},{3,2},{4,5},{5,4},{6,7},{7,6},{8,9},{9,8},{10,11... | collective-permute-start | bytes 393224 | tf_op jit(solution)/shard_map/ppermute | solution.py:367
  102.9 2.3 %collective-permute-start.35 = (f32[32,256]{1,0:T(8,128)S(1)}, f32[32,256]{1,0:T(8,128)S(1)}, u32[]{:S(2)}, u32[]{:S(2)}) collective-permute-start(f32[32,256]{1,0:T(8,128)S(1)} %select_select_fusion.4), channel_id=1, source_target_pairs={{0,6},{1,7},{2,0},{3,1},{4,2},{5,3},{6,4},{7,5},{8,14},{9,15},{10,... | collective-permute-start | bytes 98312 | tf_op jit(solution)/shard_map/ppermute | solution.py:44
  106.6 3.0 %collective-permute-done.33 = f32[32,256]{1,0:T(8,128)S(1)} collective-permute-done((f32[32,256]{1,0:T(8,128)S(1)}, f32[32,256]{1,0:T(8,128)S(1)}, u32[]{:S(2)}, u32[]{:S(2)}) %collective-permute-start.33) | collective-permute-done | bytes 32800 | tf_op jit(solution)/shard_map/ppermute | solution.py:44
  111.0 2.2 %collective-permute-start.38 = (f32[32,256]{1,0:T(8,128)S(1)}, f32[32,256]{1,0:T(8,128)S(1)}, u32[]{:S(2)}, u32[]{:S(2)}) collective-permute-start(f32[32,256]{1,0:T(8,128)S(1)} %add_add_fusion.2), channel_id=1, source_target_pairs={{0,24},{8,0},{16,8},{24,16},{32,56},{40,32},{48,40},{56,48},{64,88... | collective-permute-start | bytes 98312 | tf_op jit(solution)/shard_map/ppermute | solution.py:36
  114.5 2.7 %collective-permute-done.37 = f32[32,256]{1,0:T(8,128)S(1)} collective-permute-done((f32[32,256]{1,0:T(8,128)S(1)}, f32[32,256]{1,0:T(8,128)S(1)}, u32[]{:S(2)}, u32[]{:S(2)}) %collective-permute-start.37) | collective-permute-done | bytes 32800 | tf_op jit(solution)/shard_map/ppermute | solution.py:36
  120.6 2.7 %collective-permute-done.40 = f32[32,256]{1,0:T(8,128)S(1)} collective-permute-done((f32[32,256]{1,0:T(8,128)S(1)}, f32[32,256]{1,0:T(8,128)S(1)}, u32[]{:S(2)}, u32[]{:S(2)}) %collective-permute-start.40) | collective-permute-done | bytes 32800 | tf_op jit(solution)/shard_map/ppermute | solution.py:40
  128.7 6.2 %collective-permute-start.45 = (f32[128,256]{1,0:T(8,128)S(1)}, f32[128,256]{1,0:T(8,128)S(1)}, u32[]{:S(2)}, u32[]{:S(2)}) collective-permute-start(f32[128,256]{1,0:T(8,128)S(1)} %pad_maximum_fusion), channel_id=1, source_target_pairs={{0,1},{1,0},{2,3},{3,2},{4,5},{5,4},{6,7},{7,6},{8,9},{9,8},{10,11... | collective-permute-start | bytes 393224 | tf_op jit(solution)/shard_map/ppermute | solution.py:48
  (114 shorter events, 50.3 us)
Async XLA Ops:
  1.8 16.0 %collective-permute-start.2 = (bf16[8,128,128]{2,1,0:T(8,128)(2,1)S(1)}, bf16[8,128,128]{2,1,0:T(8,128)(2,1)S(1)}, u32[]{:S(2)}, u32[]{:S(2)}) collective-permute-start(bf16[8,128,128]{2,1,0:T(8,128)(2,1)S(1)} %low_panels.1.after.refs_0_), channel_id=1, source_target_pairs={{0,2},{1,3},{2,4},{3,5},{4,6},{5,7},{6,0},{7,1},{8,10},{9,11},{10,... | collective-permute-start | bytes 786440 | tf_op jit(solution)/shard_map/ppermute | solution.py:44
  4.4 13.5 %collective-permute-start.1 = (bf16[8,128,128]{2,1,0:T(8,128)(2,1)S(1)}, bf16[8,128,128]{2,1,0:T(8,128)(2,1)S(1)}, u32[]{:S(2)}, u32[]{:S(2)}) collective-permute-start(bf16[8,128,128]{2,1,0:T(8,128)(2,1)S(1)} %low_panels.1.after.refs_0_), channel_id=1, source_target_pairs={{0,6},{1,7},{2,0},{3,1},{4,2},{5,3},{6,4},{7,5},{8,14},{9,15},{10,... | collective-permute-start | bytes 786440 | tf_op jit(solution)/shard_map/ppermute | solution.py:44
  6.6 12.4 %collective-permute-start = (bf16[8,128,128]{2,1,0:T(8,128)(2,1)S(1)}, bf16[8,128,128]{2,1,0:T(8,128)(2,1)S(1)}, u32[]{:S(2)}, u32[]{:S(2)}) collective-permute-start(bf16[8,128,128]{2,1,0:T(8,128)(2,1)S(1)} %low_panels.1.after.refs_0_), channel_id=1, source_target_pairs={{0,4},{1,5},{2,6},{3,7},{4,0},{5,1},{6,2},{7,3},{8,12},{9,13},{10,... | collective-permute-start | bytes 786440 | tf_op jit(solution)/shard_map/ppermute | solution.py:44
  7.8 14.5 %collective-permute-start.5 = (bf16[8,128,128]{2,1,0:T(8,128)(2,1)S(1)}, bf16[8,128,128]{2,1,0:T(8,128)(2,1)S(1)}, u32[]{:S(2)}, u32[]{:S(2)}) collective-permute-start(bf16[8,128,128]{2,1,0:T(8,128)(2,1)S(1)} %low_panels.1.after.refs_0_), channel_id=1, source_target_pairs={{0,1},{1,0},{2,3},{3,2},{4,5},{5,4},{6,7},{7,6},{8,9},{9,8},{10,11... | collective-permute-start | bytes 786440 | tf_op jit(solution)/shard_map/ppermute | solution.py:48
  21.4 9.1 %collective-permute-start.4 = (bf16[8,128,128]{2,1,0:T(8,128)(2,1)S(1)}, bf16[8,128,128]{2,1,0:T(8,128)(2,1)S(1)}, u32[]{:S(2)}, u32[]{:S(2)}) collective-permute-start(bf16[8,128,128]{2,1,0:T(8,128)(2,1)S(1)} %high_panels.1.a), channel_id=1, source_target_pairs={{0,2},{1,3},{2,4},{3,5},{4,6},{5,7},{6,0},{7,1},{8,10},{9,11},{10,... | collective-permute-start | bytes 786440 | tf_op jit(solution)/shard_map/ppermute | solution.py:44
  22.3 8.2 %collective-permute-start.3 = (bf16[8,128,128]{2,1,0:T(8,128)(2,1)S(1)}, bf16[8,128,128]{2,1,0:T(8,128)(2,1)S(1)}, u32[]{:S(2)}, u32[]{:S(2)}) collective-permute-start(bf16[8,128,128]{2,1,0:T(8,128)(2,1)S(1)} %high_panels.1.a), channel_id=1, source_target_pairs={{0,6},{1,7},{2,0},{3,1},{4,2},{5,3},{6,4},{7,5},{8,14},{9,15},{10,... | collective-permute-start | bytes 786440 | tf_op jit(solution)/shard_map/ppermute | solution.py:44
  32.0 9.4 %collective-permute-start.9 = (bf16[8,128,128]{2,1,0:T(8,128)(2,1)S(1)}, bf16[8,128,128]{2,1,0:T(8,128)(2,1)S(1)}, u32[]{:S(2)}, u32[]{:S(2)}) collective-permute-start(bf16[8,128,128]{2,1,0:T(8,128)(2,1)S(1)} %get-tuple-element.63.refs_0_), channel_id=1, source_target_pairs={{0,4},{1,5},{2,6},{3,7},{4,0},{5,1},{6,2},{7,3},{8,12},{9,13},{10,... | collective-permute-start | bytes 786440 | tf_op jit(solution)/shard_map/ppermute | solution.py:44
  33.6 14.9 %collective-permute-start.14 = (bf16[16,128,128]{2,1,0:T(8,128)(2,1)S(1)}, bf16[16,128,128]{2,1,0:T(8,128)(2,1)S(1)}, u32[]{:S(2)}, u32[]{:S(2)}) collective-permute-start(bf16[16,128,128]{2,1,0:T(8,128)(2,1)S(1)} %get-tuple-element.69), channel_id=1, source_target_pairs={{0,8},{8,16},{16,24},{24,0},{32,40},{40,48},{48,56},{56,32},{64,72... | collective-permute-start | bytes 1572872 | tf_op jit(solution)/shard_map/ppermute | solution.py:36
  34.8 13.7 %collective-permute-start.15 = (bf16[16,128,128]{2,1,0:T(8,128)(2,1)S(1)}, bf16[16,128,128]{2,1,0:T(8,128)(2,1)S(1)}, u32[]{:S(2)}, u32[]{:S(2)}) collective-permute-start(bf16[16,128,128]{2,1,0:T(8,128)(2,1)S(1)} %get-tuple-element.72), channel_id=1, source_target_pairs={{0,24},{8,0},{16,8},{24,16},{32,56},{40,32},{48,40},{56,48},{64,88... | collective-permute-start | bytes 1572872 | tf_op jit(solution)/shard_map/ppermute | solution.py:36
  36.3 13.8 %collective-permute-start.16 = (bf16[16,128,128]{2,1,0:T(8,128)(2,1)S(1)}, bf16[16,128,128]{2,1,0:T(8,128)(2,1)S(1)}, u32[]{:S(2)}, u32[]{:S(2)}) collective-permute-start(bf16[16,128,128]{2,1,0:T(8,128)(2,1)S(1)} %get-tuple-element.75), channel_id=1, source_target_pairs={{0,32},{8,40},{16,48},{24,56},{32,64},{40,72},{48,80},{56,88},{64,... | collective-permute-start | bytes 1572872 | tf_op jit(solution)/shard_map/ppermute | solution.py:40
  37.6 12.6 %collective-permute-start.17 = (bf16[16,128,128]{2,1,0:T(8,128)(2,1)S(1)}, bf16[16,128,128]{2,1,0:T(8,128)(2,1)S(1)}, u32[]{:S(2)}, u32[]{:S(2)}) collective-permute-start(bf16[16,128,128]{2,1,0:T(8,128)(2,1)S(1)} %get-tuple-element.78), channel_id=1, source_target_pairs={{0,96},{8,104},{16,112},{24,120},{32,0},{40,8},{48,16},{56,24},{64... | collective-permute-start | bytes 1572872 | tf_op jit(solution)/shard_map/ppermute | solution.py:40
  50.4 18.5 %collective-permute-start.18 = (bf16[24,128,128]{2,1,0:T(8,128)(2,1)S(1)}, bf16[24,128,128]{2,1,0:T(8,128)(2,1)S(1)}, u32[]{:S(2)}, u32[]{:S(2)}) collective-permute-start(bf16[24,128,128]{2,1,0:T(8,128)(2,1)S(1)} %get-tuple-element.80), channel_id=1, source_target_pairs={{0,8},{8,16},{16,24},{24,0},{32,40},{40,48},{48,56},{56,32},{64,72... | collective-permute-start | bytes 2359304 | tf_op jit(solution)/shard_map/ppermute | solution.py:36
  50.6 18.5 %collective-permute-start.19 = (bf16[24,128,128]{2,1,0:T(8,128)(2,1)S(1)}, bf16[24,128,128]{2,1,0:T(8,128)(2,1)S(1)}, u32[]{:S(2)}, u32[]{:S(2)}) collective-permute-start(bf16[24,128,128]{2,1,0:T(8,128)(2,1)S(1)} %get-tuple-element.81), channel_id=1, source_target_pairs={{0,24},{8,0},{16,8},{24,16},{32,56},{40,32},{48,40},{56,48},{64,88... | collective-permute-start | bytes 2359304 | tf_op jit(solution)/shard_map/ppermute | solution.py:36
  53.2 18.8 %collective-permute-start.22 = (bf16[24,128,128]{2,1,0:T(8,128)(2,1)S(1)}, bf16[24,128,128]{2,1,0:T(8,128)(2,1)S(1)}, u32[]{:S(2)}, u32[]{:S(2)}) collective-permute-start(bf16[24,128,128]{2,1,0:T(8,128)(2,1)S(1)} %get-tuple-element.85), channel_id=1, source_target_pairs={{0,32},{8,40},{16,48},{24,56},{32,64},{40,72},{48,80},{56,88},{64,... | collective-permute-start | bytes 2359304 | tf_op jit(solution)/shard_map/ppermute | solution.py:40
  54.1 18.6 %collective-permute-start.23 = (bf16[24,128,128]{2,1,0:T(8,128)(2,1)S(1)}, bf16[24,128,128]{2,1,0:T(8,128)(2,1)S(1)}, u32[]{:S(2)}, u32[]{:S(2)}) collective-permute-start(bf16[24,128,128]{2,1,0:T(8,128)(2,1)S(1)} %get-tuple-element.86), channel_id=1, source_target_pairs={{0,96},{8,104},{16,112},{24,120},{32,0},{40,8},{48,16},{56,24},{64... | collective-permute-start | bytes 2359304 | tf_op jit(solution)/shard_map/ppermute | solution.py:40
  69.0 6.5 %collective-permute-start.20 = (bf16[8,128,128]{2,1,0:T(8,128)(2,1)S(1)}, bf16[8,128,128]{2,1,0:T(8,128)(2,1)S(1)}, u32[]{:S(2)}, u32[]{:S(2)}) collective-permute-start(bf16[8,128,128]{2,1,0:T(8,128)(2,1)S(1)} %add_convert_fusion.3), channel_id=1, source_target_pairs={{0,8},{8,16},{16,24},{24,0},{32,40},{40,48},{48,56},{56,32},{64,72... | collective-permute-start | bytes 786440 | tf_op jit(solution)/shard_map/ppermute | solution.py:36
  72.0 6.8 %collective-permute-start.24 = (bf16[8,128,128]{2,1,0:T(8,128)(2,1)S(1)}, bf16[8,128,128]{2,1,0:T(8,128)(2,1)S(1)}, u32[]{:S(2)}, u32[]{:S(2)}) collective-permute-start(bf16[8,128,128]{2,1,0:T(8,128)(2,1)S(1)} %add_convert_fusion.1), channel_id=1, source_target_pairs={{0,32},{8,40},{16,48},{24,56},{32,64},{40,72},{48,80},{56,88},{64,... | collective-permute-start | bytes 786440 | tf_op jit(solution)/shard_map/ppermute | solution.py:40
  79.3 6.6 %collective-permute-start.26 = (bf16[8,128,128]{2,1,0:T(8,128)(2,1)S(1)}, bf16[8,128,128]{2,1,0:T(8,128)(2,1)S(1)}, u32[]{:S(2)}, u32[]{:S(2)}) collective-permute-start(bf16[8,128,128]{2,1,0:T(8,128)(2,1)S(1)} %get-tuple-element.101), channel_id=1, source_target_pairs={{0,32},{8,40},{16,48},{24,56},{32,64},{40,72},{48,80},{56,88},{64,... | collective-permute-start | bytes 786440 | tf_op jit(solution)/shard_map/ppermute | solution.py:40
  80.0 8.8 %collective-permute-start.27 = (bf16[8,128,128]{2,1,0:T(8,128)(2,1)S(1)}, bf16[8,128,128]{2,1,0:T(8,128)(2,1)S(1)}, u32[]{:S(2)}, u32[]{:S(2)}) collective-permute-start(bf16[8,128,128]{2,1,0:T(8,128)(2,1)S(1)} %get-tuple-element.102), channel_id=1, source_target_pairs={{0,8},{8,16},{16,24},{24,0},{32,40},{40,48},{48,56},{56,32},{64,72... | collective-permute-start | bytes 786440 | tf_op jit(solution)/shard_map/ppermute | solution.py:36
  82.1 6.7 %collective-permute-start.28 = (bf16[8,128,128]{2,1,0:T(8,128)(2,1)S(1)}, bf16[8,128,128]{2,1,0:T(8,128)(2,1)S(1)}, u32[]{:S(2)}, u32[]{:S(2)}) collective-permute-start(bf16[8,128,128]{2,1,0:T(8,128)(2,1)S(1)} %get-tuple-element.103), channel_id=1, source_target_pairs={{0,96},{8,104},{16,112},{24,120},{32,0},{40,8},{48,16},{56,24},{64... | collective-permute-start | bytes 786440 | tf_op jit(solution)/shard_map/ppermute | solution.py:40
  84.8 9.2 %collective-permute-start.30 = (bf16[8,128,128]{2,1,0:T(8,128)(2,1)S(1)}, bf16[8,128,128]{2,1,0:T(8,128)(2,1)S(1)}, u32[]{:S(2)}, u32[]{:S(2)}) collective-permute-start(bf16[8,128,128]{2,1,0:T(8,128)(2,1)S(1)} %get-tuple-element.105), channel_id=1, source_target_pairs={{0,64},{8,72},{16,80},{24,88},{32,96},{40,104},{48,112},{56,120},{... | collective-permute-start | bytes 786440 | tf_op jit(solution)/shard_map/ppermute | solution.py:40
  85.9 8.1 %collective-permute-start.31 = (bf16[8,128,128]{2,1,0:T(8,128)(2,1)S(1)}, bf16[8,128,128]{2,1,0:T(8,128)(2,1)S(1)}, u32[]{:S(2)}, u32[]{:S(2)}) collective-permute-start(bf16[8,128,128]{2,1,0:T(8,128)(2,1)S(1)} %get-tuple-element.106), channel_id=1, source_target_pairs={{0,16},{8,24},{16,0},{24,8},{32,48},{40,56},{48,32},{56,40},{64,80... | collective-permute-start | bytes 786440 | tf_op jit(solution)/shard_map/ppermute | solution.py:36
  94.6 8.3 %collective-permute-start.32 = (f32[128,256]{1,0:T(8,128)S(1)}, f32[128,256]{1,0:T(8,128)S(1)}, u32[]{:S(2)}, u32[]{:S(2)}) collective-permute-start(f32[128,256]{1,0:T(8,128)S(1)} %slice_select_fusion), channel_id=1, source_target_pairs={{0,1},{1,0},{2,3},{3,2},{4,5},{5,4},{6,7},{7,6},{8,9},{9,8},{10,11... | collective-permute-start | bytes 393224 | tf_op jit(solution)/shard_map/ppermute | solution.py:367
  128.7 7.5 %collective-permute-start.45 = (f32[128,256]{1,0:T(8,128)S(1)}, f32[128,256]{1,0:T(8,128)S(1)}, u32[]{:S(2)}, u32[]{:S(2)}) collective-permute-start(f32[128,256]{1,0:T(8,128)S(1)} %pad_maximum_fusion), channel_id=1, source_target_pairs={{0,1},{1,0},{2,3},{3,2},{4,5},{5,4},{6,7},{7,6},{8,9},{9,8},{10,11... | collective-permute-start | bytes 393224 | tf_op jit(solution)/shard_map/ppermute | solution.py:48
  (29 other events, 221.9 us)

commit v5 on v4

--- a/solution.py
+++ b/solution.py
@@ -388,7 +388,7 @@
 def local(out_grad, features, weight, tiles, row_block, col_block, live):
     row, col = lax.axis_index("row"), lax.axis_index("col")
     y, x, z, core = row // NX, row % NX, col // 2, col % 2
-    low = low_panels(out_grad)
+    low = low_panels(pltpu.with_memory_space_constraint(out_grad, pltpu.HBM))
     one, three, two = zperm(low, 1), zperm(low, 3), zperm(low, 2)
     at = jnp.stack([y, x, z, core]).astype(jnp.int32)
     place = jnp.stack([y, x, core, z]).astype(jnp.int32)

time: 138 us -> 137 us (level)
  waiting for transfers between devices: 40 us -> 44.7 us
  Pallas kernels: 22.4 us -> 19.3 us
    ppermute x12, waiting for transfers between devices: 13.2 us -> 17.7 us  [xperm(): return lax.ppermute(v, 'row', XP[s])]
    ppermute x12, starting transfers between devices: 18.1 us -> 14.8 us  [xperm(): return lax.ppermute(v, 'row', XP[s])]
    ppermute x12, starting transfers between devices: 14.2 us -> 17.3 us  [yperm(): return lax.ppermute(v, 'row', YP[s])]
    pallas_call x2, Pallas kernels: 6.35 us -> 4.36 us  [send_products(): pl.pallas_call(send_kernel, in_specs=[SMEM, SMEM, VMEM] + [VMEM] * 8, out...]
    pallas_call x2, Pallas kernels: 6.24 us -> 4.26 us  [keep_products(): pl.pallas_call(keep_kernel, in_specs=[SMEM, SMEM, VMEM, VMEM], out_specs=...]
    unnamed x14 -> x12, local copies, waits for them, and re-layouts: 3.1 us -> 2.06 us
  transfers between devices with their start and end apart: 46 -> 46, of which waited for: 18 -> 21; matrix products, arithmetic and copies ran while one was open for 0% -> 0% of each run, Pallas kernels for 15% -> 12%
where the time goes in v5:
time: 137 us
  starting transfers between devices  68.4 us (50%)
  waiting for transfers between devices  44.7 us (33%)
  Pallas kernels  19.3 us (14%)
  local copies, waits for them, and re-layouts  2.06 us (2%)
    ppermute x12, waiting for transfers between devices, xperm(): return lax.ppermute(v, 'row', XP[s])  17.7 us
    ppermute x12, starting transfers between devices, yperm(): return lax.ppermute(v, 'row', YP[s])  17.3 us
    ppermute x12, starting transfers between devices, zperm(): return lax.ppermute(v, 'col', ZP[s])  17.1 us
    ppermute x12, starting transfers between devices, xperm(): return lax.ppermute(v, 'row', XP[s])  14.8 us
    ppermute x12, waiting for transfers between devices, zperm(): return lax.ppermute(v, 'col', ZP[s])  13.5 us
    ppermute x12, waiting for transfers between devices, yperm(): return lax.ppermute(v, 'row', YP[s])  12.4 us
    ppermute x9, starting transfers between devices, cperm(): return lax.ppermute(v, 'col', CP)  12.4 us
    ppermute x1, starting transfers between devices, all_sum(): v = mine + lax.ppermute(other, 'col', CP)  6.82 us
  transfers between devices with their start and end apart: 46, of which 21 were waited for; matrix products, arithmetic and copies ran while one was open for 0% of the time, Pallas kernels for 12%

profile of v5, /device:TPU:1, one launch (start us, length us, event | category | flops | bytes accessed | tf_op | source)
XLA Modules:
  0.0 136.8 jit_solution(5752374412439701336)
XLA Ops:
  1.7 2.5 %collective-permute-start.2 = (bf16[8,128,128]{2,1,0:T(8,128)(2,1)S(1)}, bf16[8,128,128]{2,1,0:T(8,128)(2,1)S(1)}, u32[]{:S(2)}, u32[]{:S(2)}) collective-permute-start(bf16[8,128,128]{2,1,0:T(8,128)(2,1)S(1)} %low_panels.1.after.refs_0_), channel_id=1, source_target_pairs={{0,2},{1,3},{2,4},{3,5},{4,6},{5,7},{6,0},{7,1},{8,10},{9,11},{10,... | collective-permute-start | bytes 786440 | tf_op jit(solution)/shard_map/ppermute | solution.py:44
  4.3 2.2 %collective-permute-start.1 = (bf16[8,128,128]{2,1,0:T(8,128)(2,1)S(1)}, bf16[8,128,128]{2,1,0:T(8,128)(2,1)S(1)}, u32[]{:S(2)}, u32[]{:S(2)}) collective-permute-start(bf16[8,128,128]{2,1,0:T(8,128)(2,1)S(1)} %low_panels.1.after.refs_0_), channel_id=1, source_target_pairs={{0,6},{1,7},{2,0},{3,1},{4,2},{5,3},{6,4},{7,5},{8,14},{9,15},{10,... | collective-permute-start | bytes 786440 | tf_op jit(solution)/shard_map/ppermute | solution.py:44
  11.9 5.8 %stage.1 = (bf16[384,128,128]{2,1,0:T(8,128)(2,1)S(1)}, s32[416]{0:T(512)S(1)}, s32[416]{0:T(512)S(1)}, s32[2]{0:T(128)S(1)}, s32[2,8,256]{2,1,0:T(8,128)S(1)}) custom-call(bf16[384,128,128]{2,1,0:T(8,128)(2,1)} %bitcast.5, s32[1,1,384]{2,1,0:T(1,128)S(1)} %codes.1.code, s32[4]{0:T(128)S(1)} %get-tuple-element.148.place, ...), custom_call_target="tpu_custom_call" | custom-call | tf_op jit(solution)/shard_map/stage/pallas_call | solution.py:162
  24.0 2.2 %send_products.2 = (bf16[64,128,128]{2,1,0:T(8,128)(2,1)S(1)}, bf16[16,128,128]{2,1,0:T(8,128)(2,1)S(1)}, bf16[16,128,128]{2,1,0:T(8,128)(2,1)S(1)}, bf16[16,128...) custom-call(s32[416]{0:T(512)S(1)} %get-tuple-element.58.entries, s32[2]{0:T(128)S(1)} %get-tuple-element.56.count, ...), custom_call_target="tpu_custom_call" | custom-call | tf_op jit(solution)/shard_map/send_products/pallas_call | solution.py:228
  26.2 4.2 %collective-permute-done.4.c = bf16[8,128,128]{2,1,0:T(8,128)(2,1)S(1)} collective-permute-done((bf16[8,128,128]{2,1,0:T(8,128)(2,1)S(1)}, bf16[8,128,128]{2,1,0:T(8,128)(2,1)S(1)}, u32[]{:S(2)}, u32[]{:S(2)}) %collective-permute-start.4) | collective-permute-done | bytes 262176 | tf_op jit(solution)/shard_map/ppermute | solution.py:44
  39.0 2.3 %collective-permute-done.9.refs_2_ = bf16[8,128,128]{2,1,0:T(8,128)(2,1)S(1)} collective-permute-done((bf16[8,128,128]{2,1,0:T(8,128)(2,1)S(1)}, bf16[8,128,128]{2,1,0:T(8,128)(2,1)S(1)}, u32[]{:S(2)}, u32[]{:S(2)}) %collective-permute-start.9) | collective-permute-done | bytes 262176 | tf_op jit(solution)/shard_map/ppermute | solution.py:44
  42.2 2.0 %keep_products.3 = (bf16[16,128,128]{2,1,0:T(8,128)(2,1)S(1)}, bf16[8,128,128]{2,1,0:T(8,128)(2,1)S(1)}, bf16[8,128,128]{2,1,0:T(8,128)(2,1)S(1)}, bf16[16,128,1...) custom-call(s32[416]{0:T(512)S(1)} %get-tuple-element.55.entries, ...), custom_call_target="tpu_custom_call" | custom-call | tf_op jit(solution)/shard_map/keep_products/pallas_call | solution.py:241
  44.2 2.2 %send_products.3 = (bf16[64,128,128]{2,1,0:T(8,128)(2,1)S(1)}, bf16[16,128,128]{2,1,0:T(8,128)(2,1)S(1)}, bf16[16,128,128]{2,1,0:T(8,128)(2,1)S(1)}, bf16[16,128...) custom-call(s32[416]{0:T(512)S(1)} %get-tuple-element.58.entries, s32[2]{0:T(128)S(1)} %get-tuple-element.56.count, ...), custom_call_target="tpu_custom_call" | custom-call | tf_op jit(solution)/shard_map/send_products/pallas_call | solution.py:228
  47.8 2.2 %collective-permute-done.16.refs_7_.refs_6_ = bf16[16,128,128]{2,1,0:T(8,128)(2,1)S(1)} collective-permute-done((bf16[16,128,128]{2,1,0:T(8,128)(2,1)S(1)}, bf16[16,128,128]{2,1,0:T(8,128)(2,1)S(1)}, u32[]{:S(2)}, u32[]{:S(2)}) %collective-permute-start.16) | collective-permute-done | bytes 524320 | tf_op jit(solution)/shard_map/ppermute | solution.py:40
  56.1 2.2 %keep_products.2 = (bf16[16,128,128]{2,1,0:T(8,128)(2,1)S(1)}, bf16[8,128,128]{2,1,0:T(8,128)(2,1)S(1)}, bf16[8,128,128]{2,1,0:T(8,128)(2,1)S(1)}, bf16[16,128,1...) custom-call(s32[416]{0:T(512)S(1)} %get-tuple-element.55.entries, ...), custom_call_target="tpu_custom_call" | custom-call | tf_op jit(solution)/shard_map/keep_products/pallas_call | solution.py:241
  58.3 10.5 %collective-permute-done.18.refs_3_.refs_1_ = bf16[24,128,128]{2,1,0:T(8,128)(2,1)S(1)} collective-permute-done((bf16[24,128,128]{2,1,0:T(8,128)(2,1)S(1)}, bf16[24,128,128]{2,1,0:T(8,128)(2,1)S(1)}, u32[]{:S(2)}, u32[]{:S(2)}) %collective-permute-start.18) | collective-permute-done | bytes 786464 | tf_op jit(solution)/shard_map/ppermute | solution.py:36
  68.9 2.2 %collective-permute-start.20 = (bf16[8,128,128]{2,1,0:T(8,128)(2,1)S(1)}, bf16[8,128,128]{2,1,0:T(8,128)(2,1)S(1)}, u32[]{:S(2)}, u32[]{:S(2)}) collective-permute-start(bf16[8,128,128]{2,1,0:T(8,128)(2,1)S(1)} %add_convert_fusion.3), channel_id=1, source_target_pairs={{0,8},{8,16},{16,24},{24,0},{32,40},{40,48},{48,56},{56,32},{64,72... | collective-permute-start | bytes 786440 | tf_op jit(solution)/shard_map/ppermute | solution.py:36
  71.9 2.2 %collective-permute-start.24 = (bf16[8,128,128]{2,1,0:T(8,128)(2,1)S(1)}, bf16[8,128,128]{2,1,0:T(8,128)(2,1)S(1)}, u32[]{:S(2)}, u32[]{:S(2)}) collective-permute-start(bf16[8,128,128]{2,1,0:T(8,128)(2,1)S(1)} %add_convert_fusion.1), channel_id=1, source_target_pairs={{0,32},{8,40},{16,48},{24,56},{32,64},{40,72},{48,80},{56,88},{64,... | collective-permute-start | bytes 786440 | tf_op jit(solution)/shard_map/ppermute | solution.py:40
  81.1 2.6 %collective-permute-start.28 = (bf16[8,128,128]{2,1,0:T(8,128)(2,1)S(1)}, bf16[8,128,128]{2,1,0:T(8,128)(2,1)S(1)}, u32[]{:S(2)}, u32[]{:S(2)}) collective-permute-start(bf16[8,128,128]{2,1,0:T(8,128)(2,1)S(1)} %get-tuple-element.103), channel_id=1, source_target_pairs={{0,96},{8,104},{16,112},{24,120},{32,0},{40,8},{48,16},{56,24},{64... | collective-permute-start | bytes 786440 | tf_op jit(solution)/shard_map/ppermute | solution.py:40
  83.7 1.9 %collective-permute-start.29 = (bf16[8,128,128]{2,1,0:T(8,128)(2,1)S(1)}, bf16[8,128,128]{2,1,0:T(8,128)(2,1)S(1)}, u32[]{:S(2)}, u32[]{:S(2)}) collective-permute-start(bf16[8,128,128]{2,1,0:T(8,128)(2,1)S(1)} %get-tuple-element.104), channel_id=1, source_target_pairs={{0,24},{8,0},{16,8},{24,16},{32,56},{40,32},{48,40},{56,48},{64,88... | collective-permute-start | bytes 786440 | tf_op jit(solution)/shard_map/ppermute | solution.py:36
  89.2 5.4 %collective-permute-done.30.refs_6_ = bf16[8,128,128]{2,1,0:T(8,128)(2,1)S(1)} collective-permute-done((bf16[8,128,128]{2,1,0:T(8,128)(2,1)S(1)}, bf16[8,128,128]{2,1,0:T(8,128)(2,1)S(1)}, u32[]{:S(2)}, u32[]{:S(2)}) %collective-permute-start.30) | collective-permute-done | bytes 262176 | tf_op jit(solution)/shard_map/ppermute | solution.py:40
  95.2 6.8 %collective-permute-start.32 = (f32[128,256]{1,0:T(8,128)S(1)}, f32[128,256]{1,0:T(8,128)S(1)}, u32[]{:S(2)}, u32[]{:S(2)}) collective-permute-start(f32[128,256]{1,0:T(8,128)S(1)} %slice_select_fusion), channel_id=1, source_target_pairs={{0,1},{1,0},{2,3},{3,2},{4,5},{5,4},{6,7},{7,6},{8,9},{9,8},{10,11... | collective-permute-start | bytes 393224 | tf_op jit(solution)/shard_map/ppermute | solution.py:367
  103.1 2.0 %collective-permute-start.35 = (f32[32,256]{1,0:T(8,128)S(1)}, f32[32,256]{1,0:T(8,128)S(1)}, u32[]{:S(2)}, u32[]{:S(2)}) collective-permute-start(f32[32,256]{1,0:T(8,128)S(1)} %select_select_fusion.4), channel_id=1, source_target_pairs={{0,6},{1,7},{2,0},{3,1},{4,2},{5,3},{6,4},{7,5},{8,14},{9,15},{10,... | collective-permute-start | bytes 98312 | tf_op jit(solution)/shard_map/ppermute | solution.py:44
  106.5 3.0 %collective-permute-done.33 = f32[32,256]{1,0:T(8,128)S(1)} collective-permute-done((f32[32,256]{1,0:T(8,128)S(1)}, f32[32,256]{1,0:T(8,128)S(1)}, u32[]{:S(2)}, u32[]{:S(2)}) %collective-permute-start.33) | collective-permute-done | bytes 32800 | tf_op jit(solution)/shard_map/ppermute | solution.py:44
  110.9 2.2 %collective-permute-start.38 = (f32[32,256]{1,0:T(8,128)S(1)}, f32[32,256]{1,0:T(8,128)S(1)}, u32[]{:S(2)}, u32[]{:S(2)}) collective-permute-start(f32[32,256]{1,0:T(8,128)S(1)} %add_add_fusion.2), channel_id=1, source_target_pairs={{0,24},{8,0},{16,8},{24,16},{32,56},{40,32},{48,40},{56,48},{64,88... | collective-permute-start | bytes 98312 | tf_op jit(solution)/shard_map/ppermute | solution.py:36
  114.4 2.7 %collective-permute-done.37 = f32[32,256]{1,0:T(8,128)S(1)} collective-permute-done((f32[32,256]{1,0:T(8,128)S(1)}, f32[32,256]{1,0:T(8,128)S(1)}, u32[]{:S(2)}, u32[]{:S(2)}) %collective-permute-start.37) | collective-permute-done | bytes 32800 | tf_op jit(solution)/shard_map/ppermute | solution.py:36
  120.4 2.5 %collective-permute-done.40 = f32[32,256]{1,0:T(8,128)S(1)} collective-permute-done((f32[32,256]{1,0:T(8,128)S(1)}, f32[32,256]{1,0:T(8,128)S(1)}, u32[]{:S(2)}, u32[]{:S(2)}) %collective-permute-start.40) | collective-permute-done | bytes 32800 | tf_op jit(solution)/shard_map/ppermute | solution.py:40
  123.3 2.0 %collective-permute-start.43 = (f32[32,256]{1,0:T(8,128)S(1)}, f32[32,256]{1,0:T(8,128)S(1)}, u32[]{:S(2)}, u32[]{:S(2)}) collective-permute-start(f32[32,256]{1,0:T(8,128)S(1)} %add_add_fusion), channel_id=1, source_target_pairs={{0,4},{1,5},{2,6},{3,7},{4,0},{5,1},{6,2},{7,3},{8,12},{9,13},{10,... | collective-permute-start | bytes 98312 | tf_op jit(solution)/shard_map/ppermute | solution.py:44
  128.2 6.4 %collective-permute-start.45 = (f32[128,256]{1,0:T(8,128)S(1)}, f32[128,256]{1,0:T(8,128)S(1)}, u32[]{:S(2)}, u32[]{:S(2)}) collective-permute-start(f32[128,256]{1,0:T(8,128)S(1)} %pad_maximum_fusion), channel_id=1, source_target_pairs={{0,1},{1,0},{2,3},{3,2},{4,5},{5,4},{6,7},{7,6},{8,9},{9,8},{10,11... | collective-permute-start | bytes 393224 | tf_op jit(solution)/shard_map/ppermute | solution.py:48
  (112 shorter events, 55.8 us)
Async XLA Ops:
  1.7 16.0 %collective-permute-start.2 = (bf16[8,128,128]{2,1,0:T(8,128)(2,1)S(1)}, bf16[8,128,128]{2,1,0:T(8,128)(2,1)S(1)}, u32[]{:S(2)}, u32[]{:S(2)}) collective-permute-start(bf16[8,128,128]{2,1,0:T(8,128)(2,1)S(1)} %low_panels.1.after.refs_0_), channel_id=1, source_target_pairs={{0,2},{1,3},{2,4},{3,5},{4,6},{5,7},{6,0},{7,1},{8,10},{9,11},{10,... | collective-permute-start | bytes 786440 | tf_op jit(solution)/shard_map/ppermute | solution.py:44
  4.3 13.5 %collective-permute-start.1 = (bf16[8,128,128]{2,1,0:T(8,128)(2,1)S(1)}, bf16[8,128,128]{2,1,0:T(8,128)(2,1)S(1)}, u32[]{:S(2)}, u32[]{:S(2)}) collective-permute-start(bf16[8,128,128]{2,1,0:T(8,128)(2,1)S(1)} %low_panels.1.after.refs_0_), channel_id=1, source_target_pairs={{0,6},{1,7},{2,0},{3,1},{4,2},{5,3},{6,4},{7,5},{8,14},{9,15},{10,... | collective-permute-start | bytes 786440 | tf_op jit(solution)/shard_map/ppermute | solution.py:44
  6.5 12.4 %collective-permute-start = (bf16[8,128,128]{2,1,0:T(8,128)(2,1)S(1)}, bf16[8,128,128]{2,1,0:T(8,128)(2,1)S(1)}, u32[]{:S(2)}, u32[]{:S(2)}) collective-permute-start(bf16[8,128,128]{2,1,0:T(8,128)(2,1)S(1)} %low_panels.1.after.refs_0_), channel_id=1, source_target_pairs={{0,4},{1,5},{2,6},{3,7},{4,0},{5,1},{6,2},{7,3},{8,12},{9,13},{10,... | collective-permute-start | bytes 786440 | tf_op jit(solution)/shard_map/ppermute | solution.py:44
  7.7 14.5 %collective-permute-start.5 = (bf16[8,128,128]{2,1,0:T(8,128)(2,1)S(1)}, bf16[8,128,128]{2,1,0:T(8,128)(2,1)S(1)}, u32[]{:S(2)}, u32[]{:S(2)}) collective-permute-start(bf16[8,128,128]{2,1,0:T(8,128)(2,1)S(1)} %low_panels.1.after.refs_0_), channel_id=1, source_target_pairs={{0,1},{1,0},{2,3},{3,2},{4,5},{5,4},{6,7},{7,6},{8,9},{9,8},{10,11... | collective-permute-start | bytes 786440 | tf_op jit(solution)/shard_map/ppermute | solution.py:48
  21.2 9.1 %collective-permute-start.4 = (bf16[8,128,128]{2,1,0:T(8,128)(2,1)S(1)}, bf16[8,128,128]{2,1,0:T(8,128)(2,1)S(1)}, u32[]{:S(2)}, u32[]{:S(2)}) collective-permute-start(bf16[8,128,128]{2,1,0:T(8,128)(2,1)S(1)} %high_panels.1.a), channel_id=1, source_target_pairs={{0,2},{1,3},{2,4},{3,5},{4,6},{5,7},{6,0},{7,1},{8,10},{9,11},{10,... | collective-permute-start | bytes 786440 | tf_op jit(solution)/shard_map/ppermute | solution.py:44
  22.2 8.2 %collective-permute-start.3 = (bf16[8,128,128]{2,1,0:T(8,128)(2,1)S(1)}, bf16[8,128,128]{2,1,0:T(8,128)(2,1)S(1)}, u32[]{:S(2)}, u32[]{:S(2)}) collective-permute-start(bf16[8,128,128]{2,1,0:T(8,128)(2,1)S(1)} %high_panels.1.a), channel_id=1, source_target_pairs={{0,6},{1,7},{2,0},{3,1},{4,2},{5,3},{6,4},{7,5},{8,14},{9,15},{10,... | collective-permute-start | bytes 786440 | tf_op jit(solution)/shard_map/ppermute | solution.py:44
  31.9 9.4 %collective-permute-start.9 = (bf16[8,128,128]{2,1,0:T(8,128)(2,1)S(1)}, bf16[8,128,128]{2,1,0:T(8,128)(2,1)S(1)}, u32[]{:S(2)}, u32[]{:S(2)}) collective-permute-start(bf16[8,128,128]{2,1,0:T(8,128)(2,1)S(1)} %get-tuple-element.63.refs_0_), channel_id=1, source_target_pairs={{0,4},{1,5},{2,6},{3,7},{4,0},{5,1},{6,2},{7,3},{8,12},{9,13},{10,... | collective-permute-start | bytes 786440 | tf_op jit(solution)/shard_map/ppermute | solution.py:44
  33.5 14.4 %collective-permute-start.14 = (bf16[16,128,128]{2,1,0:T(8,128)(2,1)S(1)}, bf16[16,128,128]{2,1,0:T(8,128)(2,1)S(1)}, u32[]{:S(2)}, u32[]{:S(2)}) collective-permute-start(bf16[16,128,128]{2,1,0:T(8,128)(2,1)S(1)} %get-tuple-element.69), channel_id=1, source_target_pairs={{0,8},{8,16},{16,24},{24,0},{32,40},{40,48},{48,56},{56,32},{64,72... | collective-permute-start | bytes 1572872 | tf_op jit(solution)/shard_map/ppermute | solution.py:36
  34.7 13.1 %collective-permute-start.15 = (bf16[16,128,128]{2,1,0:T(8,128)(2,1)S(1)}, bf16[16,128,128]{2,1,0:T(8,128)(2,1)S(1)}, u32[]{:S(2)}, u32[]{:S(2)}) collective-permute-start(bf16[16,128,128]{2,1,0:T(8,128)(2,1)S(1)} %get-tuple-element.72), channel_id=1, source_target_pairs={{0,24},{8,0},{16,8},{24,16},{32,56},{40,32},{48,40},{56,48},{64,88... | collective-permute-start | bytes 1572872 | tf_op jit(solution)/shard_map/ppermute | solution.py:36
  36.2 13.8 %collective-permute-start.16 = (bf16[16,128,128]{2,1,0:T(8,128)(2,1)S(1)}, bf16[16,128,128]{2,1,0:T(8,128)(2,1)S(1)}, u32[]{:S(2)}, u32[]{:S(2)}) collective-permute-start(bf16[16,128,128]{2,1,0:T(8,128)(2,1)S(1)} %get-tuple-element.75), channel_id=1, source_target_pairs={{0,32},{8,40},{16,48},{24,56},{32,64},{40,72},{48,80},{56,88},{64,... | collective-permute-start | bytes 1572872 | tf_op jit(solution)/shard_map/ppermute | solution.py:40
  37.5 12.6 %collective-permute-start.17 = (bf16[16,128,128]{2,1,0:T(8,128)(2,1)S(1)}, bf16[16,128,128]{2,1,0:T(8,128)(2,1)S(1)}, u32[]{:S(2)}, u32[]{:S(2)}) collective-permute-start(bf16[16,128,128]{2,1,0:T(8,128)(2,1)S(1)} %get-tuple-element.78), channel_id=1, source_target_pairs={{0,96},{8,104},{16,112},{24,120},{32,0},{40,8},{48,16},{56,24},{64... | collective-permute-start | bytes 1572872 | tf_op jit(solution)/shard_map/ppermute | solution.py:40
  50.3 18.5 %collective-permute-start.18 = (bf16[24,128,128]{2,1,0:T(8,128)(2,1)S(1)}, bf16[24,128,128]{2,1,0:T(8,128)(2,1)S(1)}, u32[]{:S(2)}, u32[]{:S(2)}) collective-permute-start(bf16[24,128,128]{2,1,0:T(8,128)(2,1)S(1)} %get-tuple-element.80), channel_id=1, source_target_pairs={{0,8},{8,16},{16,24},{24,0},{32,40},{40,48},{48,56},{56,32},{64,72... | collective-permute-start | bytes 2359304 | tf_op jit(solution)/shard_map/ppermute | solution.py:36
  52.0 19.1 %collective-permute-start.19 = (bf16[24,128,128]{2,1,0:T(8,128)(2,1)S(1)}, bf16[24,128,128]{2,1,0:T(8,128)(2,1)S(1)}, u32[]{:S(2)}, u32[]{:S(2)}) collective-permute-start(bf16[24,128,128]{2,1,0:T(8,128)(2,1)S(1)} %get-tuple-element.81), channel_id=1, source_target_pairs={{0,24},{8,0},{16,8},{24,16},{32,56},{40,32},{48,40},{56,48},{64,88... | collective-permute-start | bytes 2359304 | tf_op jit(solution)/shard_map/ppermute | solution.py:36
  53.1 18.8 %collective-permute-start.22 = (bf16[24,128,128]{2,1,0:T(8,128)(2,1)S(1)}, bf16[24,128,128]{2,1,0:T(8,128)(2,1)S(1)}, u32[]{:S(2)}, u32[]{:S(2)}) collective-permute-start(bf16[24,128,128]{2,1,0:T(8,128)(2,1)S(1)} %get-tuple-element.85), channel_id=1, source_target_pairs={{0,32},{8,40},{16,48},{24,56},{32,64},{40,72},{48,80},{56,88},{64,... | collective-permute-start | bytes 2359304 | tf_op jit(solution)/shard_map/ppermute | solution.py:40
  54.8 19.3 %collective-permute-start.23 = (bf16[24,128,128]{2,1,0:T(8,128)(2,1)S(1)}, bf16[24,128,128]{2,1,0:T(8,128)(2,1)S(1)}, u32[]{:S(2)}, u32[]{:S(2)}) collective-permute-start(bf16[24,128,128]{2,1,0:T(8,128)(2,1)S(1)} %get-tuple-element.86), channel_id=1, source_target_pairs={{0,96},{8,104},{16,112},{24,120},{32,0},{40,8},{48,16},{56,24},{64... | collective-permute-start | bytes 2359304 | tf_op jit(solution)/shard_map/ppermute | solution.py:40
  68.9 7.1 %collective-permute-start.20 = (bf16[8,128,128]{2,1,0:T(8,128)(2,1)S(1)}, bf16[8,128,128]{2,1,0:T(8,128)(2,1)S(1)}, u32[]{:S(2)}, u32[]{:S(2)}) collective-permute-start(bf16[8,128,128]{2,1,0:T(8,128)(2,1)S(1)} %add_convert_fusion.3), channel_id=1, source_target_pairs={{0,8},{8,16},{16,24},{24,0},{32,40},{40,48},{48,56},{56,32},{64,72... | collective-permute-start | bytes 786440 | tf_op jit(solution)/shard_map/ppermute | solution.py:36
  71.9 7.3 %collective-permute-start.24 = (bf16[8,128,128]{2,1,0:T(8,128)(2,1)S(1)}, bf16[8,128,128]{2,1,0:T(8,128)(2,1)S(1)}, u32[]{:S(2)}, u32[]{:S(2)}) collective-permute-start(bf16[8,128,128]{2,1,0:T(8,128)(2,1)S(1)} %add_convert_fusion.1), channel_id=1, source_target_pairs={{0,32},{8,40},{16,48},{24,56},{32,64},{40,72},{48,80},{56,88},{64,... | collective-permute-start | bytes 786440 | tf_op jit(solution)/shard_map/ppermute | solution.py:40
  80.2 6.8 %collective-permute-start.26 = (bf16[8,128,128]{2,1,0:T(8,128)(2,1)S(1)}, bf16[8,128,128]{2,1,0:T(8,128)(2,1)S(1)}, u32[]{:S(2)}, u32[]{:S(2)}) collective-permute-start(bf16[8,128,128]{2,1,0:T(8,128)(2,1)S(1)} %get-tuple-element.101), channel_id=1, source_target_pairs={{0,32},{8,40},{16,48},{24,56},{32,64},{40,72},{48,80},{56,88},{64,... | collective-permute-start | bytes 786440 | tf_op jit(solution)/shard_map/ppermute | solution.py:40
  81.1 7.1 %collective-permute-start.27 = (bf16[8,128,128]{2,1,0:T(8,128)(2,1)S(1)}, bf16[8,128,128]{2,1,0:T(8,128)(2,1)S(1)}, u32[]{:S(2)}, u32[]{:S(2)}) collective-permute-start(bf16[8,128,128]{2,1,0:T(8,128)(2,1)S(1)} %get-tuple-element.102), channel_id=1, source_target_pairs={{0,8},{8,16},{16,24},{24,0},{32,40},{40,48},{48,56},{56,32},{64,72... | collective-permute-start | bytes 786440 | tf_op jit(solution)/shard_map/ppermute | solution.py:36
  81.1 7.1 %collective-permute-start.28 = (bf16[8,128,128]{2,1,0:T(8,128)(2,1)S(1)}, bf16[8,128,128]{2,1,0:T(8,128)(2,1)S(1)}, u32[]{:S(2)}, u32[]{:S(2)}) collective-permute-start(bf16[8,128,128]{2,1,0:T(8,128)(2,1)S(1)} %get-tuple-element.103), channel_id=1, source_target_pairs={{0,96},{8,104},{16,112},{24,120},{32,0},{40,8},{48,16},{56,24},{64... | collective-permute-start | bytes 786440 | tf_op jit(solution)/shard_map/ppermute | solution.py:40
  85.6 9.1 %collective-permute-start.30 = (bf16[8,128,128]{2,1,0:T(8,128)(2,1)S(1)}, bf16[8,128,128]{2,1,0:T(8,128)(2,1)S(1)}, u32[]{:S(2)}, u32[]{:S(2)}) collective-permute-start(bf16[8,128,128]{2,1,0:T(8,128)(2,1)S(1)} %get-tuple-element.105), channel_id=1, source_target_pairs={{0,64},{8,72},{16,80},{24,88},{32,96},{40,104},{48,112},{56,120},{... | collective-permute-start | bytes 786440 | tf_op jit(solution)/shard_map/ppermute | solution.py:40
  87.0 7.7 %collective-permute-start.31 = (bf16[8,128,128]{2,1,0:T(8,128)(2,1)S(1)}, bf16[8,128,128]{2,1,0:T(8,128)(2,1)S(1)}, u32[]{:S(2)}, u32[]{:S(2)}) collective-permute-start(bf16[8,128,128]{2,1,0:T(8,128)(2,1)S(1)} %get-tuple-element.106), channel_id=1, source_target_pairs={{0,16},{8,24},{16,0},{24,8},{32,48},{40,56},{48,32},{56,40},{64,80... | collective-permute-start | bytes 786440 | tf_op jit(solution)/shard_map/ppermute | solution.py:36
  95.2 7.8 %collective-permute-start.32 = (f32[128,256]{1,0:T(8,128)S(1)}, f32[128,256]{1,0:T(8,128)S(1)}, u32[]{:S(2)}, u32[]{:S(2)}) collective-permute-start(f32[128,256]{1,0:T(8,128)S(1)} %slice_select_fusion), channel_id=1, source_target_pairs={{0,1},{1,0},{2,3},{3,2},{4,5},{5,4},{6,7},{7,6},{8,9},{9,8},{10,11... | collective-permute-start | bytes 393224 | tf_op jit(solution)/shard_map/ppermute | solution.py:367
  128.2 7.8 %collective-permute-start.45 = (f32[128,256]{1,0:T(8,128)S(1)}, f32[128,256]{1,0:T(8,128)S(1)}, u32[]{:S(2)}, u32[]{:S(2)}) collective-permute-start(f32[128,256]{1,0:T(8,128)S(1)} %pad_maximum_fusion), channel_id=1, source_target_pairs={{0,1},{1,0},{2,3},{3,2},{4,5},{5,4},{6,7},{7,6},{8,9},{9,8},{10,11... | collective-permute-start | bytes 393224 | tf_op jit(solution)/shard_map/ppermute | solution.py:48
  (28 other events, 220.5 us)

commit v6 on v4

--- a/solution.py
+++ b/solution.py
@@ -393,9 +393,9 @@
     at = jnp.stack([y, x, z, core]).astype(jnp.int32)
     place = jnp.stack([y, x, core, z]).astype(jnp.int32)
     code = codes(at, row_block, col_block, live, low)
-    held, first, second, count, masks = stage(pltpu.with_memory_space_constraint(tiles[0, 0], pltpu.HBM), code, place, low)
+    held, first, second, count, masks = stage(tiles[0, 0], code, place, low)
     low_turned = cperm(low)
-    two, three, one = again((two, three, one), held)
+    three, two, one = again((three, two, one), held)
     low_all = [low, three, two, one, low_turned, cperm(three), cperm(two), cperm(one)]
     high = high_panels(out_grad, [three])
     one, three = zperm(high, 1), zperm(high, 3)

time: 138 us -> 139 us (level)
  local copies, waits for them, and re-layouts: 3.1 us -> 7.66 us
  Pallas kernels: 22.4 us -> 18.3 us
  starting transfers between devices: 69.2 us -> 71.2 us
    ppermute x12, waiting for transfers between devices: 13.2 us -> 18.1 us  [xperm(): return lax.ppermute(v, 'row', XP[s])]
    unnamed x14 -> x16, local copies, waits for them, and re-layouts: 3.1 us -> 7.66 us
    ppermute x12, waiting for transfers between devices: 13.2 us -> 8.86 us  [yperm(): return lax.ppermute(v, 'row', YP[s])]
    ppermute x12, starting transfers between devices: 14.2 us -> 17.8 us  [yperm(): return lax.ppermute(v, 'row', YP[s])]
    ppermute x1, starting transfers between devices: 7.33 us -> 4.83 us  [all_sum(): v = mine + lax.ppermute(other, 'col', CP)]
    pallas_call x1, Pallas kernels: 5.81 us -> 3.73 us  [stage(): pl.pallas_call(stage_kernel, in_specs=[ANY, SMEM, SMEM, ANY], out_specs=[...]
    ppermute x12, starting transfers between devices: 17.4 us -> 19.3 us  [zperm(): return lax.ppermute(v, 'col', ZP[s])]
  transfers between devices with their start and end apart: 46 -> 46, of which waited for: 18 -> 22; matrix products, arithmetic and copies ran while one was open for 0% -> 0% of each run, Pallas kernels for 15% -> 12%
where the time goes in v6:
time: 139 us
  starting transfers between devices  71.2 us (51%)
  waiting for transfers between devices  39.3 us (28%)
  Pallas kernels  18.3 us (13%)
  local copies, waits for them, and re-layouts  7.66 us (6%)
    ppermute x12, starting transfers between devices, zperm(): return lax.ppermute(v, 'col', ZP[s])  19.3 us
    ppermute x12, waiting for transfers between devices, xperm(): return lax.ppermute(v, 'row', XP[s])  18.1 us
    ppermute x12, starting transfers between devices, yperm(): return lax.ppermute(v, 'row', YP[s])  17.8 us
    ppermute x12, starting transfers between devices, xperm(): return lax.ppermute(v, 'row', XP[s])  17.6 us
    ppermute x9, starting transfers between devices, cperm(): return lax.ppermute(v, 'col', CP)  11.7 us
    ppermute x12, waiting for transfers between devices, zperm(): return lax.ppermute(v, 'col', ZP[s])  11.3 us
    ppermute x12, waiting for transfers between devices, yperm(): return lax.ppermute(v, 'row', YP[s])  8.86 us
    unnamed x16, local copies, waits for them, and re-layouts  7.66 us
  transfers between devices with their start and end apart: 46, of which 22 were waited for; matrix products, arithmetic and copies ran while one was open for 0% of the time, Pallas kernels for 12%

profile of v6, /device:TPU:1, one launch (start us, length us, event | category | flops | bytes accessed | tf_op | source)
XLA Modules:
  0.0 138.7 jit_solution(387321717158605015)
XLA Ops:
  1.8 2.5 %collective-permute-start.2 = (bf16[8,128,128]{2,1,0:T(8,128)(2,1)S(1)}, bf16[8,128,128]{2,1,0:T(8,128)(2,1)S(1)}, u32[]{:S(2)}, u32[]{:S(2)}) collective-permute-start(bf16[8,128,128]{2,1,0:T(8,128)(2,1)S(1)} %low_panels.1.after.refs_0_), channel_id=1, source_target_pairs={{0,2},{1,3},{2,4},{3,5},{4,6},{5,7},{6,0},{7,1},{8,10},{9,11},{10,... | collective-permute-start | bytes 786440 | tf_op jit(solution)/shard_map/ppermute | solution.py:44
  4.4 3.3 %collective-permute-start.1 = (bf16[8,128,128]{2,1,0:T(8,128)(2,1)S(1)}, bf16[8,128,128]{2,1,0:T(8,128)(2,1)S(1)}, u32[]{:S(2)}, u32[]{:S(2)}) collective-permute-start(bf16[8,128,128]{2,1,0:T(8,128)(2,1)S(1)} %low_panels.1.after.refs_0_), channel_id=1, source_target_pairs={{0,4},{1,5},{2,6},{3,7},{4,0},{5,1},{6,2},{7,3},{8,12},{9,13},{10,... | collective-permute-start | bytes 786440 | tf_op jit(solution)/shard_map/ppermute | solution.py:44
  12.6 4.6 %copy-done = bf16[1,1,384,128,128]{4,3,2,1,0:T(8,128)(2,1)S(1)} copy-done((bf16[1,1,384,128,128]{4,3,2,1,0:T(8,128)(2,1)S(1)}, bf16[1,1,384,128,128]{4,3,2,1,0:T(8,128)(2,1)}, u32[]{:S(2)}) %copy-start) | copy-done | bytes 12582936
  17.2 3.7 %stage.1 = (bf16[384,128,128]{2,1,0:T(8,128)(2,1)S(1)}, s32[416]{0:T(512)S(1)}, s32[416]{0:T(512)S(1)}, s32[2]{0:T(128)S(1)}, s32[2,8,256]{2,1,0:T(8,128)S(1)}) custom-call(bf16[384,128,128]{2,1,0:T(8,128)(2,1)S(1)} %bitcast.5, s32[1,1,384]{2,1,0:T(1,128)S(1)} %codes.1.code, s32[4]{0:T(128)S(1)} %get-tuple-element.148.place, ...), custom_call_target="tpu_custom_call" | custom-call | tf_op jit(solution)/shard_map/stage/pallas_call | solution.py:162
  24.6 2.7 %send_products.2 = (bf16[64,128,128]{2,1,0:T(8,128)(2,1)S(1)}, bf16[16,128,128]{2,1,0:T(8,128)(2,1)S(1)}, bf16[16,128,128]{2,1,0:T(8,128)(2,1)S(1)}, bf16[16,128...) custom-call(s32[416]{0:T(512)S(1)} %get-tuple-element.58.entries, s32[2]{0:T(128)S(1)} %get-tuple-element.56.count, ...), custom_call_target="tpu_custom_call" | custom-call | tf_op jit(solution)/shard_map/send_products/pallas_call | solution.py:228
  27.3 3.3 %collective-permute-done.4.c = bf16[8,128,128]{2,1,0:T(8,128)(2,1)S(1)} collective-permute-done((bf16[8,128,128]{2,1,0:T(8,128)(2,1)S(1)}, bf16[8,128,128]{2,1,0:T(8,128)(2,1)S(1)}, u32[]{:S(2)}, u32[]{:S(2)}) %collective-permute-start.4) | collective-permute-done | bytes 262176 | tf_op jit(solution)/shard_map/ppermute | solution.py:44
  39.4 2.5 %collective-permute-done.9.refs_2_ = bf16[8,128,128]{2,1,0:T(8,128)(2,1)S(1)} collective-permute-done((bf16[8,128,128]{2,1,0:T(8,128)(2,1)S(1)}, bf16[8,128,128]{2,1,0:T(8,128)(2,1)S(1)}, u32[]{:S(2)}, u32[]{:S(2)}) %collective-permute-start.9) | collective-permute-done | bytes 262176 | tf_op jit(solution)/shard_map/ppermute | solution.py:44
  42.8 2.5 %keep_products.3 = (bf16[16,128,128]{2,1,0:T(8,128)(2,1)S(1)}, bf16[8,128,128]{2,1,0:T(8,128)(2,1)S(1)}, bf16[8,128,128]{2,1,0:T(8,128)(2,1)S(1)}, bf16[16,128,1...) custom-call(s32[416]{0:T(512)S(1)} %get-tuple-element.55.entries, ...), custom_call_target="tpu_custom_call" | custom-call | tf_op jit(solution)/shard_map/keep_products/pallas_call | solution.py:241
  45.3 2.7 %send_products.3 = (bf16[64,128,128]{2,1,0:T(8,128)(2,1)S(1)}, bf16[16,128,128]{2,1,0:T(8,128)(2,1)S(1)}, bf16[16,128,128]{2,1,0:T(8,128)(2,1)S(1)}, bf16[16,128...) custom-call(s32[416]{0:T(512)S(1)} %get-tuple-element.58.entries, s32[2]{0:T(128)S(1)} %get-tuple-element.56.count, ...), custom_call_target="tpu_custom_call" | custom-call | tf_op jit(solution)/shard_map/send_products/pallas_call | solution.py:228
  48.2 2.2 %collective-permute-done.16.refs_7_.refs_6_ = bf16[16,128,128]{2,1,0:T(8,128)(2,1)S(1)} collective-permute-done((bf16[16,128,128]{2,1,0:T(8,128)(2,1)S(1)}, bf16[16,128,128]{2,1,0:T(8,128)(2,1)S(1)}, u32[]{:S(2)}, u32[]{:S(2)}) %collective-permute-start.16) | collective-permute-done | bytes 524320 | tf_op jit(solution)/shard_map/ppermute | solution.py:40
  50.8 2.7 %collective-permute-start.19 = (bf16[24,128,128]{2,1,0:T(8,128)(2,1)S(1)}, bf16[24,128,128]{2,1,0:T(8,128)(2,1)S(1)}, u32[]{:S(2)}, u32[]{:S(2)}) collective-permute-start(bf16[24,128,128]{2,1,0:T(8,128)(2,1)S(1)} %get-tuple-element.81), channel_id=1, source_target_pairs={{0,24},{8,0},{16,8},{24,16},{32,56},{40,32},{48,40},{56,48},{64,88... | collective-permute-start | bytes 2359304 | tf_op jit(solution)/shard_map/ppermute | solution.py:36
  56.2 2.7 %keep_products.2 = (bf16[16,128,128]{2,1,0:T(8,128)(2,1)S(1)}, bf16[8,128,128]{2,1,0:T(8,128)(2,1)S(1)}, bf16[8,128,128]{2,1,0:T(8,128)(2,1)S(1)}, bf16[16,128,1...) custom-call(s32[416]{0:T(512)S(1)} %get-tuple-element.55.entries, ...), custom_call_target="tpu_custom_call" | custom-call | tf_op jit(solution)/shard_map/keep_products/pallas_call | solution.py:241
  58.9 10.4 %collective-permute-done.18.refs_3_.refs_1_ = bf16[24,128,128]{2,1,0:T(8,128)(2,1)S(1)} collective-permute-done((bf16[24,128,128]{2,1,0:T(8,128)(2,1)S(1)}, bf16[24,128,128]{2,1,0:T(8,128)(2,1)S(1)}, u32[]{:S(2)}, u32[]{:S(2)}) %collective-permute-start.18) | collective-permute-done | bytes 786464 | tf_op jit(solution)/shard_map/ppermute | solution.py:36
  75.8 3.1 %collective-permute-done.21.refs_4_ = bf16[8,128,128]{2,1,0:T(8,128)(2,1)S(1)} collective-permute-done((bf16[8,128,128]{2,1,0:T(8,128)(2,1)S(1)}, bf16[8,128,128]{2,1,0:T(8,128)(2,1)S(1)}, u32[]{:S(2)}, u32[]{:S(2)}) %collective-permute-start.21) | collective-permute-done | bytes 262176 | tf_op jit(solution)/shard_map/ppermute | solution.py:36
  82.2 2.3 %collective-permute-start.27 = (bf16[8,128,128]{2,1,0:T(8,128)(2,1)S(1)}, bf16[8,128,128]{2,1,0:T(8,128)(2,1)S(1)}, u32[]{:S(2)}, u32[]{:S(2)}) collective-permute-start(bf16[8,128,128]{2,1,0:T(8,128)(2,1)S(1)} %get-tuple-element.102), channel_id=1, source_target_pairs={{0,8},{8,16},{16,24},{24,0},{32,40},{40,48},{48,56},{56,32},{64,72... | collective-permute-start | bytes 786440 | tf_op jit(solution)/shard_map/ppermute | solution.py:36
  87.9 2.2 %collective-permute-start.31 = (bf16[8,128,128]{2,1,0:T(8,128)(2,1)S(1)}, bf16[8,128,128]{2,1,0:T(8,128)(2,1)S(1)}, u32[]{:S(2)}, u32[]{:S(2)}) collective-permute-start(bf16[8,128,128]{2,1,0:T(8,128)(2,1)S(1)} %get-tuple-element.106), channel_id=1, source_target_pairs={{0,16},{8,24},{16,0},{24,8},{32,48},{40,56},{48,32},{56,40},{64,80... | collective-permute-start | bytes 786440 | tf_op jit(solution)/shard_map/ppermute | solution.py:36
  91.6 3.9 %collective-permute-done.30.refs_6_ = bf16[8,128,128]{2,1,0:T(8,128)(2,1)S(1)} collective-permute-done((bf16[8,128,128]{2,1,0:T(8,128)(2,1)S(1)}, bf16[8,128,128]{2,1,0:T(8,128)(2,1)S(1)}, u32[]{:S(2)}, u32[]{:S(2)}) %collective-permute-start.30) | collective-permute-done | bytes 262176 | tf_op jit(solution)/shard_map/ppermute | solution.py:40
  96.1 4.8 %collective-permute-start.32 = (f32[128,256]{1,0:T(8,128)S(1)}, f32[128,256]{1,0:T(8,128)S(1)}, u32[]{:S(2)}, u32[]{:S(2)}) collective-permute-start(f32[128,256]{1,0:T(8,128)S(1)} %slice_select_fusion), channel_id=1, source_target_pairs={{0,1},{1,0},{2,3},{3,2},{4,5},{5,4},{6,7},{7,6},{8,9},{9,8},{10,11... | collective-permute-start | bytes 393224 | tf_op jit(solution)/shard_map/ppermute | solution.py:367
  101.9 4.4 %collective-permute-start.35 = (f32[32,256]{1,0:T(8,128)S(1)}, f32[32,256]{1,0:T(8,128)S(1)}, u32[]{:S(2)}, u32[]{:S(2)}) collective-permute-start(f32[32,256]{1,0:T(8,128)S(1)} %select_select_fusion.4), channel_id=1, source_target_pairs={{0,6},{1,7},{2,0},{3,1},{4,2},{5,3},{6,4},{7,5},{8,14},{9,15},{10,... | collective-permute-start | bytes 98312 | tf_op jit(solution)/shard_map/ppermute | solution.py:44
  107.4 3.3 %collective-permute-done.33 = f32[32,256]{1,0:T(8,128)S(1)} collective-permute-done((f32[32,256]{1,0:T(8,128)S(1)}, f32[32,256]{1,0:T(8,128)S(1)}, u32[]{:S(2)}, u32[]{:S(2)}) %collective-permute-start.33) | collective-permute-done | bytes 32800 | tf_op jit(solution)/shard_map/ppermute | solution.py:44
  111.1 3.3 %collective-permute-start.38 = (f32[32,256]{1,0:T(8,128)S(1)}, f32[32,256]{1,0:T(8,128)S(1)}, u32[]{:S(2)}, u32[]{:S(2)}) collective-permute-start(f32[32,256]{1,0:T(8,128)S(1)} %add_add_fusion.2), channel_id=1, source_target_pairs={{0,24},{8,0},{16,8},{24,16},{32,56},{40,32},{48,40},{56,48},{64,88... | collective-permute-start | bytes 98312 | tf_op jit(solution)/shard_map/ppermute | solution.py:36
  116.0 2.4 %collective-permute-done.37 = f32[32,256]{1,0:T(8,128)S(1)} collective-permute-done((f32[32,256]{1,0:T(8,128)S(1)}, f32[32,256]{1,0:T(8,128)S(1)}, u32[]{:S(2)}, u32[]{:S(2)}) %collective-permute-start.37) | collective-permute-done | bytes 32800 | tf_op jit(solution)/shard_map/ppermute | solution.py:36
  120.3 2.9 %collective-permute-start.39 = (f32[32,256]{1,0:T(8,128)S(1)}, f32[32,256]{1,0:T(8,128)S(1)}, u32[]{:S(2)}, u32[]{:S(2)}) collective-permute-start(f32[32,256]{1,0:T(8,128)S(1)} %add_add_fusion.1), channel_id=1, source_target_pairs={{0,64},{8,72},{16,80},{24,88},{32,96},{40,104},{48,112},{56,120},{... | collective-permute-start | bytes 98312 | tf_op jit(solution)/shard_map/ppermute | solution.py:40
  129.9 6.8 %collective-permute-start.45 = (f32[128,256]{1,0:T(8,128)S(1)}, f32[128,256]{1,0:T(8,128)S(1)}, u32[]{:S(2)}, u32[]{:S(2)}) collective-permute-start(f32[128,256]{1,0:T(8,128)S(1)} %pad_maximum_fusion), channel_id=1, source_target_pairs={{0,1},{1,0},{2,3},{3,2},{4,5},{5,4},{6,7},{7,6},{8,9},{9,8},{10,11... | collective-permute-start | bytes 393224 | tf_op jit(solution)/shard_map/ppermute | solution.py:48
  (116 shorter events, 52.6 us)
Async XLA Ops:
  1.8 19.1 %collective-permute-start.2 = (bf16[8,128,128]{2,1,0:T(8,128)(2,1)S(1)}, bf16[8,128,128]{2,1,0:T(8,128)(2,1)S(1)}, u32[]{:S(2)}, u32[]{:S(2)}) collective-permute-start(bf16[8,128,128]{2,1,0:T(8,128)(2,1)S(1)} %low_panels.1.after.refs_0_), channel_id=1, source_target_pairs={{0,2},{1,3},{2,4},{3,5},{4,6},{5,7},{6,0},{7,1},{8,10},{9,11},{10,... | collective-permute-start | bytes 786440 | tf_op jit(solution)/shard_map/ppermute | solution.py:44
  4.4 16.6 %collective-permute-start.1 = (bf16[8,128,128]{2,1,0:T(8,128)(2,1)S(1)}, bf16[8,128,128]{2,1,0:T(8,128)(2,1)S(1)}, u32[]{:S(2)}, u32[]{:S(2)}) collective-permute-start(bf16[8,128,128]{2,1,0:T(8,128)(2,1)S(1)} %low_panels.1.after.refs_0_), channel_id=1, source_target_pairs={{0,4},{1,5},{2,6},{3,7},{4,0},{5,1},{6,2},{7,3},{8,12},{9,13},{10,... | collective-permute-start | bytes 786440 | tf_op jit(solution)/shard_map/ppermute | solution.py:44
  7.7 13.3 %collective-permute-start = (bf16[8,128,128]{2,1,0:T(8,128)(2,1)S(1)}, bf16[8,128,128]{2,1,0:T(8,128)(2,1)S(1)}, u32[]{:S(2)}, u32[]{:S(2)}) collective-permute-start(bf16[8,128,128]{2,1,0:T(8,128)(2,1)S(1)} %low_panels.1.after.refs_0_), channel_id=1, source_target_pairs={{0,6},{1,7},{2,0},{3,1},{4,2},{5,3},{6,4},{7,5},{8,14},{9,15},{10,... | collective-permute-start | bytes 786440 | tf_op jit(solution)/shard_map/ppermute | solution.py:44
  8.4 14.3 %collective-permute-start.5 = (bf16[8,128,128]{2,1,0:T(8,128)(2,1)S(1)}, bf16[8,128,128]{2,1,0:T(8,128)(2,1)S(1)}, u32[]{:S(2)}, u32[]{:S(2)}) collective-permute-start(bf16[8,128,128]{2,1,0:T(8,128)(2,1)S(1)} %low_panels.1.after.refs_0_), channel_id=1, source_target_pairs={{0,1},{1,0},{2,3},{3,2},{4,5},{5,4},{6,7},{7,6},{8,9},{9,8},{10,11... | collective-permute-start | bytes 786440 | tf_op jit(solution)/shard_map/ppermute | solution.py:48
  21.9 8.8 %collective-permute-start.4 = (bf16[8,128,128]{2,1,0:T(8,128)(2,1)S(1)}, bf16[8,128,128]{2,1,0:T(8,128)(2,1)S(1)}, u32[]{:S(2)}, u32[]{:S(2)}) collective-permute-start(bf16[8,128,128]{2,1,0:T(8,128)(2,1)S(1)} %high_panels.1.a), channel_id=1, source_target_pairs={{0,2},{1,3},{2,4},{3,5},{4,6},{5,7},{6,0},{7,1},{8,10},{9,11},{10,... | collective-permute-start | bytes 786440 | tf_op jit(solution)/shard_map/ppermute | solution.py:44
  22.7 7.9 %collective-permute-start.3 = (bf16[8,128,128]{2,1,0:T(8,128)(2,1)S(1)}, bf16[8,128,128]{2,1,0:T(8,128)(2,1)S(1)}, u32[]{:S(2)}, u32[]{:S(2)}) collective-permute-start(bf16[8,128,128]{2,1,0:T(8,128)(2,1)S(1)} %high_panels.1.a), channel_id=1, source_target_pairs={{0,6},{1,7},{2,0},{3,1},{4,2},{5,3},{6,4},{7,5},{8,14},{9,15},{10,... | collective-permute-start | bytes 786440 | tf_op jit(solution)/shard_map/ppermute | solution.py:44
  32.5 9.4 %collective-permute-start.9 = (bf16[8,128,128]{2,1,0:T(8,128)(2,1)S(1)}, bf16[8,128,128]{2,1,0:T(8,128)(2,1)S(1)}, u32[]{:S(2)}, u32[]{:S(2)}) collective-permute-start(bf16[8,128,128]{2,1,0:T(8,128)(2,1)S(1)} %get-tuple-element.63.refs_0_), channel_id=1, source_target_pairs={{0,4},{1,5},{2,6},{3,7},{4,0},{5,1},{6,2},{7,3},{8,12},{9,13},{10,... | collective-permute-start | bytes 786440 | tf_op jit(solution)/shard_map/ppermute | solution.py:44
  33.9 14.4 %collective-permute-start.14 = (bf16[16,128,128]{2,1,0:T(8,128)(2,1)S(1)}, bf16[16,128,128]{2,1,0:T(8,128)(2,1)S(1)}, u32[]{:S(2)}, u32[]{:S(2)}) collective-permute-start(bf16[16,128,128]{2,1,0:T(8,128)(2,1)S(1)} %get-tuple-element.69), channel_id=1, source_target_pairs={{0,8},{8,16},{16,24},{24,0},{32,40},{40,48},{48,56},{56,32},{64,72... | collective-permute-start | bytes 1572872 | tf_op jit(solution)/shard_map/ppermute | solution.py:36
  35.1 13.1 %collective-permute-start.15 = (bf16[16,128,128]{2,1,0:T(8,128)(2,1)S(1)}, bf16[16,128,128]{2,1,0:T(8,128)(2,1)S(1)}, u32[]{:S(2)}, u32[]{:S(2)}) collective-permute-start(bf16[16,128,128]{2,1,0:T(8,128)(2,1)S(1)} %get-tuple-element.72), channel_id=1, source_target_pairs={{0,24},{8,0},{16,8},{24,16},{32,56},{40,32},{48,40},{56,48},{64,88... | collective-permute-start | bytes 1572872 | tf_op jit(solution)/shard_map/ppermute | solution.py:36
  36.6 13.8 %collective-permute-start.16 = (bf16[16,128,128]{2,1,0:T(8,128)(2,1)S(1)}, bf16[16,128,128]{2,1,0:T(8,128)(2,1)S(1)}, u32[]{:S(2)}, u32[]{:S(2)}) collective-permute-start(bf16[16,128,128]{2,1,0:T(8,128)(2,1)S(1)} %get-tuple-element.75), channel_id=1, source_target_pairs={{0,32},{8,40},{16,48},{24,56},{32,64},{40,72},{48,80},{56,88},{64,... | collective-permute-start | bytes 1572872 | tf_op jit(solution)/shard_map/ppermute | solution.py:40
  37.9 12.6 %collective-permute-start.17 = (bf16[16,128,128]{2,1,0:T(8,128)(2,1)S(1)}, bf16[16,128,128]{2,1,0:T(8,128)(2,1)S(1)}, u32[]{:S(2)}, u32[]{:S(2)}) collective-permute-start(bf16[16,128,128]{2,1,0:T(8,128)(2,1)S(1)} %get-tuple-element.78), channel_id=1, source_target_pairs={{0,96},{8,104},{16,112},{24,120},{32,0},{40,8},{48,16},{56,24},{64... | collective-permute-start | bytes 1572872 | tf_op jit(solution)/shard_map/ppermute | solution.py:40
  50.7 18.5 %collective-permute-start.18 = (bf16[24,128,128]{2,1,0:T(8,128)(2,1)S(1)}, bf16[24,128,128]{2,1,0:T(8,128)(2,1)S(1)}, u32[]{:S(2)}, u32[]{:S(2)}) collective-permute-start(bf16[24,128,128]{2,1,0:T(8,128)(2,1)S(1)} %get-tuple-element.80), channel_id=1, source_target_pairs={{0,8},{8,16},{16,24},{24,0},{32,40},{40,48},{48,56},{56,32},{64,72... | collective-permute-start | bytes 2359304 | tf_op jit(solution)/shard_map/ppermute | solution.py:36
  50.8 20.2 %collective-permute-start.19 = (bf16[24,128,128]{2,1,0:T(8,128)(2,1)S(1)}, bf16[24,128,128]{2,1,0:T(8,128)(2,1)S(1)}, u32[]{:S(2)}, u32[]{:S(2)}) collective-permute-start(bf16[24,128,128]{2,1,0:T(8,128)(2,1)S(1)} %get-tuple-element.81), channel_id=1, source_target_pairs={{0,24},{8,0},{16,8},{24,16},{32,56},{40,32},{48,40},{56,48},{64,88... | collective-permute-start | bytes 2359304 | tf_op jit(solution)/shard_map/ppermute | solution.py:36
  53.5 18.8 %collective-permute-start.22 = (bf16[24,128,128]{2,1,0:T(8,128)(2,1)S(1)}, bf16[24,128,128]{2,1,0:T(8,128)(2,1)S(1)}, u32[]{:S(2)}, u32[]{:S(2)}) collective-permute-start(bf16[24,128,128]{2,1,0:T(8,128)(2,1)S(1)} %get-tuple-element.85), channel_id=1, source_target_pairs={{0,32},{8,40},{16,48},{24,56},{32,64},{40,72},{48,80},{56,88},{64,... | collective-permute-start | bytes 2359304 | tf_op jit(solution)/shard_map/ppermute | solution.py:40
  54.4 18.6 %collective-permute-start.23 = (bf16[24,128,128]{2,1,0:T(8,128)(2,1)S(1)}, bf16[24,128,128]{2,1,0:T(8,128)(2,1)S(1)}, u32[]{:S(2)}, u32[]{:S(2)}) collective-permute-start(bf16[24,128,128]{2,1,0:T(8,128)(2,1)S(1)} %get-tuple-element.86), channel_id=1, source_target_pairs={{0,96},{8,104},{16,112},{24,120},{32,0},{40,8},{48,16},{56,24},{64... | collective-permute-start | bytes 2359304 | tf_op jit(solution)/shard_map/ppermute | solution.py:40
  69.3 6.5 %collective-permute-start.20 = (bf16[8,128,128]{2,1,0:T(8,128)(2,1)S(1)}, bf16[8,128,128]{2,1,0:T(8,128)(2,1)S(1)}, u32[]{:S(2)}, u32[]{:S(2)}) collective-permute-start(bf16[8,128,128]{2,1,0:T(8,128)(2,1)S(1)} %add_convert_fusion.3), channel_id=1, source_target_pairs={{0,8},{8,16},{16,24},{24,0},{32,40},{40,48},{48,56},{56,32},{64,72... | collective-permute-start | bytes 786440 | tf_op jit(solution)/shard_map/ppermute | solution.py:36
  71.0 7.9 %collective-permute-start.21 = (bf16[8,128,128]{2,1,0:T(8,128)(2,1)S(1)}, bf16[8,128,128]{2,1,0:T(8,128)(2,1)S(1)}, u32[]{:S(2)}, u32[]{:S(2)}) collective-permute-start(bf16[8,128,128]{2,1,0:T(8,128)(2,1)S(1)} %add_convert_fusion.2), channel_id=1, source_target_pairs={{0,24},{8,0},{16,8},{24,16},{32,56},{40,32},{48,40},{56,48},{64,88... | collective-permute-start | bytes 786440 | tf_op jit(solution)/shard_map/ppermute | solution.py:36
  72.3 6.8 %collective-permute-start.24 = (bf16[8,128,128]{2,1,0:T(8,128)(2,1)S(1)}, bf16[8,128,128]{2,1,0:T(8,128)(2,1)S(1)}, u32[]{:S(2)}, u32[]{:S(2)}) collective-permute-start(bf16[8,128,128]{2,1,0:T(8,128)(2,1)S(1)} %add_convert_fusion.1), channel_id=1, source_target_pairs={{0,32},{8,40},{16,48},{24,56},{32,64},{40,72},{48,80},{56,88},{64,... | collective-permute-start | bytes 786440 | tf_op jit(solution)/shard_map/ppermute | solution.py:40
  73.1 7.0 %collective-permute-start.25 = (bf16[8,128,128]{2,1,0:T(8,128)(2,1)S(1)}, bf16[8,128,128]{2,1,0:T(8,128)(2,1)S(1)}, u32[]{:S(2)}, u32[]{:S(2)}) collective-permute-start(bf16[8,128,128]{2,1,0:T(8,128)(2,1)S(1)} %add_convert_fusion), channel_id=1, source_target_pairs={{0,96},{8,104},{16,112},{24,120},{32,0},{40,8},{48,16},{56,24},{64... | collective-permute-start | bytes 786440 | tf_op jit(solution)/shard_map/ppermute | solution.py:40
  80.5 7.4 %collective-permute-start.26 = (bf16[8,128,128]{2,1,0:T(8,128)(2,1)S(1)}, bf16[8,128,128]{2,1,0:T(8,128)(2,1)S(1)}, u32[]{:S(2)}, u32[]{:S(2)}) collective-permute-start(bf16[8,128,128]{2,1,0:T(8,128)(2,1)S(1)} %get-tuple-element.101), channel_id=1, source_target_pairs={{0,32},{8,40},{16,48},{24,56},{32,64},{40,72},{48,80},{56,88},{64,... | collective-permute-start | bytes 786440 | tf_op jit(solution)/shard_map/ppermute | solution.py:40
  82.2 8.0 %collective-permute-start.27 = (bf16[8,128,128]{2,1,0:T(8,128)(2,1)S(1)}, bf16[8,128,128]{2,1,0:T(8,128)(2,1)S(1)}, u32[]{:S(2)}, u32[]{:S(2)}) collective-permute-start(bf16[8,128,128]{2,1,0:T(8,128)(2,1)S(1)} %get-tuple-element.102), channel_id=1, source_target_pairs={{0,8},{8,16},{16,24},{24,0},{32,40},{40,48},{48,56},{56,32},{64,72... | collective-permute-start | bytes 786440 | tf_op jit(solution)/shard_map/ppermute | solution.py:36
  86.1 9.4 %collective-permute-start.30 = (bf16[8,128,128]{2,1,0:T(8,128)(2,1)S(1)}, bf16[8,128,128]{2,1,0:T(8,128)(2,1)S(1)}, u32[]{:S(2)}, u32[]{:S(2)}) collective-permute-start(bf16[8,128,128]{2,1,0:T(8,128)(2,1)S(1)} %get-tuple-element.105), channel_id=1, source_target_pairs={{0,64},{8,72},{16,80},{24,88},{32,96},{40,104},{48,112},{56,120},{... | collective-permute-start | bytes 786440 | tf_op jit(solution)/shard_map/ppermute | solution.py:40
  87.9 7.6 %collective-permute-start.31 = (bf16[8,128,128]{2,1,0:T(8,128)(2,1)S(1)}, bf16[8,128,128]{2,1,0:T(8,128)(2,1)S(1)}, u32[]{:S(2)}, u32[]{:S(2)}) collective-permute-start(bf16[8,128,128]{2,1,0:T(8,128)(2,1)S(1)} %get-tuple-element.106), channel_id=1, source_target_pairs={{0,16},{8,24},{16,0},{24,8},{32,48},{40,56},{48,32},{56,40},{64,80... | collective-permute-start | bytes 786440 | tf_op jit(solution)/shard_map/ppermute | solution.py:36
  129.9 8.1 %collective-permute-start.45 = (f32[128,256]{1,0:T(8,128)S(1)}, f32[128,256]{1,0:T(8,128)S(1)}, u32[]{:S(2)}, u32[]{:S(2)}) collective-permute-start(f32[128,256]{1,0:T(8,128)S(1)} %pad_maximum_fusion), channel_id=1, source_target_pairs={{0,1},{1,0},{2,3},{3,2},{4,5},{5,4},{6,7},{7,6},{8,9},{9,8},{10,11... | collective-permute-start | bytes 393224 | tf_op jit(solution)/shard_map/ppermute | solution.py:48
  (30 other events, 226.1 us)
